TPU v7x, 128 devices: a whole 4x4x4 slice. The times are simulated.
128 devices in a mesh: row: 8 (over x, core), col: 16 (over z, y).
Axes of the slice: x: 4, y: 4, z: 4, core: 2. Of those that a mesh axis runs over, the one named last changes fastest.
Arguments:
- load_force: float32 [2, 2, 256, 2048], P(None, None, 'row', 'col'), may hold values from -24 to 24
- stiffness: float32 [2, 2, 256, 2048], P(None, None, 'row', 'col'), may hold values from 0.5 to 2
- cracks: int32 [2, 2, 256, 2048], P(None, None, 'row', 'col'), may hold values 0 or 1
- anchor: float32 [2, 256, 2048], P(None, 'row', 'col'), may hold values from 0.1 to 2
- images: bfloat16 [2, 2048, 16384], P(None, 'row', 'col'), may hold values from -6 to 6
- owners: int32 [6144, 1], P(('row', 'col')), may hold values from 0 to 15; in each aligned block of 48 rows (0 to 47, 48 to 95, ...) at most 4 rows name the same one
- source_tile: int32 [6144], P(('row', 'col')), may hold values from 0 to 3
- offsets: int32 [2, 6144], P(None, ('row', 'col')), may hold values from -96 to 96
- blend_weight: float32 [6144], P(('row', 'col')), may hold values from 0.5 to 2
- counts: int32 [1024], P(('row', 'col')), may hold values from 1 to 6
Outputs:
- displacement: float32 [2, 2, 256, 2048], P(None, None, 'row', 'col')
- residual: float32 [2, 2, 256, 2048], P(None, None, 'row', 'col')
- level_zero: bfloat16 [2, 2048, 16384], P(None, 'row', 'col')
- level_one: bfloat16 [2, 1024, 8192], P(None, 'row', 'col')
- level_two: bfloat16 [2, 512, 4096], P(None, 'row', 'col')
Inputs may be any that keep to these rules, and one draw needn't show every extreme that they name: `owners`: within the entries of one device no value appears more than 4 times, and some value appears exactly 4 times in some device's entries.
All inputs are finite; a program needn't handle non-finite values. No bound on the sum of `cracks` on one device may be relied on, other than what follows from the above.
Results may differ from a plain program's by a relative error of at most 0.0085.
Values may be sent and summed in bfloat16 or wider, within the bound.
A program may use at most 384 MiB of HBM per device.

v0:
```python
import jax
import jax.numpy as jnp
from jax import lax
from jax.sharding import PartitionSpec as P

S = 2
TILE = 256
SPACING = 8
K = 6
ITERS = 4
TR = 1
TC = 4
TILES_DEV = 8
ENT_DEV = 48


def extended(block, sides, width):
    for axis, dim in sides:
        count = lax.axis_size(axis)
        forward = [(i, i + 1) for i in range(count - 1)]
        backward = [(target, source) for source, target in forward]
        low = lax.ppermute(
            lax.slice_in_dim(block, block.shape[dim] - width, None, axis=dim), axis, forward
        )
        high = lax.ppermute(lax.slice_in_dim(block, 0, width, axis=dim), axis, backward)
        block = jnp.concatenate([low, block, high], axis=dim)
    return block


def from_behind(array, axis, by):
    size = lax.axis_size(axis)
    pairs = [(i, i + by) for i in range(size) if 0 <= i + by < size]
    return lax.ppermute(array, axis, pairs)


def tent_weight(offset):
    return jnp.maximum(0.0, 1.0 - jnp.abs(offset))


def sample_matrix(shift_value):
    position = jnp.arange(TILE, dtype=jnp.float32)
    matrix = tent_weight(
        position[None, None, :] - position[None, :, None] - shift_value[:, None, None]
    )
    return matrix.astype(jnp.bfloat16)


def warp_tiles(picked, local_anchor, offset_pair, weights):
    shift_y = offset_pair[0].astype(jnp.float32) + SPACING * jnp.repeat(
        local_anchor[:, 0].reshape(-1), K
    )
    shift_x = offset_pair[1].astype(jnp.float32) + SPACING * jnp.repeat(
        local_anchor[:, 1].reshape(-1), K
    )

    def warp_group(inputs):
        tiles_group, along_y, along_x, weight_group = inputs
        across_matrix = sample_matrix(along_x)
        down_matrix = sample_matrix(along_y)
        across = jnp.einsum(
            "ecw,ebw->ecb", tiles_group, across_matrix, preferred_element_type=jnp.float32
        )
        across = across.astype(jnp.bfloat16)
        result = jnp.einsum("eac,ecb->eab", down_matrix, across, preferred_element_type=jnp.float32)
        result = result * weight_group[:, None, None]
        return jnp.sum(result.reshape(TC, K, TILE, TILE), axis=1)

    groups = S * TR
    warped = lax.map(
        warp_group,
        (
            picked.reshape(groups, TC * K, TILE, TILE),
            shift_y.reshape(groups, TC * K),
            shift_x.reshape(groups, TC * K),
            weights.reshape(groups, TC * K),
        ),
    )
    return warped.reshape(S, TR, TC, TILE, TILE)


def operate(field_now, springs_all):
    right_spring, left_spring, down_spring, up_spring, anchor_spring = springs_all
    padded = extended(field_now, (("row", 2), ("col", 3)), 1)
    return (
        anchor_spring * field_now
        + right_spring * (field_now - padded[:, :, 1:-1, 2:])
        + left_spring * (field_now - padded[:, :, 1:-1, :-2])
        + down_spring * (field_now - padded[:, :, 2:, 1:-1])
        + up_spring * (field_now - padded[:, :, :-2, 1:-1])
    )


def section_dot(first, second):
    return jnp.sum(first * second, axis=(1, 2, 3), keepdims=True)


def squares_sum(residual):
    return lax.psum(section_dot(residual, residual), ("row", "col"))


def shards(
    load_force,
    stiffness,
    cracks,
    anchor,
    images,
    owners,
    source_tile,
    offsets,
    blend_weight,
    counts,
):
    springs = stiffness * cracks.astype(jnp.float32)
    right_spring = springs[:, 0:1]
    down_spring = springs[:, 1:2]
    left_edge = from_behind(right_spring[:, :, :, -1:], "col", 1)
    up_edge = from_behind(down_spring[:, :, -1:, :], "row", 1)
    left_spring = jnp.concatenate([left_edge, right_spring[..., :-1]], axis=3)
    up_spring = jnp.concatenate([up_edge, down_spring[:, :, :-1]], axis=2)
    springs_all = (right_spring, left_spring, down_spring, up_spring, anchor[:, None])
    displacement = jnp.zeros_like(load_force)
    residual = load_force
    direction = load_force
    norm_now = squares_sum(residual)
    for iteration in range(ITERS):
        applied = operate(direction, springs_all)
        step_size = norm_now / lax.psum(section_dot(direction, applied), ("row", "col"))
        displacement = displacement + step_size * direction
        residual = residual - step_size * applied
        norm_next = squares_sum(residual)
        direction = residual + norm_next / norm_now * direction
        norm_now = norm_next
    half_cell = TILE // SPACING // 2
    vertex_step = TILE // SPACING
    local_anchor = displacement[:, :, half_cell::vertex_step, half_cell::vertex_step]
    my_tiles = (
        images.reshape(S, TR, TILE, TC, TILE)
        .transpose(0, 1, 3, 2, 4)
        .reshape(TILES_DEV, TILE, TILE)
    )
    entry_index = jnp.arange(ENT_DEV, dtype=jnp.int32)
    section_of = entry_index // (TR * TC * K)
    list_slot = entry_index % K
    owner_col = owners[:, 0]
    tile_id = section_of * (TR * TC) + source_tile
    row_tiles = lax.all_gather(my_tiles, "col", axis=0, tiled=True)
    picked = jnp.take(row_tiles, owner_col * TILES_DEV + tile_id, axis=0)
    weights = blend_weight * (list_slot < jnp.repeat(counts, K)).astype(jnp.float32)
    warped = warp_tiles(picked, local_anchor, offsets, weights)
    warped = warped.transpose(0, 1, 3, 2, 4).reshape(S, TR * TILE, TC * TILE)
    rows_local = TR * TILE
    cols_local = TC * TILE
    level_zero = warped.astype(jnp.bfloat16)
    level_one = jnp.mean(
        warped.reshape(S, rows_local // 2, 2, cols_local // 2, 2), axis=(2, 4)
    ).astype(jnp.bfloat16)
    level_two = jnp.mean(
        warped.reshape(S, rows_local // 4, 4, cols_local // 4, 4), axis=(2, 4)
    ).astype(jnp.bfloat16)
    return (displacement, residual, level_zero, level_one, level_two)


def solution(mesh):
    in_specs = (
        P(None, None, "row", "col"),
        P(None, None, "row", "col"),
        P(None, None, "row", "col"),
        P(None, "row", "col"),
        P(None, "row", "col"),
        P(("row", "col"), None),
        P(("row", "col")),
        P(None, ("row", "col")),
        P(("row", "col")),
        P(("row", "col")),
    )
    out_specs = (
        P(None, None, "row", "col"),
        P(None, None, "row", "col"),
        P(None, "row", "col"),
        P(None, "row", "col"),
        P(None, "row", "col"),
    )
    return jax.shard_map(shards, mesh=mesh, in_specs=in_specs, out_specs=out_specs, check_vma=False)
```

profile of v0, /device:TPU:4, one launch (start us, length us, event | category | flops | bytes accessed | tf_op | source)
XLA Modules:
  0.0 863.7 jit_solution(13179199595800641510)
XLA Ops:
  7.3 1.5 copy.24
  8.8 1.3 copy.25
  10.1 0.7 fusion.94
  10.9 1.9 collective-permute-start.1
  12.8 2.4 collective-permute-start
  15.2 0.9 convert_multiply_fusion
  16.1 3.0 collective-permute-start.5
  19.1 3.5 collective-permute-start.3
  22.7 1.5 collective-permute-done.3
  24.3 0.9 pad_maximum_fusion
  25.2 1.3 collective-permute-start.2
  26.5 4.9 collective-permute-start.4
  31.4 2.5 collective-permute-done.2
  34.0 1.3 collective-permute-done.4
  35.2 0.2 multiply_reduce_fusion.6
  35.4 71.0 %all-reduce = (f32[2,1,1,1]{0,3,2,1:T(1,128)S(1)}, f32[2,1,1,1]{0,3,2,1:T(1,128)S(1)}) all-reduce(f32[2,1,1,1]{0,3,2,1:T(1,128)S(1)} %bitcast.92, f32[2,1,1,1]{0,3,2,1:T(1,128)S(1)} %bitcast.91), channel_id=1, replica_groups=mesh['row'=8,'col'=16] {'row','col'}, use_global_device_ids=true, to_apply=%region_1.0 | all-reduce | flops 4 | bytes 32 | tf_op jit(solution)/shard_map/psum | solution.py:98
  106.6 64.5 %psum.58 = f32[2,1,1,1]{0,3,2,1:T(1,128)S(1)} all-reduce(f32[2,1,1,1]{0,3,2,1:T(1,128)S(1)} %bitcast.95), channel_id=1, replica_groups=mesh['row'=8,'col'=16] {'row','col'}, use_global_device_ids=true, to_apply=%region_5.0 | all-reduce | flops 2 | bytes 16 | tf_op jit(solution)/shard_map/psum | solution.py:98
  171.2 1.9 collective-permute-start.7
  173.1 2.4 collective-permute-start.6
  175.5 2.5 collective-permute-done.6
  178.1 1.3 collective-permute-start.8
  179.4 4.6 collective-permute-start.9
  184.2 0.3 collective-permute-done.8
  184.5 1.6 collective-permute-done.9
  186.0 0.2 multiply_reduce_fusion.4
  186.2 65.8 %psum.59 = f32[2,1,1,1]{0,3,2,1:T(1,128)S(1)} all-reduce(f32[2,1,1,1]{0,3,2,1:T(1,128)S(1)} %bitcast.97), channel_id=1, replica_groups=mesh['row'=8,'col'=16] {'row','col'}, use_global_device_ids=true, to_apply=%region_7.0 | all-reduce | flops 2 | bytes 16 | tf_op jit(solution)/shard_map/psum | solution.py:127
  252.3 62.5 %psum.60 = f32[2,1,1,1]{0,3,2,1:T(1,128)S(1)} all-reduce(f32[2,1,1,1]{0,3,2,1:T(1,128)S(1)} %bitcast.93), channel_id=1, replica_groups=mesh['row'=8,'col'=16] {'row','col'}, use_global_device_ids=true, to_apply=%region_9.0 | all-reduce | flops 2 | bytes 16 | tf_op jit(solution)/shard_map/psum | solution.py:98
  314.9 2.8 collective-permute-start.11
  317.7 1.9 collective-permute-start.10
  319.7 2.9 collective-permute-done.10
  322.7 1.3 collective-permute-start.12
  324.0 4.6 collective-permute-start.13
  328.6 0.4 collective-permute-done.12
  329.1 1.6 collective-permute-done.13
  330.6 0.2 multiply_reduce_fusion.2
  330.8 66.4 %psum.61 = f32[2,1,1,1]{0,3,2,1:T(1,128)S(1)} all-reduce(f32[2,1,1,1]{0,3,2,1:T(1,128)S(1)} %bitcast.98), channel_id=1, replica_groups=mesh['row'=8,'col'=16] {'row','col'}, use_global_device_ids=true, to_apply=%region_11.0 | all-reduce | flops 2 | bytes 16 | tf_op jit(solution)/shard_map/psum | solution.py:127
  397.2 0.2 multiply_reduce_fusion.1
  397.4 62.2 %psum.62 = f32[2,1,1,1]{0,3,2,1:T(1,128)S(1)} all-reduce(f32[2,1,1,1]{0,3,2,1:T(1,128)S(1)} %bitcast.94), channel_id=1, replica_groups=mesh['row'=8,'col'=16] {'row','col'}, use_global_device_ids=true, to_apply=%region_13.0 | all-reduce | flops 2 | bytes 16 | tf_op jit(solution)/shard_map/psum | solution.py:98
  459.7 3.0 collective-permute-start.15
  462.7 1.9 collective-permute-start.14
  464.7 3.0 collective-permute-done.14
  467.7 1.3 collective-permute-start.16
  469.0 4.6 collective-permute-start.17
  474.1 1.6 collective-permute-done.17
  475.6 0.2 multiply_reduce_fusion
  475.9 66.3 %psum.63 = f32[2,1,1,1]{0,3,2,1:T(1,128)S(1)} all-reduce(f32[2,1,1,1]{0,3,2,1:T(1,128)S(1)} %bitcast.96), channel_id=1, replica_groups=mesh['row'=8,'col'=16] {'row','col'}, use_global_device_ids=true, to_apply=%region_15.0 | all-reduce | flops 2 | bytes 16 | tf_op jit(solution)/shard_map/psum | solution.py:127
  542.2 0.7 multiply_subtract_fusion
  543.5 10.7 %gather_fusion = bf16[48,256,256]{2,1,0:T(8,128)(2,1)} fusion(bf16[128,256,256]{2,1,0:T(8,128)(2,1)} %all-gather.2.cloned.1.call-done, s32[1024]{0:T(1024)S(1)} %pad_clamp_fusion), kind=kCustom, calls=%fused_computation | custom fusion | bytes 12583104 | tf_op jit(solution)/shard_map/jit(_take)/gather | solution.py:147
  554.2 6.1 broadcast_select_fusion
  560.3 21.6 %while.10 = (s32[]{:T(128)}, f32[2,4,256,256]{3,2,1,0:T(8,128)S(1)}, f32[2,24]{1,0:T(2,128)S(1)}, bf16[2,24,256,256]{3,2,1,0:T(8,128)(2,1)}, f32[2,24]{1,0:T(2,1...) while((s32[]{:T(128)}, f32[2,4,256,256]{3,2,1,0:T(8,128)S(1)}, f32[2,24]{1,0:T(2,128)S(1)}, ...), condition=%wide.region_18.19_spmd, body=%wide.region_16.18_spmd.sunk | while | flops 1630863360 | bytes 19663024 | solution.py:69
  560.4 7.3 broadcast_multiply_fusion.2
  567.6 3.3 reduce_sum.118
  571.2 7.3 broadcast_multiply_fusion.2
  578.5 3.3 reduce_sum.118
  582.0 1.2 copy-done
  583.3 1.9 copy.27
  585.2 70.6 %reshape_reshape.7 = f32[2,64,4,256,4]{2,1,4,3,0:T(8,128)} reshape(f32[2,1,256,4,256]{2,4,3,0,1:T(8,128)S(1)} %copy.27) | data formatting | bytes 4194304 | tf_op jit(solution)/shard_map/reshape;reshape | solution.py:158
  655.8 135.4 %reshape_reshape.6 = f32[2,128,2,512,2]{2,1,4,3,0:T(8,128)} reshape(f32[2,1,256,4,256]{2,4,3,0,1:T(8,128)S(1)} %copy.27) | data formatting | bytes 4194304 | tf_op jit(solution)/shard_map/reshape;reshape | solution.py:155
  791.1 0.8 copy.26
  791.9 1.5 convert_element_type.45
  793.5 20.8 %reduce_sum.108 = f32[2,64,256]{1,2,0:T(8,128)S(1)} reduce(f32[2,64,4,256,4]{2,1,4,3,0:T(8,128)} %reshape_reshape.7, f32[]{:T(128)} %constant.58.clone.1), dimensions={2,4}, to_apply=%region_20.21 | reduce | flops 491520 | bytes 2228228 | tf_op jit(solution)/shard_map/reduce_sum | solution.py:157
  814.3 0.7 copy.30
  815.0 40.9 %reduce_sum.107 = f32[2,128,512]{1,2,0:T(8,128)S(1)} reduce(f32[2,128,2,512,2]{2,1,4,3,0:T(8,128)} %reshape_reshape.6, f32[]{:T(128)} %constant.58.clone.1), dimensions={2,4}, to_apply=%region_19.20 | reduce | flops 393216 | bytes 2621444 | tf_op jit(solution)/shard_map/reduce_sum | solution.py:154
  856.0 0.9 copy.29
  (86 shorter events, 3.0 us)
Async XLA Ops:
  7.2 28.1 %copy-start.1 = (f32[2,2,32,128]{3,2,1,0:T(8,128)S(1)}, f32[2,2,32,128]{3,2,1,0:T(8,128)}, u32[]{:S(2)}) copy-start(f32[2,2,32,128]{3,2,1,0:T(8,128)} %param.12) | copy-start | bytes 196612
  7.2 28.0 %copy-start.2 = (f32[2,32,128]{2,1,0:T(8,128)S(1)}, f32[2,32,128]{2,1,0:T(8,128)}, u32[]{:S(2)}) copy-start(f32[2,32,128]{2,1,0:T(8,128)} %param.15) | copy-start | bytes 98308
  7.2 176.8 %copy-start.6 = (s32[48]{0:T(128)S(1)}, s32[48]{0:T(128)}, u32[]{:S(2)}) copy-start(s32[48]{0:T(128)} %param.18) | copy-start | bytes 580
  7.2 176.8 %copy-start.7 = (s32[48,1]{0,1:T(1,128)S(1)}, s32[48,1]{0,1:T(1,128)}, u32[]{:S(2)}) copy-start(s32[48,1]{0,1:T(1,128)} %param.17) | copy-start | bytes 580
  7.2 176.8 %copy-start.5 = (s32[8]{0:T(128)S(1)}, s32[8]{0:T(128)}, u32[]{:S(2)}) copy-start(s32[8]{0:T(128)} %param.21) | copy-start | bytes 100
  7.2 312.4 %copy-start.8 = (f32[48]{0:T(128)S(1)}, f32[48]{0:T(128)}, u32[]{:S(2)}) copy-start(f32[48]{0:T(128)} %param.20) | copy-start | bytes 580
  7.2 321.4 %copy-start.4 = (s32[2,48]{1,0:T(2,128)S(1)}, s32[2,48]{1,0:T(2,128)}, u32[]{:S(2)}) copy-start(s32[2,48]{1,0:T(2,128)} %param.19) | copy-start | bytes 1156
  7.2 536.2 %all-gather.2.cloned.1.call-start = ((), (), s32[]{:S(2)}) async-start(), calls=%async_computation | async-start | bytes 17825792 | tf_op jit(solution)/shard_map/all_gather | solution.py:146
  10.9 13.4 %collective-permute-start.1 = (f32[2,2,1,128]{3,2,1,0:T(1,128)S(1)}, f32[2,2,1,128]{3,2,1,0:T(1,128)S(1)}, u32[]{:S(2)}, u32[]{:S(2)}) collective-permute-start(f32[2,2,1,128]{3,2,1,0:T(1,128)S(1)} %get-tuple-element.92), channel_id=1, source_target_pairs={{16,0},{32,16},{48,32},{64,48},{80,64},{96,80},{112,96},{17,1},{33... | collective-permute-start | bytes 6152 | tf_op jit(solution)/shard_map/ppermute | solution.py:25
  12.8 11.5 %collective-permute-start = (f32[2,2,1,128]{3,2,1,0:T(1,128)S(1)}, f32[2,2,1,128]{3,2,1,0:T(1,128)S(1)}, u32[]{:S(2)}, u32[]{:S(2)}) collective-permute-start(f32[2,2,1,128]{3,2,1,0:T(1,128)S(1)} %get-tuple-element.93), channel_id=1, source_target_pairs={{0,16},{16,32},{32,48},{48,64},{64,80},{80,96},{96,112},{1,17},{17... | collective-permute-start | bytes 6152 | tf_op jit(solution)/shard_map/ppermute | solution.py:22
  16.1 15.3 %collective-permute-start.5 = (f32[2,1,1,128]{3,2,1,0:T(1,128)S(1)}, f32[2,1,1,128]{3,2,1,0:T(1,128)S(1)}, u32[]{:S(2)}, u32[]{:S(2)}) collective-permute-start(f32[2,1,1,128]{3,2,1,0:T(1,128)S(1)} %slice.201), channel_id=1, source_target_pairs={{0,16},{16,32},{32,48},{48,64},{64,80},{80,96},{96,112},{1,17},{17... | collective-permute-start | bytes 3080 | tf_op jit(solution)/shard_map/ppermute | solution.py:33
  19.1 5.1 collective-permute-start.3
  25.2 8.7 %collective-permute-start.2 = (f32[2,2,34,1]{3,2,1,0:T(8,128)S(1)}, f32[2,2,34,1]{3,2,1,0:T(8,128)S(1)}, u32[]{:S(2)}, u32[]{:S(2)}) collective-permute-start(f32[2,2,34,1]{3,2,1,0:T(8,128)S(1)} %get-tuple-element.82), channel_id=1, source_target_pairs={{1,0},{2,1},{3,2},{4,3},{5,4},{6,5},{7,6},{8,7},{9,8},{10,9},{11,1... | collective-permute-start | bytes 1640 | tf_op jit(solution)/shard_map/ppermute | solution.py:25
  26.5 8.7 %collective-permute-start.4 = (f32[2,2,34,1]{3,2,1,0:T(8,128)S(1)}, f32[2,2,34,1]{3,2,1,0:T(8,128)S(1)}, u32[]{:S(2)}, u32[]{:S(2)}) collective-permute-start(f32[2,2,34,1]{3,2,1,0:T(8,128)S(1)} %get-tuple-element.83), channel_id=1, source_target_pairs={{0,1},{1,2},{2,3},{3,4},{4,5},{5,6},{6,7},{7,8},{8,9},{9,10},{10,1... | collective-permute-start | bytes 1640 | tf_op jit(solution)/shard_map/ppermute | solution.py:22
  171.2 4.3 collective-permute-start.7
  173.1 4.9 collective-permute-start.6
  178.1 6.3 collective-permute-start.8
  179.4 6.6 collective-permute-start.9
  314.9 4.8 collective-permute-start.11
  317.7 4.9 collective-permute-start.10
  322.7 6.3 collective-permute-start.12
  324.0 6.6 collective-permute-start.13
  459.7 4.9 collective-permute-start.15
  462.7 4.9 collective-permute-start.14
  467.7 6.3 collective-permute-start.16
  469.0 6.6 collective-permute-start.17
  542.9 11.3 %copy-start.3 = (f32[2,2,32,128]{3,2,1,0:T(8,128)}, f32[2,2,32,128]{3,2,1,0:T(8,128)S(1)}, u32[]{:S(2)}) copy-start(f32[2,2,32,128]{3,2,1,0:T(8,128)S(1)} %get-tuple-element.97) | copy-start | bytes 196612
  581.9 1.4 copy-start
Sparse Core Ops, SparseCore 0:
  10.8 117.5 all-gather.1
where the time goes:
time: 867 us; the launch traced here: 864 us
  blocking collectives  459 us (53%)
  local copies, waits for them, and re-layouts  229 us (26%)
  other arithmetic  79.1 us (9%)
  starting transfers between devices  48.5 us (6%)
  waiting for transfers between devices  19.3 us (2%)
  matrix products  14.5 us (2%)
  between operations  14.5 us (2%)
    psum x4, blocking collectives, squares_sum(): return lax.psum(section_dot(residual, residual), ('row', 'col'))  260 us
    psum x3, blocking collectives, shards(): lax.psum(section_dot(direction, applied), ('row', 'col'))  199 us
    another operation x1, local copies, waits for them, and re-layouts, shards(): warped.reshape(S, rows_local // 2, 2, cols_local // 2, 2)  135 us
    another operation x1, local copies, waits for them, and re-layouts, shards(): warped.reshape(S, rows_local // 4, 4, cols_local // 4, 4)  70.6 us
    reduce_sum x1, other arithmetic, shards(): jnp.mean(warped.reshape(S, rows_local // 2, 2, cols_local // 2, 2), axis=...  40.9 us
    ppermute x8, starting transfers between devices, extended(): lax.ppermute(lax.slice_in_dim(block, block.shape[dim] - width, None, axis...  27.2 us
    reduce_sum x1, other arithmetic, shards(): jnp.mean(warped.reshape(S, rows_local // 4, 4, cols_local // 4, 4), axis=...  20.8 us
  transfers between devices with their start and end apart: 19, of which 12 were waited for; matrix products, arithmetic and copies ran while one was open for 1% of the time, Pallas kernels for 0%

commit v1 on v0

v1 whole, which is shorter than its diff:
```python
import jax
import jax.numpy as jnp
from jax import lax
from jax.experimental import pallas as pl
from jax.experimental.pallas import tpu as pltpu
from jax.sharding import PartitionSpec as P

S = 2
TILE = 256
SPACING = 8
K = 6
ITERS = 4
TC = 4
ENT_DEV = 48
VR = 32
VC = 128
N_ROW = 8
N_COL = 16
WIDE = TC * TILE
ROWS = VR + 16
COLS = 2 * VC
MESH = pl.DeviceIdType.MESH
F32 = jnp.float32
BF16 = jnp.bfloat16


def flipped(v, mask):
    if mask == 1:
        return v + 1 - 2 * lax.rem(v, 2)
    return 3 - v


def peer_col(y, z, mask, i):
    py = flipped(y, mask) if i % 2 == 1 else y
    pz = flipped(z, mask) if i // 2 == 1 else z
    return pz * 4 + py


GATHER_MASK = (1, 3)
SCATTER_MASK = (3, 1)


def relax_kernel(
    load_ref, stiff_ref, crack_ref, anchor_ref, meta_ref, images_ref,
    disp_ref, resid_ref, metas_ref, gathered_ref,
    fields, strips, halo_v, halo_h, halo_c,
    coef, xs, rs, ps, qs, ws,
    part_a, part_b, got_a, got_b, note, notes,
    halo_send, halo_recv, send_a, recv_a, send_b, recv_b,
    note_send, note_recv, tile_send, tile_recv,
):
    r = lax.axis_index("row")
    c = lax.axis_index("col")
    y = lax.rem(c, 4)
    z = c // 4
    up, down = lax.rem(r + N_ROW - 1, N_ROW), lax.rem(r + 1, N_ROW)
    left, right = lax.rem(c + N_COL - 1, N_COL), lax.rem(c + 1, N_COL)
    corners = ((up, left), (up, right), (down, left), (down, right))

    barrier = pltpu.get_barrier_semaphore()

    @pl.loop(1, N_ROW)
    def _(d):
        pl.semaphore_signal(barrier, inc=1, device_id=(lax.rem(r + d, N_ROW), c), device_id_type=MESH)

    @pl.loop(1, N_COL)
    def _(d):
        pl.semaphore_signal(barrier, inc=1, device_id=(r, lax.rem(c + d, N_COL)), device_id_type=MESH)

    for corner in corners:
        pl.semaphore_signal(barrier, inc=1, device_id=corner, device_id_type=MESH)

    for s in range(S):
        for k in range(2):
            fields[2 * s + k] = load_ref[s, k]
            fields[4 + 2 * s + k] = stiff_ref[s, k] * crack_ref[s, k].astype(F32)
        fields[8 + s] = anchor_ref[s]
    lane = lax.broadcasted_iota(jnp.int32, (VR, VC), 1)
    first = jnp.zeros((VR, VC), F32)
    last = jnp.zeros((VR, VC), F32)
    for f in range(10):
        block = fields[f]
        here = (lane >= 4 * f) & (lane < 4 * f + 4)
        first = jnp.where(here, block if f == 0 else pltpu.roll(block, 4 * f, 1), first)
        last = jnp.where(here, pltpu.roll(block, 4 * f + 4, 1), last)
    strips[0] = first
    strips[1] = last

    pl.semaphore_wait(barrier, N_ROW - 1 + N_COL - 1 + 4)

    halo = []
    for n, (source, target, device) in enumerate((
        (fields.at[:, pl.ds(VR - 8, 8), :], halo_v.at[0], (down, c)),
        (fields.at[:, pl.ds(0, 8), :], halo_v.at[1], (up, c)),
        (strips.at[1], halo_h.at[0], (r, right)),
        (strips.at[0], halo_h.at[1], (r, left)),
        (strips.at[1, pl.ds(VR - 8, 8)], halo_c.at[0], (down, right)),
        (strips.at[0, pl.ds(VR - 8, 8)], halo_c.at[1], (down, left)),
        (strips.at[1, pl.ds(0, 8)], halo_c.at[2], (up, right)),
        (strips.at[0, pl.ds(0, 8)], halo_c.at[3], (up, left)),
    )):
        halo.append(pltpu.make_async_remote_copy(
            src_ref=source, dst_ref=target, send_sem=halo_send.at[n], recv_sem=halo_recv.at[n],
            device_id=device, device_id_type=MESH))
    for copy in halo:
        copy.start()

    tiles = []
    for i in (3, 1, 2):
        for s in range(S):
            tiles.append(pltpu.make_async_remote_copy(
                src_ref=images_ref.at[s], dst_ref=gathered_ref.at[s, i - 1],
                send_sem=tile_send.at[s, i - 1], recv_sem=tile_recv.at[s, i - 1],
                device_id=(r, peer_col(y, z, GATHER_MASK[s], i)), device_id_type=MESH))
    for copy in tiles:
        copy.start()

    for copy in halo:
        copy.wait_recv()

    wide_row = lax.broadcasted_iota(jnp.int32, (ROWS, VC), 0) + r * VR - 8
    wide_lane = lax.broadcasted_iota(jnp.int32, (ROWS, VC), 1)
    side_col = jnp.where(wide_lane < VC // 2, wide_lane + VC, wide_lane - VC) + c * VC
    row_in = (wide_row >= 0) & (wide_row < VR * N_ROW)
    side_in = row_in & (side_col >= 0) & (side_col < VC * N_COL)
    from_left = jnp.concatenate([halo_c[0], halo_h[0], halo_c[2]], axis=0)
    from_right = jnp.concatenate([halo_c[1], halo_h[1], halo_c[3]], axis=0)

    def widened(f):
        own = jnp.concatenate([halo_v[0, f], fields[f], halo_v[1, f]], axis=0)
        to_left = pltpu.roll(from_left, 124 - 4 * f, 1)
        to_right = from_right if f == 0 else pltpu.roll(from_right, VC - 4 * f, 1)
        side = jnp.where(wide_lane < 4, to_right, jnp.where(wide_lane >= 124, to_left, 0.0))
        return jnp.concatenate(
            [jnp.where(row_in, own, 0.0), jnp.where(side_in, side, 0.0)], axis=1)

    inside = jnp.concatenate([row_in.astype(F32), side_in.astype(F32)], axis=1)
    for s in range(S):
        to_right = widened(4 + 2 * s)
        to_low = widened(5 + 2 * s)
        to_left = pltpu.roll(to_right, 1, 1) * inside
        to_high = pltpu.roll(to_low, 1, 0) * inside
        coef[s, 0] = widened(8 + s) + to_right + to_left + to_low + to_high
        coef[s, 1] = to_right
        coef[s, 2] = to_left
        coef[s, 3] = to_low
        coef[s, 4] = to_high
        for k in range(2):
            rs[2 * s + k] = widened(2 * s + k)
    zero = jnp.zeros((ROWS, COLS), F32)
    for f in range(4):
        xs[f] = zero
        ps[f] = zero
        qs[f] = zero

    def step(it, carry):
        sums = []
        for s in range(S):
            rr = jnp.zeros((8, VC), F32)
            rw = jnp.zeros((8, VC), F32)
            for k in range(2):
                v = rs[2 * s + k]
                w = coef[s, 0] * v
                w = w - coef[s, 1] * pltpu.roll(v, COLS - 1, 1)
                w = w - coef[s, 2] * pltpu.roll(v, 1, 1)
                w = w - coef[s, 3] * pltpu.roll(v, ROWS - 1, 0)
                w = w - coef[s, 4] * pltpu.roll(v, 1, 0)
                ws[2 * s + k] = w
                own_v = v[8:8 + VR, 0:VC]
                own_w = w[8:8 + VR, 0:VC]
                rr = rr + jnp.sum((own_v * own_v).reshape(VR // 8, 8, VC), axis=0)
                rw = rw + jnp.sum((own_v * own_w).reshape(VR // 8, 8, VC), axis=0)
            sums.append((jnp.sum(rr, axis=0, keepdims=True), jnp.sum(rw, axis=0, keepdims=True)))
        part_a[it] = jnp.concatenate(
            [sums[0][0], sums[1][0], sums[0][1], sums[1][1], jnp.zeros((4, VC), F32)], axis=0)

        @pl.loop(1, N_ROW)
        def _(d):
            pltpu.make_async_remote_copy(
                src_ref=part_a.at[it], dst_ref=got_a.at[it, d - 1], send_sem=send_a.at[it],
                recv_sem=recv_a.at[it], device_id=(lax.rem(r + d, N_ROW), c), device_id_type=MESH).start()

        pltpu.make_async_remote_copy(
            src_ref=got_a.at[it], dst_ref=got_a.at[it], send_sem=send_a.at[it],
            recv_sem=recv_a.at[it], device_id=(down, c), device_id_type=MESH).wait_recv()
        part_b[it] = part_a[it] + jnp.sum(got_a[it], axis=0)

        @pl.loop(1, N_COL)
        def _(d):
            pltpu.make_async_remote_copy(
                src_ref=part_b.at[it], dst_ref=got_b.at[it, d - 1], send_sem=send_b.at[it],
                recv_sem=recv_b.at[it], device_id=(r, lax.rem(c + d, N_COL)), device_id_type=MESH).start()

        pltpu.make_async_remote_copy(
            src_ref=got_b.at[it], dst_ref=got_b.at[it], send_sem=send_b.at[it],
            recv_sem=recv_b.at[it], device_id=(r, right), device_id_type=MESH).wait_recv()
        total = jnp.sum(part_b[it] + jnp.sum(got_b[it], axis=0), axis=1, keepdims=True)
        rr = total[0:2]
        rw = total[2:4]
        rr_old, alpha_old = carry
        beta = jnp.where(it == 0, 0.0, rr / rr_old)
        alpha = rr / (rw - beta * rr / alpha_old)
        for s in range(S):
            a = alpha[s:s + 1]
            b = beta[s:s + 1]
            for k in range(2):
                f = 2 * s + k
                p = rs[f] + b * ps[f]
                q = ws[f] + b * qs[f]
                ps[f] = p
                qs[f] = q
                xs[f] = xs[f] + a * p
                rs[f] = rs[f] - a * q
        return rr, alpha

    lax.fori_loop(0, ITERS, step, (jnp.ones((2, 1), F32), jnp.ones((2, 1), F32)))

    rows = [xs[f, pl.ds(8 + VR // 2, 1), pl.ds(0, VC)] for f in range(4)]
    note[...] = jnp.concatenate([meta_ref[pl.ds(0, 4), :]] + rows, axis=0)
    told = []
    for s in range(S):
        for i in (1, 2, 3):
            told.append(pltpu.make_async_remote_copy(
                src_ref=note, dst_ref=notes.at[s, i - 1],
                send_sem=note_send.at[s, i - 1], recv_sem=note_recv.at[s, i - 1],
                device_id=(r, peer_col(y, z, SCATTER_MASK[s], i)), device_id_type=MESH))
    for copy in told:
        copy.start()
    for s in range(S):
        metas_ref[s, 0] = note[...]
        for k in range(2):
            f = 2 * s + k
            disp_ref[s, k] = xs[f, pl.ds(8, VR), pl.ds(0, VC)]
            resid_ref[s, k] = rs[f, pl.ds(8, VR), pl.ds(0, VC)]
    for copy in told:
        copy.wait_recv()
    for s in range(S):
        for i in (1, 2, 3):
            metas_ref[s, i] = notes[s, i - 1]

    for copy in told:
        copy.wait_send()
    for copy in halo:
        copy.wait_send()

    @pl.loop(0, ITERS)
    def _(it):
        pltpu.make_async_remote_copy(
            src_ref=got_a.at[it], dst_ref=got_a.at[it], send_sem=send_a.at[it],
            recv_sem=recv_a.at[it], device_id=(down, c), device_id_type=MESH).wait_send()
        pltpu.make_async_remote_copy(
            src_ref=got_b.at[it], dst_ref=got_b.at[it], send_sem=send_b.at[it],
            recv_sem=recv_b.at[it], device_id=(r, right), device_id_type=MESH).wait_send()

    for copy in tiles:
        copy.wait()


def relax(load_force, stiffness, cracks, anchor, meta, images):
    vmem = pl.BlockSpec(memory_space=pltpu.VMEM)
    anywhere = pl.BlockSpec(memory_space=pl.ANY)
    dma = pltpu.SemaphoreType.DMA
    wide = (ROWS, COLS)
    return pl.pallas_call(
        relax_kernel,
        out_shape=(
            jax.ShapeDtypeStruct((S, 2, VR, VC), F32),
            jax.ShapeDtypeStruct((S, 2, VR, VC), F32),
            jax.ShapeDtypeStruct((S, 4, 8, VC), F32),
            jax.ShapeDtypeStruct((S, 3, TILE, WIDE), BF16),
        ),
        in_specs=[vmem] * 5 + [anywhere],
        out_specs=(vmem, vmem, vmem, anywhere),
        scratch_shapes=[
            pltpu.VMEM((10, VR, VC), F32),
            pltpu.VMEM((2, VR, VC), F32),
            pltpu.VMEM((2, 10, 8, VC), F32),
            pltpu.VMEM((2, VR, VC), F32),
            pltpu.VMEM((4, 8, VC), F32),
            pltpu.VMEM((S, 5) + wide, F32),
            pltpu.VMEM((4,) + wide, F32),
            pltpu.VMEM((4,) + wide, F32),
            pltpu.VMEM((4,) + wide, F32),
            pltpu.VMEM((4,) + wide, F32),
            pltpu.VMEM((4,) + wide, F32),
            pltpu.VMEM((ITERS, 8, VC), F32),
            pltpu.VMEM((ITERS, 8, VC), F32),
            pltpu.VMEM((ITERS, N_ROW - 1, 8, VC), F32),
            pltpu.VMEM((ITERS, N_COL - 1, 8, VC), F32),
            pltpu.VMEM((8, VC), F32),
            pltpu.VMEM((S, 3, 8, VC), F32),
            dma((8,)), dma((8,)),
            dma((ITERS,)), dma((ITERS,)), dma((ITERS,)), dma((ITERS,)),
            dma((S, 3)), dma((S, 3)), dma((S, 3)), dma((S, 3)),
        ],
        compiler_params=pltpu.CompilerParams(
            collective_id=0, has_side_effects=True, vmem_limit_bytes=32 * 1024 * 1024),
        name="relax_and_gather",
    )(load_force, stiffness, cracks, anchor, meta, images)


def warp_kernel(meta_ref, images_ref, gathered_ref, part_ref, tiles, acc, out, sems, out_sems):
    c = lax.axis_index("col")
    y = lax.rem(c, 4)
    z = c // 4
    loads = []
    for s in range(S):
        loads.append(pltpu.make_async_copy(images_ref.at[s], tiles.at[s, 0], sems.at[s, 0]))
        loads.append(pltpu.make_async_copy(
            gathered_ref.at[s], tiles.at[s, pl.ds(1, 3)], sems.at[s, 1]))
    for copy in loads:
        copy.start()
    for copy in loads:
        copy.wait()
    row = lax.broadcasted_iota(jnp.int32, (TILE, TILE), 0)
    lane = lax.broadcasted_iota(jnp.int32, (TILE, TILE), 1)
    apart = (lane - row).astype(F32)

    def tent(offset):
        return jnp.maximum(0.0, 1.0 - jnp.abs(offset)).astype(BF16)

    for s in range(S):
        mask = GATHER_MASK[s]

        def target(n, carry):
            i = n // TC
            j = lax.rem(n, TC)
            acc[...] = jnp.zeros((TILE, TILE), F32)

            def entry(k, carry):
                e = s * 24 + j * K + k
                code = meta_ref[s, i, 0, e].astype(jnp.int32)
                weight = meta_ref[s, i, 3, e]
                owner = code // 4
                tile = lax.rem(code, 4)
                oy = lax.rem(owner, 4)
                oz = owner // 4
                mine = ((oy == y) | (oy == flipped(y, mask))) & ((oz == z) | (oz == flipped(z, mask)))

                @pl.when(mine & (weight > 0.0))
                def _():
                    slot = jnp.where(oy == y, 0, 1) + jnp.where(oz == z, 0, 2)
                    at = 32 * j + 16
                    sy = meta_ref[s, i, 1, e] + SPACING * meta_ref[s, i, 4 + 2 * s, at]
                    sx = meta_ref[s, i, 2, e] + SPACING * meta_ref[s, i, 5 + 2 * s, at]
                    source = tiles[s, slot, :, pl.ds(pl.multiple_of(tile * TILE, TILE), TILE)]
                    across = jnp.dot(source, tent(-apart - sx), preferred_element_type=F32)
                    down = jnp.dot(tent(apart - sy), across.astype(BF16), preferred_element_type=F32)
                    acc[...] += weight * down

                return carry

            lax.fori_loop(0, K, entry, 0)
            out[s, i, :, pl.ds(pl.multiple_of(j * TILE, TILE), TILE)] = acc[...].astype(BF16)

            @pl.when(j == TC - 1)
            def _():
                pltpu.make_async_copy(out.at[s, i], part_ref.at[s, i], out_sems.at[s, i]).start()

            return carry

        lax.fori_loop(0, 4 * TC, target, 0)

    for s in range(S):
        for i in range(4):
            pltpu.make_async_copy(out.at[s, i], part_ref.at[s, i], out_sems.at[s, i]).wait()


def warp(metas, images, gathered):
    anywhere = pl.BlockSpec(memory_space=pl.ANY)
    dma = pltpu.SemaphoreType.DMA
    return pl.pallas_call(
        warp_kernel,
        out_shape=jax.ShapeDtypeStruct((S, 4, TILE, WIDE), BF16),
        in_specs=[pl.BlockSpec(memory_space=pltpu.SMEM), anywhere, anywhere],
        out_specs=anywhere,
        scratch_shapes=[
            pltpu.VMEM((S, 4, TILE, WIDE), BF16),
            pltpu.VMEM((TILE, TILE), F32),
            pltpu.VMEM((S, 4, TILE, WIDE), BF16),
            dma((S, 2)), dma((S, 4)),
        ],
        compiler_params=pltpu.CompilerParams(vmem_limit_bytes=32 * 1024 * 1024),
        name="warp_partials",
    )(metas, images, gathered)


CHUNK = 64
CHUNKS = TILE // CHUNK


def scatter_kernel(part_ref, zero_ref, one_ref, two_ref, own, got, pool, half, quarter, own_sem, send_sem, recv_sem):
    r = lax.axis_index("row")
    c = lax.axis_index("col")
    y = lax.rem(c, 4)
    z = c // 4
    barrier = pltpu.get_barrier_semaphore()
    for s in range(S):
        for i in (1, 2, 3):
            pl.semaphore_signal(
                barrier, inc=1, device_id=(r, peer_col(y, z, SCATTER_MASK[s], i)), device_id_type=MESH)
    mine = pltpu.make_async_copy(part_ref.at[:, 0], own, own_sem)
    mine.start()
    row = lax.broadcasted_iota(jnp.int32, (TILE, VC), 0)
    lane = lax.broadcasted_iota(jnp.int32, (TILE, VC), 1)
    pool[...] = jnp.where(row // 2 == lane, 0.25, 0.0).astype(BF16)
    pl.semaphore_wait(barrier, 6)

    def sent(q, s, i):
        rows = pl.ds(pl.multiple_of(q * CHUNK, CHUNK), CHUNK)
        return pltpu.make_async_remote_copy(
            src_ref=part_ref.at[s, i, rows], dst_ref=got.at[s, i - 1, rows],
            send_sem=send_sem.at[s, i - 1, q], recv_sem=recv_sem.at[s, i - 1, q],
            device_id=(r, peer_col(y, z, SCATTER_MASK[s], i)), device_id_type=MESH)

    @pl.loop(0, CHUNKS)
    def _(q):
        for i in (3, 1, 2):
            for s in range(S):
                sent(q, s, i).start()

    mine.wait()

    def pooled(block):
        high = block.astype(BF16)
        low = (block - high.astype(F32)).astype(BF16)
        matrix = pool[...]
        return (jnp.dot(high, matrix, preferred_element_type=F32)
                + jnp.dot(low, matrix, preferred_element_type=F32))

    @pl.loop(0, CHUNKS)
    def _(q):
        rows = pl.ds(pl.multiple_of(q * CHUNK, CHUNK), CHUNK)
        for s in range(S):
            for i in (1, 2, 3):
                sent(q, s, i).wait_recv()
            for j in range(TC):
                cols = pl.ds(j * TILE, TILE)
                block = own[s, rows, cols].astype(F32)
                for i in range(3):
                    block = block + got[s, i, rows, cols].astype(F32)
                zero_ref[s, rows, cols] = block.astype(BF16)
                half[j] = pooled(block)
            ones = []
            for j in range(TC):
                piece = half[j, pl.ds(0, CHUNK // 2, stride=2), :] + half[j, pl.ds(1, CHUNK // 2, stride=2), :]
                one_ref[s, pl.ds(pl.multiple_of(q * (CHUNK // 2), CHUNK // 2), CHUNK // 2), pl.ds(j * VC, VC)] = (
                    piece.astype(BF16))
                ones.append(piece)
            for j in range(2):
                quarter[j] = pooled(jnp.concatenate(ones[2 * j:2 * j + 2], axis=1))
                piece = quarter[j, pl.ds(0, CHUNK // 4, stride=2), :] + quarter[j, pl.ds(1, CHUNK // 4, stride=2), :]
                two_ref[s, pl.ds(pl.multiple_of(q * (CHUNK // 4), CHUNK // 4), CHUNK // 4), pl.ds(j * VC, VC)] = (
                    piece.astype(BF16))

    @pl.loop(0, CHUNKS)
    def _(q):
        for i in (3, 1, 2):
            for s in range(S):
                sent(q, s, i).wait_send()


def scatter(part):
    vmem = pl.BlockSpec(memory_space=pltpu.VMEM)
    dma = pltpu.SemaphoreType.DMA
    return pl.pallas_call(
        scatter_kernel,
        out_shape=(
            jax.ShapeDtypeStruct((S, TILE, WIDE), BF16),
            jax.ShapeDtypeStruct((S, TILE // 2, WIDE // 2), BF16),
            jax.ShapeDtypeStruct((S, TILE // 4, WIDE // 4), BF16),
        ),
        in_specs=[pl.BlockSpec(memory_space=pl.ANY)],
        out_specs=(vmem, vmem, vmem),
        scratch_shapes=[
            pltpu.VMEM((S, TILE, WIDE), BF16),
            pltpu.VMEM((S, 3, TILE, WIDE), BF16),
            pltpu.VMEM((TILE, VC), BF16),
            pltpu.VMEM((TC, CHUNK, VC), F32),
            pltpu.VMEM((2, CHUNK // 2, VC), F32),
            dma, dma((S, 3, CHUNKS)), dma((S, 3, CHUNKS)),
        ],
        compiler_params=pltpu.CompilerParams(
            collective_id=1, has_side_effects=True, vmem_limit_bytes=32 * 1024 * 1024),
        name="scatter_and_pool",
    )(part)


def shards(load_force, stiffness, cracks, anchor, images, owners, source_tile, offsets, blend_weight, counts):
    slot = jnp.arange(ENT_DEV, dtype=jnp.int32) % K
    weights = jnp.where(slot < jnp.repeat(counts, K), blend_weight, 0.0)
    codes = (owners[:, 0] * TC + source_tile).astype(F32)
    meta = jnp.concatenate([codes[None], offsets.astype(F32), weights[None]], axis=0)
    meta = jnp.pad(meta, ((0, 4), (0, VC - ENT_DEV)))
    displacement, residual, metas, gathered = relax(load_force, stiffness, cracks, anchor, meta, images)
    part = warp(metas, images, gathered)
    level_zero, level_one, level_two = scatter(part)
    return displacement, residual, level_zero, level_one, level_two


def solution(mesh):
    flat = P(("row", "col"))
    in_specs = (
        P(None, None, "row", "col"),
        P(None, None, "row", "col"),
        P(None, None, "row", "col"),
        P(None, "row", "col"),
        P(None, "row", "col"),
        P(("row", "col"), None),
        flat,
        P(None, ("row", "col")),
        flat,
        flat,
    )
    out_specs = (
        P(None, None, "row", "col"),
        P(None, None, "row", "col"),
        P(None, "row", "col"),
        P(None, "row", "col"),
        P(None, "row", "col"),
    )
    return jax.shard_map(shards, mesh=mesh, in_specs=in_specs, out_specs=out_specs, check_vma=False)
```

time: 867 us -> 131 us (0.15)
  the two profiles are of different devices: /device:TPU:4 before, /device:TPU:1 now
where the time goes in v1:
time: 131 us
  Pallas kernels  118 us (90%)
  local copies, waits for them, and re-layouts  10.1 us (8%)
  other arithmetic  2.04 us (2%)
    pallas_call x1, Pallas kernels, relax(): pl.pallas_call(relax_kernel, out_shape=(jax.ShapeDtypeStruct((S, 2, VR, V...  65.5 us
    pallas_call x1, Pallas kernels, scatter(): pl.pallas_call(scatter_kernel, out_shape=(jax.ShapeDtypeStruct((S, TILE,...  30.8 us
    pallas_call x1, Pallas kernels, warp(): pl.pallas_call(warp_kernel, out_shape=jax.ShapeDtypeStruct((S, 4, TILE, W...  21.8 us
    unnamed x17, local copies, waits for them, and re-layouts  9.28 us

profile of v1, /device:TPU:1, one launch (start us, length us, event | category | flops | bytes accessed | tf_op | source)
XLA Modules:
  0.0 130.8 jit_solution(16304940020836953527)
XLA Ops:
  0.6 0.7 fusion.1
  1.3 0.7 convert_element_type.9
  2.0 0.7 broadcast_in_dim.14
  2.7 0.1 reshape.15
  2.8 0.7 fusion.2
  3.5 0.0 copy-start
  3.5 1.2 copy-done
  4.7 0.0 copy-start.2
  4.7 0.8 copy-done.2
  5.5 0.0 copy-start.3
  5.5 0.8 copy-done.3
  6.4 0.0 copy-start.4
  6.4 0.8 copy-done.4
  7.2 0.0 copy-start.5
  7.2 0.8 copy-done.5
  8.0 65.5 %relax_and_gather.1 = (f32[2,2,32,128]{3,2,1,0:T(8,128)S(1)}, f32[2,2,32,128]{3,2,1,0:T(8,128)S(1)}, f32[2,4,8,128]{3,2,1,0:T(8,128)S(1)}, bf16[2,3,256,1024]{3,2,1,0:T(8,128)(2,1)S(1)}) custom-call(f32[2,2,32,128]{3,2,1,0:T(8,128)S(1)} %copy-done.2, f32[2,2,32,128]{3,2,1,0:T(8,128)S(1)} %copy-done.3, s32[2,2,32,128]{3,2,1,0:T(8,128)S(1)} %copy-done.4, ...), custom_call_target="tpu_custom_call" | custom-call | tf_op jit(solution)/shard_map/relax_and_gather/pallas_call | solution.py:264
  73.4 0.0 copy-start.1
  73.5 1.2 copy-done.1
  74.7 21.8 %warp_partials.1.part_ref = bf16[2,4,256,1024]{3,2,1,0:T(8,128)(2,1)S(1)} custom-call(f32[2,4,8,128]{3,2,1,0:T(8,128)S(1)} %get-tuple-element.14.meta_ref, bf16[2,256,1024]{2,1,0:T(8,128)(2,1)S(1)} %copy-done.1, bf16[2,3,256,1024]{3,2,1,0:T(8,128)(2,1)S(1)} %get-tuple-element.15.gathered_ref), custom_call_target="tpu_custom_call" | custom-call | tf_op jit(solution)/shard_map/warp_partials/pallas_call | solution.py:372
  96.4 30.8 %scatter_and_pool.1 = (bf16[2,256,1024]{2,1,0:T(8,128)(2,1)S(1)}, bf16[2,128,512]{2,1,0:T(8,128)(2,1)S(1)}, bf16[2,64,256]{2,1,0:T(8,128)(2,1)S(1)}) custom-call(bf16[2,4,256,1024]{3,2,1,0:T(8,128)(2,1)S(1)} %warp_partials.1.part_ref), custom_call_target="tpu_custom_call" | custom-call | tf_op jit(solution)/shard_map/scatter_and_pool/pallas_call | solution.py:466
  127.3 0.6 copy.20
  127.9 0.6 copy.21
  128.5 1.0 copy.22
  129.5 0.7 copy.23
  130.2 0.6 copy.24
  (1 shorter events, 0.0 us)
Async XLA Ops:
  3.5 1.2 copy-start
  4.7 0.8 copy-start.2
  5.5 0.8 copy-start.3
  6.4 0.8 copy-start.4
  7.2 0.8 copy-start.5
  73.4 1.2 copy-start.1

commit v2 on v1

v2 whole, which is shorter than its diff:
```python
import jax
import jax.numpy as jnp
from jax import lax
from jax.experimental import pallas as pl
from jax.experimental.pallas import tpu as pltpu
from jax.sharding import PartitionSpec as P

S = 2
TILE = 256
SPACING = 8
K = 6
ITERS = 4
TC = 4
ENT_DEV = 48
VR = 32
VC = 128
N_ROW = 8
N_COL = 16
WIDE = TC * TILE
ROWS = VR + 16
COLS = 2 * VC
MESH = pl.DeviceIdType.MESH
F32 = jnp.float32
BF16 = jnp.bfloat16


def flipped(v, mask):
    if mask == 1:
        return v + 1 - 2 * lax.rem(v, 2)
    return 3 - v


def peer_col(y, z, mask, i):
    py = flipped(y, mask) if i % 2 == 1 else y
    pz = flipped(z, mask) if i // 2 == 1 else z
    return pz * 4 + py


GATHER_MASK = (1, 3)
SCATTER_MASK = (3, 1)


NOTE = 32


def relax_kernel(
    load_hbm, stiff_hbm, crack_hbm, anchor_hbm, owner_hbm, source_hbm, offset_hbm, blend_hbm, count_hbm, images_hbm,
    disp_ref, resid_ref, metas_ref, tiles_ref,
    fields, stiff, crack, owner, source, offset, blend, count,
    strips, halo_v, halo_h, halo_c, coef, rs, ws, us, qs, ts, ps, xs,
    part_a, part_b, got_a, got_b, note, notes,
    load_sem, own_sem, halo_send, halo_recv, send_a, recv_a, send_b, recv_b,
    note_send, note_recv, tile_send, tile_recv,
):
    r = lax.axis_index("row")
    c = lax.axis_index("col")
    y = lax.rem(c, 4)
    z = c // 4
    up, down = lax.rem(r + N_ROW - 1, N_ROW), lax.rem(r + 1, N_ROW)
    left, right = lax.rem(c + N_COL - 1, N_COL), lax.rem(c + 1, N_COL)
    corners = ((up, left), (up, right), (down, left), (down, right))

    barrier = pltpu.get_barrier_semaphore()

    @pl.loop(1, N_ROW)
    def _(d):
        pl.semaphore_signal(barrier, inc=1, device_id=(lax.rem(r + d, N_ROW), c), device_id_type=MESH)

    @pl.loop(1, N_COL)
    def _(d):
        pl.semaphore_signal(barrier, inc=1, device_id=(r, lax.rem(c + d, N_COL)), device_id_type=MESH)

    for corner in corners:
        pl.semaphore_signal(barrier, inc=1, device_id=corner, device_id_type=MESH)

    loads = []
    for n, (near, far) in enumerate((
        (stiff_hbm, stiff), (crack_hbm, crack),
        (load_hbm.at[0], fields.at[pl.ds(0, 2)]), (load_hbm.at[1], fields.at[pl.ds(2, 2)]),
        (anchor_hbm, fields.at[pl.ds(8, 2)]),
        (owner_hbm, owner), (source_hbm, source), (offset_hbm, offset), (blend_hbm, blend), (count_hbm, count),
    )):
        loads.append(pltpu.make_async_copy(near, far, load_sem.at[n]))
    for copy in loads:
        copy.start()
    for copy in loads:
        copy.wait()
    for s in range(S):
        for k in range(2):
            fields[4 + 2 * s + k] = stiff[s, k] * crack[s, k].astype(F32)
    lane = lax.broadcasted_iota(jnp.int32, (VR, VC), 1)
    first = jnp.zeros((VR, VC), F32)
    last = jnp.zeros((VR, VC), F32)
    for f in range(10):
        block = fields[f]
        here = (lane >= 4 * f) & (lane < 4 * f + 4)
        first = jnp.where(here, block if f == 0 else pltpu.roll(block, 4 * f, 1), first)
        last = jnp.where(here, pltpu.roll(block, 4 * f + 4, 1), last)
    strips[0] = first
    strips[1] = last

    pl.semaphore_wait(barrier, N_ROW - 1 + N_COL - 1 + 4)

    halo = []
    for n, (near, far, device) in enumerate((
        (fields.at[:, pl.ds(VR - 8, 8), :], halo_v.at[0], (down, c)),
        (fields.at[:, pl.ds(0, 8), :], halo_v.at[1], (up, c)),
        (strips.at[1], halo_h.at[0], (r, right)),
        (strips.at[0], halo_h.at[1], (r, left)),
        (strips.at[1, pl.ds(VR - 8, 8)], halo_c.at[0], (down, right)),
        (strips.at[0, pl.ds(VR - 8, 8)], halo_c.at[1], (down, left)),
        (strips.at[1, pl.ds(0, 8)], halo_c.at[2], (up, right)),
        (strips.at[0, pl.ds(0, 8)], halo_c.at[3], (up, left)),
    )):
        halo.append(pltpu.make_async_remote_copy(
            src_ref=near, dst_ref=far, send_sem=halo_send.at[n], recv_sem=halo_recv.at[n],
            device_id=device, device_id_type=MESH))
    for copy in halo:
        copy.start()

    half = TILE // 2

    def tile_copy(s, n, slot_from, slot_to, part, peer):
        rows = pl.ds(part * half, half)
        near = images_hbm.at[s, rows] if slot_from == 0 else tiles_ref.at[s, slot_from, rows]
        return pltpu.make_async_remote_copy(
            src_ref=near, dst_ref=tiles_ref.at[s, slot_to, rows],
            send_sem=tile_send.at[s, n], recv_sem=tile_recv.at[s, n],
            device_id=(r, peer_col(y, z, GATHER_MASK[s], peer)), device_id_type=MESH)

    direct = [
        [tile_copy(s, 0, 0, 2, 0, 2), tile_copy(s, 1, 0, 1, 1, 1), tile_copy(s, 2, 0, 1, 0, 1), tile_copy(s, 3, 0, 2, 1, 2)]
        for s in range(S)
    ]
    relayed = [[tile_copy(s, 4, 2, 3, 0, 1), tile_copy(s, 5, 1, 3, 1, 2)] for s in range(S)]
    for n in range(4):
        for s in range(S):
            direct[s][n].start()
    own = pltpu.make_async_copy(images_hbm, tiles_ref.at[:, 0], own_sem)
    own.start()

    entry_lane = lax.broadcasted_iota(jnp.int32, (1, ENT_DEV), 1)
    listed = jnp.zeros((1, ENT_DEV), jnp.int32)
    for t in range(ENT_DEV // K):
        listed = jnp.where(entry_lane // K == t, count[:, t:t + 1], listed)
    note[...] = jnp.zeros((NOTE, VC), F32)
    note[0:1, 0:ENT_DEV] = owner[...].astype(F32)
    note[1:2, 0:ENT_DEV] = source[...].astype(F32)
    note[2:4, 0:ENT_DEV] = offset[...].astype(F32)
    note[4:5, 0:ENT_DEV] = jnp.where(lax.rem(entry_lane, K) < listed, blend[...], 0.0)

    for copy in halo:
        copy.wait_recv()

    wide_row = lax.broadcasted_iota(jnp.int32, (ROWS, VC), 0) + r * VR - 8
    wide_lane = lax.broadcasted_iota(jnp.int32, (ROWS, VC), 1)
    side_col = jnp.where(wide_lane < VC // 2, wide_lane + VC, wide_lane - VC) + c * VC
    row_in = (wide_row >= 0) & (wide_row < VR * N_ROW)
    side_in = row_in & (side_col >= 0) & (side_col < VC * N_COL)
    from_left = jnp.concatenate([halo_c[0], halo_h[0], halo_c[2]], axis=0)
    from_right = jnp.concatenate([halo_c[1], halo_h[1], halo_c[3]], axis=0)

    def widened(f):
        center = jnp.concatenate([halo_v[0, f], fields[f], halo_v[1, f]], axis=0)
        to_left = pltpu.roll(from_left, 124 - 4 * f, 1)
        to_right = from_right if f == 0 else pltpu.roll(from_right, VC - 4 * f, 1)
        side = jnp.where(wide_lane < 4, to_right, jnp.where(wide_lane >= 124, to_left, 0.0))
        return jnp.concatenate(
            [jnp.where(row_in, center, 0.0), jnp.where(side_in, side, 0.0)], axis=1)

    inside = jnp.concatenate([row_in.astype(F32), side_in.astype(F32)], axis=1)
    for s in range(S):
        to_right = widened(4 + 2 * s)
        to_low = widened(5 + 2 * s)
        to_left = pltpu.roll(to_right, 1, 1) * inside
        to_high = pltpu.roll(to_low, 1, 0) * inside
        coef[s, 0] = widened(8 + s) + to_right + to_left + to_low + to_high
        coef[s, 1] = to_right
        coef[s, 2] = to_left
        coef[s, 3] = to_low
        coef[s, 4] = to_high
        for k in range(2):
            rs[2 * s + k] = widened(2 * s + k)

    def operate(near, far):
        for f in range(4):
            s = f // 2
            v = near[f]
            w = coef[s, 0] * v
            w = w - coef[s, 1] * pltpu.roll(v, COLS - 1, 1)
            w = w - coef[s, 2] * pltpu.roll(v, 1, 1)
            w = w - coef[s, 3] * pltpu.roll(v, ROWS - 1, 0)
            w = w - coef[s, 4] * pltpu.roll(v, 1, 0)
            far[f] = w

    def core(ref, f):
        return ref[f, pl.ds(8, VR), pl.ds(0, VC)]

    def reduced(n, pairs):
        rows = []
        for one, other in pairs:
            for s in range(S):
                total = jnp.zeros((8, VC), F32)
                for k in range(2):
                    f = 2 * s + k
                    total = total + jnp.sum((core(one, f) * core(other, f)).reshape(VR // 8, 8, VC), axis=0)
                rows.append(jnp.sum(total, axis=0, keepdims=True))
        height = -(-len(rows) // 8) * 8
        if height > len(rows):
            rows.append(jnp.zeros((height - len(rows), VC), F32))
        span = pl.ds(0, height)
        part_a[n, span] = jnp.concatenate(rows, axis=0)

        @pl.loop(1, N_ROW)
        def _(d):
            pltpu.make_async_remote_copy(
                src_ref=part_a.at[n, span], dst_ref=got_a.at[n, d - 1, span], send_sem=send_a.at[n],
                recv_sem=recv_a.at[n], device_id=(lax.rem(r + d, N_ROW), c), device_id_type=MESH).start()

        sum_copy(n, height, 0).wait_recv()
        part_b[n, span] = part_a[n, span] + jnp.sum(got_a[n, :, span], axis=0)

        @pl.loop(1, N_COL)
        def _(d):
            pltpu.make_async_remote_copy(
                src_ref=part_b.at[n, span], dst_ref=got_b.at[n, d - 1, span], send_sem=send_b.at[n],
                recv_sem=recv_b.at[n], device_id=(r, lax.rem(c + d, N_COL)), device_id_type=MESH).start()

        sum_copy(n, height, 1).wait_recv()
        total = part_b[n, span] + jnp.sum(got_b[n, :, span], axis=0)
        total = jnp.sum(total, axis=1, keepdims=True)
        return [total[2 * m:2 * m + 2] for m in range(len(pairs))]

    def sum_copy(n, height, phase):
        got, send, recv = ((got_a, send_a, recv_a), (got_b, send_b, recv_b))[phase]
        return pltpu.make_async_remote_copy(
            src_ref=got.at[n, :, pl.ds(0, height)], dst_ref=got.at[n, :, pl.ds(0, height)],
            send_sem=send.at[n], recv_sem=recv.at[n],
            device_id=((down, c), (r, right))[phase], device_id_type=MESH)

    operate(rs, ws)
    operate(ws, us)
    m0, m1, m2, m3 = reduced(0, ((rs, rs), (rs, ws), (ws, ws), (ws, us)))
    a0 = m0 / m1
    n1 = a0 * a0 * m2 - m0
    b0 = n1 / m0
    g0 = 1.0 + b0
    a1 = n1 / (g0 * g0 * m1 - 2.0 * g0 * a0 * m2 + a0 * a0 * m3)
    for f in range(4):
        s = f // 2
        step0, step1, grow = a0[s:s + 1], a1[s:s + 1], g0[s:s + 1]
        v, w = rs[f], ws[f]
        p = grow * v - step0 * w
        q = grow * w - step0 * us[f]
        ps[f] = p
        qs[f] = q
        xs[f] = step0 * v + step1 * p
        rs[f] = v - step0 * w - step1 * q

    for s in range(S):
        direct[s][0].wait_recv()
        relayed[s][0].start()
        direct[s][1].wait_recv()
        relayed[s][1].start()

    operate(rs, ws)
    middle = 8 + VR // 2
    basis = (xs, ps, rs, ws, qs)
    for b, ref in enumerate(basis):
        for f in range(4):
            note[8 + 4 * b + f:9 + 4 * b + f, :] = ref[f, pl.ds(middle, 1), pl.ds(0, VC)]
    told = []
    for s in range(S):
        for i in (1, 2, 3):
            told.append(pltpu.make_async_remote_copy(
                src_ref=note, dst_ref=notes.at[s, i - 1],
                send_sem=note_send.at[s, i - 1], recv_sem=note_recv.at[s, i - 1],
                device_id=(r, peer_col(y, z, SCATTER_MASK[s], i)), device_id_type=MESH))
    for copy in told:
        copy.start()
    operate(ws, us)
    operate(qs, ts)
    rr, rw, rq, ww, wq, qq, wu, uq, qt = reduced(1, (
        (rs, rs), (rs, ws), (rs, qs), (ws, ws), (ws, qs), (qs, qs), (ws, us), (us, qs), (qs, ts)))
    b1 = rr / n1
    a2 = rr / (rw - b1 * rr / a1)
    q2q2 = ww + 2.0 * b1 * wq + b1 * b1 * qq
    n3 = rr - 2.0 * a2 * (rw + b1 * rq) + a2 * a2 * q2q2
    b2 = n3 / rr
    r3ar3 = rw - 2.0 * a2 * (ww + b1 * wq) + a2 * a2 * (wu + 2.0 * b1 * uq + b1 * b1 * qt)
    a3 = n3 / (r3ar3 - b2 * n3 / a2)

    weights = (None, (a2 + a3 * b2) * b1, a2 + a3 * b2 + a3, -a3 * a2, -a3 * a2 * b1)
    for f in range(4):
        s, k = f // 2, f % 2
        step2, step3 = a2[s:s + 1], a3[s:s + 1]
        grow1, grow2 = b1[s:s + 1], b2[s:s + 1]
        v, w, q = core(rs, f), core(ws, f), core(qs, f)
        p2 = v + grow1 * core(ps, f)
        q2 = w + grow1 * q
        r3 = v - step2 * q2
        p3 = r3 + grow2 * p2
        q3 = w - step2 * (core(us, f) + grow1 * core(ts, f)) + grow2 * q2
        disp_ref[s, k] = core(xs, f) + step2 * p2 + step3 * p3
        resid_ref[s, k] = r3 - step3 * q3

    for copy in told:
        copy.wait_recv()
    note_lane = lax.broadcasted_iota(jnp.int32, (1, VC), 1)
    for s in range(S):
        for i in range(4):
            text = note if i == 0 else notes.at[s, i - 1]
            at = text[0:1, :].astype(jnp.int32)
            at_y, at_z = lax.rem(at, 4), at // 4
            weight = text[4:5, :]
            mine = (at_y == y) | (at_y == flipped(y, GATHER_MASK[s]))
            mine = mine & ((at_z == z) | (at_z == flipped(z, GATHER_MASK[s])))
            mine = mine & (weight > 0.0) & (note_lane < ENT_DEV)
            slot = jnp.where(at_y == y, 0, 1) + jnp.where(at_z == z, 0, 2)
            key = jnp.where(mine, slot * TC + text[1:2, :].astype(jnp.int32), -1)
            shift = text[8 + 2 * s:10 + 2 * s, :]
            for b in range(1, 5):
                shift = shift + weights[b][s:s + 1] * text[8 + 4 * b + 2 * s:10 + 4 * b + 2 * s, :]
            metas_ref[s, i] = jnp.concatenate(
                [key.astype(F32), text[2:4, :], weight, shift, jnp.zeros((2, VC), F32)], axis=0)

    for copy in told:
        copy.wait_send()
    for copy in halo:
        copy.wait_send()
    for n, height in enumerate((8, 24)):
        for phase in range(2):
            sum_copy(n, height, phase).wait_send()
    own.wait()
    for s in range(S):
        direct[s][2].wait_recv()
        direct[s][3].wait_recv()
        for copy in relayed[s]:
            copy.wait()
        for copy in direct[s]:
            copy.wait_send()


def relax(*operands):
    vmem = pl.BlockSpec(memory_space=pltpu.VMEM)
    hbm = pl.BlockSpec(memory_space=pltpu.HBM)
    dma = pltpu.SemaphoreType.DMA
    wide = pltpu.VMEM((4, ROWS, COLS), F32)
    block = (S, 2, VR, VC)
    return pl.pallas_call(
        relax_kernel,
        out_shape=(
            jax.ShapeDtypeStruct(block, F32),
            jax.ShapeDtypeStruct(block, F32),
            jax.ShapeDtypeStruct((S, 4, 8, VC), F32),
            jax.ShapeDtypeStruct((S, 4, TILE, WIDE), BF16),
        ),
        in_specs=[hbm] * 10,
        out_specs=(vmem, vmem, vmem, vmem),
        scratch_shapes=[
            pltpu.VMEM((10, VR, VC), F32),
            pltpu.VMEM(block, F32),
            pltpu.VMEM(block, jnp.int32),
            pltpu.VMEM((1, ENT_DEV), jnp.int32),
            pltpu.VMEM((1, ENT_DEV), jnp.int32),
            pltpu.VMEM((2, ENT_DEV), jnp.int32),
            pltpu.VMEM((1, ENT_DEV), F32),
            pltpu.VMEM((1, ENT_DEV // K), jnp.int32),
            pltpu.VMEM((2, VR, VC), F32),
            pltpu.VMEM((2, 10, 8, VC), F32),
            pltpu.VMEM((2, VR, VC), F32),
            pltpu.VMEM((4, 8, VC), F32),
            pltpu.VMEM((S, 5, ROWS, COLS), F32),
            wide, wide, wide, wide, wide, wide, wide,
            pltpu.VMEM((2, 24, VC), F32),
            pltpu.VMEM((2, 24, VC), F32),
            pltpu.VMEM((2, N_ROW - 1, 24, VC), F32),
            pltpu.VMEM((2, N_COL - 1, 24, VC), F32),
            pltpu.VMEM((NOTE, VC), F32),
            pltpu.VMEM((S, 3, NOTE, VC), F32),
            dma((10,)), dma, dma((8,)), dma((8,)),
            dma((2,)), dma((2,)), dma((2,)), dma((2,)),
            dma((S, 3)), dma((S, 3)), dma((S, 6)), dma((S, 6)),
        ],
        compiler_params=pltpu.CompilerParams(
            collective_id=0, has_side_effects=True, vmem_limit_bytes=32 * 1024 * 1024),
        name="relax_and_gather",
    )(*operands)


BATCH = 2


def warp_kernel(meta_ref, tiles_ref, part_ref, apart, where_list, weight_list):
    def listing(s, n, count):
        i = n // (TC * K)
        e = lax.rem(n, TC * K)
        key = meta_ref[s, i, 0, s * TC * K + e].astype(jnp.int32)
        where_list[count] = ((s * 4 + i) * 32 + e) * 16 + jnp.maximum(key, 0)
        weight_list[count] = meta_ref[s, i, 3, s * TC * K + e]
        return count + jnp.where(key >= 0, 1, 0)

    count = 0
    for s in range(S):
        count = lax.fori_loop(0, 4 * TC * K, lambda n, total, s=s: listing(s, n, total), count)
    for n in range(BATCH - 1):
        where_list[count + n] = 0
        weight_list[count + n] = 0.0

    row = lax.broadcasted_iota(jnp.int32, (TILE, TILE), 0)
    lane = lax.broadcasted_iota(jnp.int32, (TILE, TILE), 1)
    apart[...] = (lane - row).astype(F32).astype(BF16)
    part_ref[...] = jnp.zeros(part_ref.shape, BF16)

    def sampled(shift, side):
        shift = jnp.full((1, TILE), shift, F32)
        low = jnp.floor(shift)
        at_low = jnp.maximum(0.0, 1.0 - jnp.abs(low - shift)).astype(BF16)
        at_high = jnp.maximum(0.0, 1.0 - jnp.abs(low + 1.0 - shift)).astype(BF16)
        low_place = (side * low).astype(BF16)
        high_place = (side * (low + 1.0)).astype(BF16)
        matrix = apart[...]
        return jnp.where(matrix == low_place, at_low, jnp.where(matrix == high_place, at_high, jnp.zeros((), BF16)))

    def entry(n):
        code = where_list[n]
        key = code & 15
        e = (code >> 4) & 31
        place = code >> 9
        s = place >> 2
        i = place & 3
        j = (e * 43) >> 8
        at = s * TC * K + e
        sy = meta_ref[s, i, 1, at] + SPACING * meta_ref[s, i, 4, 32 * j + 16]
        sx = meta_ref[s, i, 2, at] + SPACING * meta_ref[s, i, 5, 32 * j + 16]
        source = tiles_ref[s, key >> 2, :, pl.ds(pl.multiple_of((key & 3) * TILE, TILE), TILE)]
        across = jnp.dot(source, sampled(sx, -1.0), preferred_element_type=F32)
        down = jnp.dot(sampled(sy, 1.0), across.astype(BF16), preferred_element_type=F32)
        return weight_list[n] * down, (s, i, slice(None), pl.ds(pl.multiple_of(j * TILE, TILE), TILE))

    def batch(b, carry):
        found = [entry(b * BATCH + n) for n in range(BATCH)]
        for value, place in found:
            part_ref[place] = (part_ref[place].astype(F32) + value).astype(BF16)
        return carry

    lax.fori_loop(0, (count + BATCH - 1) // BATCH, batch, 0)


def warp(metas, tiles):
    vmem = pl.BlockSpec(memory_space=pltpu.VMEM)
    return pl.pallas_call(
        warp_kernel,
        out_shape=jax.ShapeDtypeStruct((S, 4, TILE, WIDE), BF16),
        in_specs=[pl.BlockSpec(memory_space=pltpu.SMEM), vmem],
        out_specs=vmem,
        scratch_shapes=[
            pltpu.VMEM((TILE, TILE), BF16),
            pltpu.SMEM((256,), jnp.int32),
            pltpu.SMEM((256,), F32),
        ],
        compiler_params=pltpu.CompilerParams(vmem_limit_bytes=32 * 1024 * 1024),
        name="warp_partials",
    )(metas, tiles)


CHUNK = 64
HALVES = 2
SUBS = TILE // CHUNK // HALVES


def scatter_kernel(
    part_ref, zero_ref, one_ref, two_ref,
    relay, onward, got, pool, half, quarter,
    relay_send, relay_recv, direct_send, direct_recv, onward_send, onward_recv,
):
    r = lax.axis_index("row")
    c = lax.axis_index("col")
    y = lax.rem(c, 4)
    z = c // 4
    barrier = pltpu.get_barrier_semaphore()
    for s in range(S):
        for i in (1, 2):
            pl.semaphore_signal(
                barrier, inc=1, device_id=(r, peer_col(y, z, SCATTER_MASK[s], i)), device_id_type=MESH)
    row = lax.broadcasted_iota(jnp.int32, (TILE, VC), 0)
    lane = lax.broadcasted_iota(jnp.int32, (TILE, VC), 1)
    pool[...] = jnp.where(row // 2 == lane, 0.25, 0.0).astype(BF16)
    pl.semaphore_wait(barrier, 2 * S)

    def rows_of(h, u):
        return pl.ds((h * SUBS + u) * CHUNK, CHUNK)

    def copy_to(s, peer, near, far, send, recv):
        return pltpu.make_async_remote_copy(
            src_ref=near, dst_ref=far, send_sem=send, recv_sem=recv,
            device_id=(r, peer_col(y, z, SCATTER_MASK[s], peer)), device_id_type=MESH)

    def to_relay(s, h, u):
        return copy_to(s, h + 1, part_ref.at[s, 3, rows_of(h, u)], relay.at[s, h, u],
                       relay_send.at[s, h, u], relay_recv.at[s, h, u])

    def to_end(s, h, u):
        return copy_to(s, h + 1, part_ref.at[s, h + 1, rows_of(h, u)], got.at[s, h, rows_of(h, u)],
                       direct_send.at[s, h, u], direct_recv.at[s, h, u])

    def to_end_summed(s, h, u):
        other = 1 - h
        return copy_to(s, other + 1, onward.at[s, h, u], got.at[s, other, rows_of(h, u)],
                       onward_send.at[s, h, u], onward_recv.at[s, h, u])

    steps = [(u, h, s) for u in range(SUBS) for h in range(HALVES) for s in range(S)]
    for u, h, s in steps:
        to_relay(s, h, u).start()
    for u, h, s in steps:
        to_end(s, h, u).start()
    for u, h, s in steps:
        to_relay(s, h, u).wait_recv()
        added = relay[s, h, u].astype(F32) + part_ref[s, 2 - h, rows_of(h, u)].astype(F32)
        onward[s, h, u] = added.astype(BF16)
        to_end_summed(s, h, u).start()

    def pooled(block):
        high = block.astype(BF16)
        low = (block - high.astype(F32)).astype(BF16)
        matrix = pool[...]
        return (jnp.dot(high, matrix, preferred_element_type=F32)
                + jnp.dot(low, matrix, preferred_element_type=F32))

    for u, h, s in steps:
        to_end(s, h, u).wait_recv()
        to_end_summed(s, h, u).wait_recv()
        q = h * SUBS + u
        rows = rows_of(h, u)
        for j in range(TC):
            cols = pl.ds(j * TILE, TILE)
            block = part_ref[s, 0, rows, cols].astype(F32)
            for i in range(2):
                block = block + got[s, i, rows, cols].astype(F32)
            zero_ref[s, rows, cols] = block.astype(BF16)
            half[j] = pooled(block)
        ones = []
        for j in range(TC):
            piece = half[j, pl.ds(0, CHUNK // 2, stride=2), :] + half[j, pl.ds(1, CHUNK // 2, stride=2), :]
            one_ref[s, pl.ds(q * (CHUNK // 2), CHUNK // 2), pl.ds(j * VC, VC)] = piece.astype(BF16)
            ones.append(piece)
        for j in range(2):
            quarter[j] = pooled(jnp.concatenate(ones[2 * j:2 * j + 2], axis=1))
            piece = quarter[j, pl.ds(0, CHUNK // 4, stride=2), :] + quarter[j, pl.ds(1, CHUNK // 4, stride=2), :]
            two_ref[s, pl.ds(q * (CHUNK // 4), CHUNK // 4), pl.ds(j * VC, VC)] = piece.astype(BF16)

    for u, h, s in steps:
        to_relay(s, h, u).wait_send()
        to_end(s, h, u).wait_send()
        to_end_summed(s, h, u).wait_send()


def scatter(part):
    vmem = pl.BlockSpec(memory_space=pltpu.VMEM)
    dma = pltpu.SemaphoreType.DMA
    parts = (S, HALVES, SUBS)
    return pl.pallas_call(
        scatter_kernel,
        out_shape=(
            jax.ShapeDtypeStruct((S, TILE, WIDE), BF16),
            jax.ShapeDtypeStruct((S, TILE // 2, WIDE // 2), BF16),
            jax.ShapeDtypeStruct((S, TILE // 4, WIDE // 4), BF16),
        ),
        in_specs=[vmem],
        out_specs=(vmem, vmem, vmem),
        scratch_shapes=[
            pltpu.VMEM(parts + (CHUNK, WIDE), BF16),
            pltpu.VMEM(parts + (CHUNK, WIDE), BF16),
            pltpu.VMEM((S, 2, TILE, WIDE), BF16),
            pltpu.VMEM((TILE, VC), BF16),
            pltpu.VMEM((TC, CHUNK, VC), F32),
            pltpu.VMEM((2, CHUNK // 2, VC), F32),
            dma(parts), dma(parts), dma(parts), dma(parts), dma(parts), dma(parts),
        ],
        compiler_params=pltpu.CompilerParams(
            collective_id=1, has_side_effects=True, vmem_limit_bytes=32 * 1024 * 1024),
        name="scatter_and_pool",
    )(part)


def store_kernel(*refs):
    count = (len(refs) - 1) // 2
    sems = refs[-1]
    copies = [pltpu.make_async_copy(refs[n], refs[count + n], sems.at[n]) for n in range(count)]
    for copy in copies:
        copy.start()
    for copy in copies:
        copy.wait()


def store(*arrays):
    count = len(arrays)
    return pl.pallas_call(
        store_kernel,
        out_shape=tuple(jax.ShapeDtypeStruct(a.shape, a.dtype) for a in arrays),
        in_specs=[pl.BlockSpec(memory_space=pltpu.VMEM)] * count,
        out_specs=(pl.BlockSpec(memory_space=pltpu.HBM),) * count,
        scratch_shapes=[pltpu.SemaphoreType.DMA((count,))],
        compiler_params=pltpu.CompilerParams(vmem_limit_bytes=32 * 1024 * 1024),
        name="store_results",
    )(*arrays)


def shards(load_force, stiffness, cracks, anchor, images, owners, source_tile, offsets, blend_weight, counts):
    flat = [a.reshape(1, -1) for a in (owners, source_tile)]
    displacement, residual, metas, tiles = relax(
        load_force, stiffness, cracks, anchor, *flat, offsets, blend_weight.reshape(1, -1), counts.reshape(1, -1), images)
    part = warp(metas, tiles)
    level_zero, level_one, level_two = scatter(part)
    return store(displacement, residual, level_zero, level_one, level_two)


def solution(mesh):
    flat = P(("row", "col"))
    in_specs = (
        P(None, None, "row", "col"),
        P(None, None, "row", "col"),
        P(None, None, "row", "col"),
        P(None, "row", "col"),
        P(None, "row", "col"),
        P(("row", "col"), None),
        flat,
        P(None, ("row", "col")),
        flat,
        flat,
    )
    out_specs = (
        P(None, None, "row", "col"),
        P(None, None, "row", "col"),
        P(None, "row", "col"),
        P(None, "row", "col"),
        P(None, "row", "col"),
    )
    return jax.shard_map(shards, mesh=mesh, in_specs=in_specs, out_specs=out_specs, check_vma=False)
```

time: 131 us -> 82 us (0.63)
  the two profiles are of different devices: /device:TPU:1 before, /device:TPU:4 now
where the time goes in v2:
time: 82 us; the launch traced here: 81.6 us
  Pallas kernels  73.2 us (89%)
  local copies, waits for them, and re-layouts  7.79 us (10%)
    pallas_call x1, Pallas kernels, relax(): pl.pallas_call(relax_kernel, out_shape=(jax.ShapeDtypeStruct(block, F32),...  36.5 us
    pallas_call x1, Pallas kernels, scatter(): pl.pallas_call(scatter_kernel, out_shape=(jax.ShapeDtypeStruct((S, TILE,...  20.9 us
    pallas_call x1, Pallas kernels, warp(): pl.pallas_call(warp_kernel, out_shape=jax.ShapeDtypeStruct((S, 4, TILE, W...  14.6 us
    unnamed x20, local copies, waits for them, and re-layouts  7.79 us

profile of v2, /device:TPU:4, one launch (start us, length us, event | category | flops | bytes accessed | tf_op | source)
XLA Modules:
  0.0 81.6 jit_solution(2986383727238140317)
XLA Ops:
  0.6 0.0 copy-start
  0.6 1.2 %copy-done = bf16[2,256,1024]{2,1,0:T(8,128)(2,1)S(1)} copy-done((bf16[2,256,1024]{2,1,0:T(8,128)(2,1)S(1)}, bf16[2,256,1024]{2,1,0:T(8,128)(2,1)}, u32[]{:S(2)}) %copy-start) | copy-done | bytes 1048600
  1.9 0.0 copy-start.1
  1.9 0.8 %copy-done.1 = f32[2,2,32,128]{3,2,1,0:T(8,128)S(1)} copy-done((f32[2,2,32,128]{3,2,1,0:T(8,128)S(1)}, f32[2,2,32,128]{3,2,1,0:T(8,128)}, u32[]{:S(2)}) %copy-start.1) | copy-done | bytes 65560
  2.7 0.0 copy-start.2
  2.7 0.8 %copy-done.2 = f32[2,2,32,128]{3,2,1,0:T(8,128)S(1)} copy-done((f32[2,2,32,128]{3,2,1,0:T(8,128)S(1)}, f32[2,2,32,128]{3,2,1,0:T(8,128)}, u32[]{:S(2)}) %copy-start.2) | copy-done | bytes 65560
  3.5 0.0 copy-start.3
  3.5 0.8 %copy-done.3 = s32[2,2,32,128]{3,2,1,0:T(8,128)S(1)} copy-done((s32[2,2,32,128]{3,2,1,0:T(8,128)S(1)}, s32[2,2,32,128]{3,2,1,0:T(8,128)}, u32[]{:S(2)}) %copy-start.3) | copy-done | bytes 65560
  4.4 0.0 copy-start.4
  4.4 0.8 copy-done.4
  5.1 0.0 copy-start.5
  5.1 0.7 copy-done.5
  5.8 0.0 copy-start.6
  5.8 0.7 copy-done.6
  6.5 0.0 copy-start.7
  6.5 0.7 copy-done.7
  7.1 0.0 copy-start.8
  7.1 0.7 copy-done.8
  7.8 0.0 copy-start.9
  7.8 0.7 copy-done.9
  8.4 36.5 %relax_and_gather.1 = (f32[2,2,32,128]{3,2,1,0:T(8,128)S(1)}, f32[2,2,32,128]{3,2,1,0:T(8,128)S(1)}, f32[2,4,8,128]{3,2,1,0:T(8,128)S(1)}, bf16[2,4,256,1024]{3,2,1,0:T(8,128)(2,1)S(1)}) custom-call(f32[2,2,32,128]{3,2,1,0:T(8,128)S(1)} %copy-done.1, f32[2,2,32,128]{3,2,1,0:T(8,128)S(1)} %copy-done.2, s32[2,2,32,128]{3,2,1,0:T(8,128)S(1)} %copy-done.3, ...), custom_call_target="tpu_custom_call" | custom-call | tf_op jit(solution)/shard_map/relax_and_gather/pallas_call | solution.py:350
  44.9 14.6 %warp_partials.1.part_ref = bf16[2,4,256,1024]{3,2,1,0:T(8,128)(2,1)S(1)} custom-call(f32[2,4,8,128]{3,2,1,0:T(8,128)S(1)} %get-tuple-element.14.meta_ref, bf16[2,4,256,1024]{3,2,1,0:T(8,128)(2,1)S(1)} %get-tuple-element.15.tiles_ref), custom_call_target="tpu_custom_call" | custom-call | tf_op jit(solution)/shard_map/warp_partials/pallas_call | solution.py:452
  59.6 20.9 %scatter_and_pool.1 = (bf16[2,256,1024]{2,1,0:T(8,128)(2,1)S(1)}, bf16[2,128,512]{2,1,0:T(8,128)(2,1)S(1)}, bf16[2,64,256]{2,1,0:T(8,128)(2,1)S(1)}) custom-call(bf16[2,4,256,1024]{3,2,1,0:T(8,128)(2,1)S(1)} %warp_partials.1.part_ref), custom_call_target="tpu_custom_call" | custom-call | tf_op jit(solution)/shard_map/scatter_and_pool/pallas_call | solution.py:562
  80.5 1.2 %store_results.1 = (f32[2,2,32,128]{3,2,1,0:T(8,128)}, f32[2,2,32,128]{3,2,1,0:T(8,128)}, bf16[2,256,1024]{2,1,0:T(8,128)(2,1)}, bf16[2,128,512]{2,1,0:T(8,128)(2,1)}, bf16[2,64,256]{2,1,0:T(8,128)(2,1)}) custom-call(f32[2,2,32,128]{3,2,1,0:T(8,128)S(1)} %get-tuple-element.12.refs_0_, f32[2,2,32,128]{3,2,1,0:T(8,128)S(1)} %get-tuple-element.13.refs_1_, ...), custom_call_target="tpu_custom_call" | custom-call | tf_op jit(solution)/shard_map/store_results/pallas_call | solution.py:598
Async XLA Ops:
  0.6 1.2 %copy-start = (bf16[2,256,1024]{2,1,0:T(8,128)(2,1)S(1)}, bf16[2,256,1024]{2,1,0:T(8,128)(2,1)}, u32[]{:S(2)}) copy-start(bf16[2,256,1024]{2,1,0:T(8,128)(2,1)} %images_hbm.1) | copy-start | bytes 3145732
  1.9 0.8 %copy-start.1 = (f32[2,2,32,128]{3,2,1,0:T(8,128)S(1)}, f32[2,2,32,128]{3,2,1,0:T(8,128)}, u32[]{:S(2)}) copy-start(f32[2,2,32,128]{3,2,1,0:T(8,128)} %load_hbm.1) | copy-start | bytes 196612
  2.7 0.8 %copy-start.2 = (f32[2,2,32,128]{3,2,1,0:T(8,128)S(1)}, f32[2,2,32,128]{3,2,1,0:T(8,128)}, u32[]{:S(2)}) copy-start(f32[2,2,32,128]{3,2,1,0:T(8,128)} %stiff_hbm.1) | copy-start | bytes 196612
  3.5 0.8 %copy-start.3 = (s32[2,2,32,128]{3,2,1,0:T(8,128)S(1)}, s32[2,2,32,128]{3,2,1,0:T(8,128)}, u32[]{:S(2)}) copy-start(s32[2,2,32,128]{3,2,1,0:T(8,128)} %crack_hbm.1) | copy-start | bytes 196612
  4.4 0.8 copy-start.4
  5.1 0.7 copy-start.5
  5.8 0.7 copy-start.6
  6.5 0.7 copy-start.7
  7.1 0.7 copy-start.8
  7.8 0.7 copy-start.9

commit v3 on v2

--- a/solution.py
+++ b/solution.py
@@ -40,15 +40,82 @@
 SCATTER_MASK = (3, 1)
 
 
-NOTE = 32
+NOTE = 24
+MOMENTS = 2 * ITERS
+SCALE = 8.0
+
+
+def two_sum(a, b):
+    total = a + b
+    part = total - a
+    return total, (a - (total - part)) + (b - part)
+
+
+def renormed(high, low):
+    total = high + low
+    return total, low - (total - high)
+
+
+def split(a):
+    wide = a * 4097.0
+    high = wide - (wide - a)
+    return high, a - high
+
+
+def two_product(a, b, a_parts, b_parts):
+    (ah, al), (bh, bl) = a_parts, b_parts
+    product = a * b
+    return product, ((ah * bh - product) + ah * bl + al * bh) + al * bl
+
+
+def added(x, y):
+    total, rest = two_sum(x[0], y[0])
+    return renormed(total, rest + (x[1] + y[1]))
+
+
+def times(x, y):
+    product, rest = two_product(x[0], y[0], split(x[0]), split(y[0]))
+    return renormed(product, rest + (x[0] * y[1] + x[1] * y[0]))
+
+
+def minus(x):
+    return -x[0], -x[1]
+
+
+def over(x, y):
+    first = x[0] / y[0]
+    nothing = jnp.zeros_like(first)
+    rest = added(x, minus(times((first, nothing), y)))
+    return renormed(first, rest[0] / y[0])
+
+
+def residual_polynomial(moment):
+    one = (jnp.ones_like(moment[0][0]), jnp.zeros_like(moment[0][0]))
+    rho, pi = [one], [one]
+    upper = moment[0]
+    for k in range(ITERS):
+        lower = None
+        for j, weight in enumerate(pi):
+            term = moment[j + k + 1] if k == 0 else times(weight, moment[j + k + 1])
+            lower = term if lower is None else added(lower, term)
+        step = over(upper, lower)
+        moved = [minus(times(step, weight)) if k else minus(step) for weight in pi]
+        rho = [rho[0]] + [added(rho[j], moved[j - 1]) for j in range(1, k + 1)] + [moved[k]]
+        if k == ITERS - 1:
+            return rho
+        upper = moment[k + 1]
+        for j in range(1, k + 2):
+            upper = added(upper, times(rho[j], moment[j + k + 1]))
+        grow = minus(over(upper, lower))
+        pi = [added(rho[j], times(grow, pi[j]) if k else grow) for j in range(k + 1)] + [rho[k + 1]]
 
 
 def relax_kernel(
     load_hbm, stiff_hbm, crack_hbm, anchor_hbm, owner_hbm, source_hbm, offset_hbm, blend_hbm, count_hbm, images_hbm,
-    disp_ref, resid_ref, metas_ref, tiles_ref,
+    disp_ref, resid_ref, metas_ref, codes_ref, tiles_ref, blank_ref,
     fields, stiff, crack, owner, source, offset, blend, count,
-    strips, halo_v, halo_h, halo_c, coef, rs, ws, us, qs, ts, ps, xs,
-    part_a, part_b, got_a, got_b, note, notes,
+    strips, halo_v, halo_h, halo_c, coef, krylov,
+    part_a, part_b, got_a, got_b, note, notes, sums,
     load_sem, own_sem, halo_send, halo_recv, send_a, recv_a, send_b, recv_b,
     note_send, note_recv, tile_send, tile_recv,
 ):
@@ -149,6 +216,8 @@
     note[2:4, 0:ENT_DEV] = offset[...].astype(F32)
     note[4:5, 0:ENT_DEV] = jnp.where(lax.rem(entry_lane, K) < listed, blend[...], 0.0)
 
+    blank_ref[...] = jnp.zeros(blank_ref.shape, BF16)
+
     for copy in halo:
         copy.wait_recv()
 
@@ -180,95 +249,23 @@
         coef[s, 3] = to_low
         coef[s, 4] = to_high
         for k in range(2):
-            rs[2 * s + k] = widened(2 * s + k)
-
-    def operate(near, far):
+            krylov[0, 2 * s + k] = widened(2 * s + k)
+
+    for n in range(ITERS):
         for f in range(4):
             s = f // 2
-            v = near[f]
+            v = krylov[n, f]
             w = coef[s, 0] * v
             w = w - coef[s, 1] * pltpu.roll(v, COLS - 1, 1)
             w = w - coef[s, 2] * pltpu.roll(v, 1, 1)
             w = w - coef[s, 3] * pltpu.roll(v, ROWS - 1, 0)
             w = w - coef[s, 4] * pltpu.roll(v, 1, 0)
-            far[f] = w
-
-    def core(ref, f):
-        return ref[f, pl.ds(8, VR), pl.ds(0, VC)]
-
-    def reduced(n, pairs):
-        rows = []
-        for one, other in pairs:
-            for s in range(S):
-                total = jnp.zeros((8, VC), F32)
-                for k in range(2):
-                    f = 2 * s + k
-                    total = total + jnp.sum((core(one, f) * core(other, f)).reshape(VR // 8, 8, VC), axis=0)
-                rows.append(jnp.sum(total, axis=0, keepdims=True))
-        height = -(-len(rows) // 8) * 8
-        if height > len(rows):
-            rows.append(jnp.zeros((height - len(rows), VC), F32))
-        span = pl.ds(0, height)
-        part_a[n, span] = jnp.concatenate(rows, axis=0)
-
-        @pl.loop(1, N_ROW)
-        def _(d):
-            pltpu.make_async_remote_copy(
-                src_ref=part_a.at[n, span], dst_ref=got_a.at[n, d - 1, span], send_sem=send_a.at[n],
-                recv_sem=recv_a.at[n], device_id=(lax.rem(r + d, N_ROW), c), device_id_type=MESH).start()
-
-        sum_copy(n, height, 0).wait_recv()
-        part_b[n, span] = part_a[n, span] + jnp.sum(got_a[n, :, span], axis=0)
-
-        @pl.loop(1, N_COL)
-        def _(d):
-            pltpu.make_async_remote_copy(
-                src_ref=part_b.at[n, span], dst_ref=got_b.at[n, d - 1, span], send_sem=send_b.at[n],
-                recv_sem=recv_b.at[n], device_id=(r, lax.rem(c + d, N_COL)), device_id_type=MESH).start()
-
-        sum_copy(n, height, 1).wait_recv()
-        total = part_b[n, span] + jnp.sum(got_b[n, :, span], axis=0)
-        total = jnp.sum(total, axis=1, keepdims=True)
-        return [total[2 * m:2 * m + 2] for m in range(len(pairs))]
-
-    def sum_copy(n, height, phase):
-        got, send, recv = ((got_a, send_a, recv_a), (got_b, send_b, recv_b))[phase]
-        return pltpu.make_async_remote_copy(
-            src_ref=got.at[n, :, pl.ds(0, height)], dst_ref=got.at[n, :, pl.ds(0, height)],
-            send_sem=send.at[n], recv_sem=recv.at[n],
-            device_id=((down, c), (r, right))[phase], device_id_type=MESH)
-
-    operate(rs, ws)
-    operate(ws, us)
-    m0, m1, m2, m3 = reduced(0, ((rs, rs), (rs, ws), (ws, ws), (ws, us)))
-    a0 = m0 / m1
-    n1 = a0 * a0 * m2 - m0
-    b0 = n1 / m0
-    g0 = 1.0 + b0
-    a1 = n1 / (g0 * g0 * m1 - 2.0 * g0 * a0 * m2 + a0 * a0 * m3)
-    for f in range(4):
-        s = f // 2
-        step0, step1, grow = a0[s:s + 1], a1[s:s + 1], g0[s:s + 1]
-        v, w = rs[f], ws[f]
-        p = grow * v - step0 * w
-        q = grow * w - step0 * us[f]
-        ps[f] = p
-        qs[f] = q
-        xs[f] = step0 * v + step1 * p
-        rs[f] = v - step0 * w - step1 * q
-
-    for s in range(S):
-        direct[s][0].wait_recv()
-        relayed[s][0].start()
-        direct[s][1].wait_recv()
-        relayed[s][1].start()
-
-    operate(rs, ws)
+            krylov[n + 1, f] = w * (1.0 / SCALE)
+
     middle = 8 + VR // 2
-    basis = (xs, ps, rs, ws, qs)
-    for b, ref in enumerate(basis):
+    for n in range(ITERS):
         for f in range(4):
-            note[8 + 4 * b + f:9 + 4 * b + f, :] = ref[f, pl.ds(middle, 1), pl.ds(0, VC)]
+            note[8 + 4 * n + f:9 + 4 * n + f, :] = krylov[n, f, pl.ds(middle, 1), pl.ds(0, VC)]
     told = []
     for s in range(S):
         for i in (1, 2, 3):
@@ -276,33 +273,106 @@
                 src_ref=note, dst_ref=notes.at[s, i - 1],
                 send_sem=note_send.at[s, i - 1], recv_sem=note_recv.at[s, i - 1],
                 device_id=(r, peer_col(y, z, SCATTER_MASK[s], i)), device_id_type=MESH))
+
+    moments = [[None] * S for _ in range(MOMENTS)]
+    for s in range(S):
+        totals = [None] * MOMENTS
+        for f in (2 * s, 2 * s + 1):
+            for g in range(VR // 8):
+                vectors = [krylov[n, f, pl.ds(8 + 8 * g, 8), pl.ds(0, VC)] for n in range(ITERS + 1)]
+                parts = [split(v) for v in vectors]
+                for m in range(MOMENTS):
+                    a, b = m // 2, m - m // 2
+                    product, rest = two_product(vectors[a], vectors[b], parts[a], parts[b])
+                    if totals[m] is None:
+                        totals[m] = (product, rest)
+                    else:
+                        total, slip = two_sum(totals[m][0], product)
+                        totals[m] = (total, totals[m][1] + (rest + slip))
+        for m in range(MOMENTS):
+            moments[m][s] = totals[m]
+
+    level = [moments[m][s] for m in range(MOMENTS) for s in range(S)]
+    sublane = lax.broadcasted_iota(jnp.int32, (8, VC), 0)
+    packed = []
+    for base in range(0, len(level), 8):
+        group = level[base:base + 8]
+        shift = 4
+        while shift:
+            low = lax.rem(sublane // shift, 2) == 0
+            merged = []
+            for n in range(shift):
+                a, b = group[n], group[n + shift]
+                first = tuple(jnp.where(low, u, pltpu.roll(v, shift, 0)) for u, v in zip(a, b))
+                second = tuple(jnp.where(low, pltpu.roll(u, 8 - shift, 0), v) for u, v in zip(a, b))
+                merged.append(added(first, second))
+            group = merged
+            shift //= 2
+        packed.append(group[0])
+    height = 4 * 8
+    part_a[...] = jnp.concatenate([packed[0][0], packed[1][0], packed[0][1], packed[1][1]], axis=0)
+
+    @pl.loop(1, N_ROW)
+    def _(d):
+        pltpu.make_async_remote_copy(
+            src_ref=part_a, dst_ref=got_a.at[d - 1], send_sem=send_a,
+            recv_sem=recv_a, device_id=(lax.rem(r + d, N_ROW), c), device_id_type=MESH).start()
+
     for copy in told:
         copy.start()
-    operate(ws, us)
-    operate(qs, ts)
-    rr, rw, rq, ww, wq, qq, wu, uq, qt = reduced(1, (
-        (rs, rs), (rs, ws), (rs, qs), (ws, ws), (ws, qs), (qs, qs), (ws, us), (us, qs), (qs, ts)))
-    b1 = rr / n1
-    a2 = rr / (rw - b1 * rr / a1)
-    q2q2 = ww + 2.0 * b1 * wq + b1 * b1 * qq
-    n3 = rr - 2.0 * a2 * (rw + b1 * rq) + a2 * a2 * q2q2
-    b2 = n3 / rr
-    r3ar3 = rw - 2.0 * a2 * (ww + b1 * wq) + a2 * a2 * (wu + 2.0 * b1 * uq + b1 * b1 * qt)
-    a3 = n3 / (r3ar3 - b2 * n3 / a2)
-
-    weights = (None, (a2 + a3 * b2) * b1, a2 + a3 * b2 + a3, -a3 * a2, -a3 * a2 * b1)
+
+    def sum_copy(phase):
+        got, send, recv = ((got_a, send_a, recv_a), (got_b, send_b, recv_b))[phase]
+        return pltpu.make_async_remote_copy(
+            src_ref=got, dst_ref=got, send_sem=send, recv_sem=recv,
+            device_id=((down, c), (r, right))[phase], device_id_type=MESH)
+
+    def gathered(own_part, got):
+        terms = [(own_part[0:16], own_part[16:32])]
+        terms += [(got[n, 0:16], got[n, 16:32]) for n in range(got.shape[0])]
+        while len(terms) > 1:
+            terms = [added(terms[n], terms[n + 1]) if n + 1 < len(terms) else terms[n]
+                     for n in range(0, len(terms), 2)]
+        return terms[0]
+
+    sum_copy(0).wait_recv()
+    part_b[...] = jnp.concatenate(gathered(part_a, got_a), axis=0)
+
+    @pl.loop(1, N_COL)
+    def _(d):
+        pltpu.make_async_remote_copy(
+            src_ref=part_b, dst_ref=got_b.at[d - 1], send_sem=send_b,
+            recv_sem=recv_b, device_id=(r, lax.rem(c + d, N_COL)), device_id_type=MESH).start()
+
+    for s in range(S):
+        direct[s][0].wait_recv()
+        relayed[s][0].start()
+        direct[s][1].wait_recv()
+        relayed[s][1].start()
+
+    sum_copy(1).wait_recv()
+    total = gathered(part_b, got_b)
+    shift = VC // 2
+    while shift:
+        total = added(total, tuple(pltpu.roll(part, shift, 1) for part in total))
+        shift //= 2
+    sums[0:16] = total[0]
+    sums[16:32] = total[1]
+    rho = residual_polynomial([
+        (sums[2 * m:2 * m + 2, :], sums[16 + 2 * m:18 + 2 * m, :]) for m in range(MOMENTS)])
+    rho = [weight[0] for weight in rho]
+
     for f in range(4):
         s, k = f // 2, f % 2
-        step2, step3 = a2[s:s + 1], a3[s:s + 1]
-        grow1, grow2 = b1[s:s + 1], b2[s:s + 1]
-        v, w, q = core(rs, f), core(ws, f), core(qs, f)
-        p2 = v + grow1 * core(ps, f)
-        q2 = w + grow1 * q
-        r3 = v - step2 * q2
-        p3 = r3 + grow2 * p2
-        q3 = w - step2 * (core(us, f) + grow1 * core(ts, f)) + grow2 * q2
-        disp_ref[s, k] = core(xs, f) + step2 * p2 + step3 * p3
-        resid_ref[s, k] = r3 - step3 * q3
+        vectors = [krylov[n, f, pl.ds(8, VR), pl.ds(0, VC)] for n in range(ITERS + 1)]
+        moved = rho[1][s:s + 1] * vectors[0]
+        rest = vectors[0]
+        for n in range(1, ITERS + 1):
+            rest = rest + rho[n][s:s + 1] * vectors[n]
+            if n < ITERS:
+                moved = moved + rho[n + 1][s:s + 1] * vectors[n]
+        disp_ref[s, k] = moved * (-1.0 / SCALE)
+        resid_ref[s, k] = rest
 
     for copy in told:
         copy.wait_recv()
@@ -315,22 +385,23 @@
             weight = text[4:5, :]
             mine = (at_y == y) | (at_y == flipped(y, GATHER_MASK[s]))
             mine = mine & ((at_z == z) | (at_z == flipped(z, GATHER_MASK[s])))
-            mine = mine & (weight > 0.0) & (note_lane < ENT_DEV)
+            mine = mine & (weight > 0.0)
             slot = jnp.where(at_y == y, 0, 1) + jnp.where(at_z == z, 0, 2)
-            key = jnp.where(mine, slot * TC + text[1:2, :].astype(jnp.int32), -1)
-            shift = text[8 + 2 * s:10 + 2 * s, :]
-            for b in range(1, 5):
-                shift = shift + weights[b][s:s + 1] * text[8 + 4 * b + 2 * s:10 + 4 * b + 2 * s, :]
+            key = slot * TC + text[1:2, :].astype(jnp.int32)
+            code = ((s * 4 + i) * 32 + note_lane - s * TC * K) * 16 + key
+            codes_ref[s * 4 + i:s * 4 + i + 1, :] = jnp.where(mine, code, -1)
+            shift = rho[1][s:s + 1] * text[8 + 2 * s:10 + 2 * s, :]
+            for n in range(1, ITERS):
+                shift = shift + rho[n + 1][s:s + 1] * text[8 + 4 * n + 2 * s:10 + 4 * n + 2 * s, :]
             metas_ref[s, i] = jnp.concatenate(
-                [key.astype(F32), text[2:4, :], weight, shift, jnp.zeros((2, VC), F32)], axis=0)
+                [text[2:4, :], weight, shift * (-SPACING / SCALE), jnp.zeros((3, VC), F32)], axis=0)
 
     for copy in told:
         copy.wait_send()
     for copy in halo:
         copy.wait_send()
-    for n, height in enumerate((8, 24)):
-        for phase in range(2):
-            sum_copy(n, height, phase).wait_send()
+    for phase in range(2):
+        sum_copy(phase).wait_send()
     own.wait()
     for s in range(S):
         direct[s][2].wait_recv()
@@ -345,18 +416,20 @@
     vmem = pl.BlockSpec(memory_space=pltpu.VMEM)
     hbm = pl.BlockSpec(memory_space=pltpu.HBM)
     dma = pltpu.SemaphoreType.DMA
-    wide = pltpu.VMEM((4, ROWS, COLS), F32)
     block = (S, 2, VR, VC)
+    operands = [pltpu.with_memory_space_constraint(a, pltpu.HBM) for a in operands]
     return pl.pallas_call(
         relax_kernel,
         out_shape=(
             jax.ShapeDtypeStruct(block, F32),
             jax.ShapeDtypeStruct(block, F32),
             jax.ShapeDtypeStruct((S, 4, 8, VC), F32),
+            jax.ShapeDtypeStruct((S * 4, VC), jnp.int32),
+            jax.ShapeDtypeStruct((S, 4, TILE, WIDE), BF16),
             jax.ShapeDtypeStruct((S, 4, TILE, WIDE), BF16),
         ),
         in_specs=[hbm] * 10,
-        out_specs=(vmem, vmem, vmem, vmem),
+        out_specs=(vmem,) * 6,
         scratch_shapes=[
             pltpu.VMEM((10, VR, VC), F32),
             pltpu.VMEM(block, F32),
@@ -371,15 +444,16 @@
             pltpu.VMEM((2, VR, VC), F32),
             pltpu.VMEM((4, 8, VC), F32),
             pltpu.VMEM((S, 5, ROWS, COLS), F32),
-            wide, wide, wide, wide, wide, wide, wide,
-            pltpu.VMEM((2, 24, VC), F32),
-            pltpu.VMEM((2, 24, VC), F32),
-            pltpu.VMEM((2, N_ROW - 1, 24, VC), F32),
-            pltpu.VMEM((2, N_COL - 1, 24, VC), F32),
+            pltpu.VMEM((ITERS + 1, 4, ROWS, COLS), F32),
+            pltpu.VMEM((32, VC), F32),
+            pltpu.VMEM((32, VC), F32),
+            pltpu.VMEM((N_ROW - 1, 32, VC), F32),
+            pltpu.VMEM((N_COL - 1, 32, VC), F32),
             pltpu.VMEM((NOTE, VC), F32),
             pltpu.VMEM((S, 3, NOTE, VC), F32),
+            pltpu.VMEM((32, VC), F32),
             dma((10,)), dma, dma((8,)), dma((8,)),
-            dma((2,)), dma((2,)), dma((2,)), dma((2,)),
+            dma, dma, dma, dma,
             dma((S, 3)), dma((S, 3)), dma((S, 6)), dma((S, 6)),
         ],
         compiler_params=pltpu.CompilerParams(
@@ -388,29 +462,24 @@
     )(*operands)
 
 
-BATCH = 2
-
-
-def warp_kernel(meta_ref, tiles_ref, part_ref, apart, where_list, weight_list):
-    def listing(s, n, count):
-        i = n // (TC * K)
-        e = lax.rem(n, TC * K)
-        key = meta_ref[s, i, 0, s * TC * K + e].astype(jnp.int32)
-        where_list[count] = ((s * 4 + i) * 32 + e) * 16 + jnp.maximum(key, 0)
-        weight_list[count] = meta_ref[s, i, 3, s * TC * K + e]
-        return count + jnp.where(key >= 0, 1, 0)
-
+BATCH = 4
+
+
+def warp_kernel(code_ref, meta_ref, tiles_ref, blank_ref, part_ref, apart, listed):
     count = 0
-    for s in range(S):
-        count = lax.fori_loop(0, 4 * TC * K, lambda n, total, s=s: listing(s, n, total), count)
+    for n in range(S * 4):
+        def listing(e, total, n=n):
+            code = code_ref[n, n // 4 * TC * K + e]
+            listed[total] = code
+            return total + jnp.where(code >= 0, 1, 0)
+
+        count = lax.fori_loop(0, TC * K, listing, count, unroll=8)
     for n in range(BATCH - 1):
-        where_list[count + n] = 0
-        weight_list[count + n] = 0.0
+        listed[count + n] = -1
 
     row = lax.broadcasted_iota(jnp.int32, (TILE, TILE), 0)
     lane = lax.broadcasted_iota(jnp.int32, (TILE, TILE), 1)
     apart[...] = (lane - row).astype(F32).astype(BF16)
-    part_ref[...] = jnp.zeros(part_ref.shape, BF16)
 
     def sampled(shift, side):
         shift = jnp.full((1, TILE), shift, F32)
@@ -423,7 +492,9 @@
         return jnp.where(matrix == low_place, at_low, jnp.where(matrix == high_place, at_high, jnp.zeros((), BF16)))
 
     def entry(n):
-        code = where_list[n]
+        code = listed[n]
+        weight_on = jnp.where(code >= 0, 1.0, 0.0)
+        code = jnp.maximum(code, 0)
         key = code & 15
         e = (code >> 4) & 31
         place = code >> 9
@@ -431,12 +502,13 @@
         i = place & 3
         j = (e * 43) >> 8
         at = s * TC * K + e
-        sy = meta_ref[s, i, 1, at] + SPACING * meta_ref[s, i, 4, 32 * j + 16]
-        sx = meta_ref[s, i, 2, at] + SPACING * meta_ref[s, i, 5, 32 * j + 16]
+        sy = meta_ref[s, i, 0, at] + meta_ref[s, i, 3, 32 * j + 16]
+        sx = meta_ref[s, i, 1, at] + meta_ref[s, i, 4, 32 * j + 16]
         source = tiles_ref[s, key >> 2, :, pl.ds(pl.multiple_of((key & 3) * TILE, TILE), TILE)]
         across = jnp.dot(source, sampled(sx, -1.0), preferred_element_type=F32)
         down = jnp.dot(sampled(sy, 1.0), across.astype(BF16), preferred_element_type=F32)
-        return weight_list[n] * down, (s, i, slice(None), pl.ds(pl.multiple_of(j * TILE, TILE), TILE))
+        weight = weight_on * meta_ref[s, i, 2, at]
+        return weight * down, (s, i, slice(None), pl.ds(pl.multiple_of(j * TILE, TILE), TILE))
 
     def batch(b, carry):
         found = [entry(b * BATCH + n) for n in range(BATCH)]
@@ -447,21 +519,19 @@
     lax.fori_loop(0, (count + BATCH - 1) // BATCH, batch, 0)
 
 
-def warp(metas, tiles):
+def warp(codes, metas, tiles, blank):
     vmem = pl.BlockSpec(memory_space=pltpu.VMEM)
+    smem = pl.BlockSpec(memory_space=pltpu.SMEM)
     return pl.pallas_call(
         warp_kernel,
         out_shape=jax.ShapeDtypeStruct((S, 4, TILE, WIDE), BF16),
-        in_specs=[pl.BlockSpec(memory_space=pltpu.SMEM), vmem],
+        in_specs=[smem, smem, vmem, vmem],
         out_specs=vmem,
-        scratch_shapes=[
-            pltpu.VMEM((TILE, TILE), BF16),
-            pltpu.SMEM((256,), jnp.int32),
-            pltpu.SMEM((256,), F32),
-        ],
+        scratch_shapes=[pltpu.VMEM((TILE, TILE), BF16), pltpu.SMEM((256,), jnp.int32)],
+        input_output_aliases={3: 0},
         compiler_params=pltpu.CompilerParams(vmem_limit_bytes=32 * 1024 * 1024),
         name="warp_partials",
-    )(metas, tiles)
+    )(codes, metas, tiles, blank)
 
 
 CHUNK = 64
@@ -608,9 +678,9 @@
 
 def shards(load_force, stiffness, cracks, anchor, images, owners, source_tile, offsets, blend_weight, counts):
     flat = [a.reshape(1, -1) for a in (owners, source_tile)]
-    displacement, residual, metas, tiles = relax(
+    displacement, residual, metas, codes, tiles, blank = relax(
         load_force, stiffness, cracks, anchor, *flat, offsets, blend_weight.reshape(1, -1), counts.reshape(1, -1), images)
-    part = warp(metas, tiles)
+    part = warp(codes, metas, tiles, blank)
     level_zero, level_one, level_two = scatter(part)
     return store(displacement, residual, level_zero, level_one, level_two)
 

time: 82 us -> 64.3 us (0.78)
  the two profiles are of different devices: /device:TPU:4 before, /device:TPU:1 now
where the time goes in v3:
time: 64.3 us; the launch traced here: 64.1 us
  Pallas kernels  63.5 us (99%)
  between operations  0.66 us (1%)
    pallas_call x1, Pallas kernels, relax(): pl.pallas_call(relax_kernel, out_shape=(jax.ShapeDtypeStruct(block, F32),...  30.6 us
    pallas_call x1, Pallas kernels, scatter(): pl.pallas_call(scatter_kernel, out_shape=(jax.ShapeDtypeStruct((S, TILE,...  26.1 us
    pallas_call x1, Pallas kernels, warp(): pl.pallas_call(warp_kernel, out_shape=jax.ShapeDtypeStruct((S, 4, TILE, W...  5.7 us

profile of v3, /device:TPU:1, one launch (start us, length us, event | category | flops | bytes accessed | tf_op | source)
XLA Modules:
  0.0 64.1 jit_solution(4777018598687791387)
XLA Ops:
  0.6 30.6 %relax_and_gather.1 = (f32[2,2,32,128]{3,2,1,0:T(8,128)S(1)}, f32[2,2,32,128]{3,2,1,0:T(8,128)S(1)}, f32[2,4,8,128]{3,2,1,0:T(8,128)S(1)}, s32[8,128]{1,0:T(8,12...) custom-call(f32[2,2,32,128]{3,2,1,0:T(8,128)} %load_hbm.1, ...), custom_call_target="tpu_custom_call" | custom-call | tf_op jit(solution)/shard_map/relax_and_gather/pallas_call | solution.py:421
  31.2 5.7 %warp_partials.1.part_ref = bf16[2,4,256,1024]{3,2,1,0:T(8,128)(2,1)S(1)} custom-call(s32[8,128]{1,0:T(8,128)S(1)} %get-tuple-element.16.code_ref, f32[2,4,8,128]{3,2,1,0:T(8,128)S(1)} %get-tuple-element.17.meta_ref, bf16[2,4,256,1024]{3,2,1,0:T(8,128)(2,1)S(1)} %get-tuple-element.18.tiles_ref, ...), custom_call_target="tpu_custom_call", output_to_operand_aliasing={{}: (3, {})} | custom-call | tf_op jit(solution)/shard_map/warp_partials/pallas_call | solution.py:525
  36.9 26.1 %scatter_and_pool.1 = (bf16[2,256,1024]{2,1,0:T(8,128)(2,1)S(1)}, bf16[2,128,512]{2,1,0:T(8,128)(2,1)S(1)}, bf16[2,64,256]{2,1,0:T(8,128)(2,1)S(1)}) custom-call(bf16[2,4,256,1024]{3,2,1,0:T(8,128)(2,1)S(1)} %warp_partials.1.part_ref), custom_call_target="tpu_custom_call" | custom-call | tf_op jit(solution)/shard_map/scatter_and_pool/pallas_call | solution.py:632
  63.0 1.2 %store_results.1 = (f32[2,2,32,128]{3,2,1,0:T(8,128)}, f32[2,2,32,128]{3,2,1,0:T(8,128)}, bf16[2,256,1024]{2,1,0:T(8,128)(2,1)}, bf16[2,128,512]{2,1,0:T(8,128)(2,1)}, bf16[2,64,256]{2,1,0:T(8,128)(2,1)}) custom-call(f32[2,2,32,128]{3,2,1,0:T(8,128)S(1)} %get-tuple-element.14.refs_0_, f32[2,2,32,128]{3,2,1,0:T(8,128)S(1)} %get-tuple-element.15.refs_1_, ...), custom_call_target="tpu_custom_call" | custom-call | tf_op jit(solution)/shard_map/store_results/pallas_call | solution.py:668

commit v4 on v3

--- a/solution.py
+++ b/solution.py
@@ -41,6 +41,7 @@
 
 
 NOTE = 24
+LIST = 256
 MOMENTS = 2 * ITERS
 SCALE = 8.0
 
@@ -112,7 +113,7 @@
 
 def relax_kernel(
     load_hbm, stiff_hbm, crack_hbm, anchor_hbm, owner_hbm, source_hbm, offset_hbm, blend_hbm, count_hbm, images_hbm,
-    disp_ref, resid_ref, metas_ref, codes_ref, tiles_ref, blank_ref,
+    disp_ref, resid_ref, list_ref, tiles_ref, blank_ref,
     fields, stiff, crack, owner, source, offset, blend, count,
     strips, halo_v, halo_h, halo_c, coef, krylov,
     part_a, part_b, got_a, got_b, note, notes, sums,
@@ -309,8 +310,10 @@
             group = merged
             shift //= 2
         packed.append(group[0])
-    height = 4 * 8
-    part_a[...] = jnp.concatenate([packed[0][0], packed[1][0], packed[0][1], packed[1][1]], axis=0)
+    packed = [added(pair, tuple(pltpu.roll(part, VC // 2, 1) for part in pair)) for pair in packed]
+    sum_lane = lax.broadcasted_iota(jnp.int32, (8, VC), 1)
+    part_a[...] = jnp.concatenate(
+        [jnp.where(sum_lane < VC // 2, one, two) for one, two in zip(*packed)], axis=0)
 
     @pl.loop(1, N_ROW)
     def _(d):
@@ -318,9 +321,6 @@
             src_ref=part_a, dst_ref=got_a.at[d - 1], send_sem=send_a,
             recv_sem=recv_a, device_id=(lax.rem(r + d, N_ROW), c), device_id_type=MESH).start()
 
-    for copy in told:
-        copy.start()
-
     def sum_copy(phase):
         got, send, recv = ((got_a, send_a, recv_a), (got_b, send_b, recv_b))[phase]
         return pltpu.make_async_remote_copy(
@@ -328,8 +328,8 @@
             device_id=((down, c), (r, right))[phase], device_id_type=MESH)
 
     def gathered(own_part, got):
-        terms = [(own_part[0:16], own_part[16:32])]
-        terms += [(got[n, 0:16], got[n, 16:32]) for n in range(got.shape[0])]
+        terms = [(own_part[0:8], own_part[8:16])]
+        terms += [(got[n, 0:8], got[n, 8:16]) for n in range(got.shape[0])]
         while len(terms) > 1:
             terms = [added(terms[n], terms[n + 1]) if n + 1 < len(terms) else terms[n]
                      for n in range(0, len(terms), 2)]
@@ -344,6 +344,9 @@
             src_ref=part_b, dst_ref=got_b.at[d - 1], send_sem=send_b,
             recv_sem=recv_b, device_id=(r, lax.rem(c + d, N_COL)), device_id_type=MESH).start()
 
+    for copy in told:
+        copy.start()
+
     for s in range(S):
         direct[s][0].wait_recv()
         relayed[s][0].start()
@@ -352,10 +355,16 @@
 
     sum_copy(1).wait_recv()
     total = gathered(part_b, got_b)
-    shift = VC // 2
+    shift = VC // 4
     while shift:
-        total = added(total, tuple(pltpu.roll(part, shift, 1) for part in total))
+        inner = lax.rem(sum_lane, VC // 2) < VC // 2 - shift
+        total = added(total, tuple(
+            jnp.where(inner, pltpu.roll(part, VC - shift, 1), pltpu.roll(part, VC // 2 - shift, 1)) for part in total))
         shift //= 2
+    upper_lanes = sum_lane < VC // 2
+    spread = [(jnp.where(upper_lanes, part, pltpu.roll(part, VC // 2, 1)),
+               jnp.where(upper_lanes, pltpu.roll(part, VC // 2, 1), part)) for part in total]
+    total = [jnp.concatenate(pair, axis=0) for pair in spread]
     sums[0:16] = total[0]
     sums[16:32] = total[1]
     rho = residual_polynomial([
@@ -376,25 +385,54 @@
 
     for copy in told:
         copy.wait_recv()
-    note_lane = lax.broadcasted_iota(jnp.int32, (1, VC), 1)
-    for s in range(S):
-        for i in range(4):
-            text = note if i == 0 else notes.at[s, i - 1]
-            at = text[0:1, :].astype(jnp.int32)
-            at_y, at_z = lax.rem(at, 4), at // 4
-            weight = text[4:5, :]
-            mine = (at_y == y) | (at_y == flipped(y, GATHER_MASK[s]))
-            mine = mine & ((at_z == z) | (at_z == flipped(z, GATHER_MASK[s])))
-            mine = mine & (weight > 0.0)
-            slot = jnp.where(at_y == y, 0, 1) + jnp.where(at_z == z, 0, 2)
-            key = slot * TC + text[1:2, :].astype(jnp.int32)
-            code = ((s * 4 + i) * 32 + note_lane - s * TC * K) * 16 + key
-            codes_ref[s * 4 + i:s * 4 + i + 1, :] = jnp.where(mine, code, -1)
-            shift = rho[1][s:s + 1] * text[8 + 2 * s:10 + 2 * s, :]
+    texts = [(s, note if i == 0 else notes.at[s, i - 1]) for s in range(S) for i in range(4)]
+    note_lane = lax.broadcasted_iota(jnp.int32, (8, VC), 1)
+    note_row = lax.broadcasted_iota(jnp.int32, (8, VC), 0)
+
+    def stacked(n):
+        rows = jnp.concatenate([text[n:n + 1, :] for _, text in texts], axis=0)
+        return jnp.where(note_row < 4, rows, pltpu.roll(rows, VC - TC * K, 1))
+
+    def shifted(k):
+        rows = []
+        for s, text in texts:
+            row = rho[1][s:s + 1] * text[8 + 2 * s + k:9 + 2 * s + k, :]
             for n in range(1, ITERS):
-                shift = shift + rho[n + 1][s:s + 1] * text[8 + 4 * n + 2 * s:10 + 4 * n + 2 * s, :]
-            metas_ref[s, i] = jnp.concatenate(
-                [text[2:4, :], weight, shift * (-SPACING / SCALE), jnp.zeros((3, VC), F32)], axis=0)
+                row = row + rho[n + 1][s:s + 1] * text[8 + 4 * n + 2 * s + k:9 + 4 * n + 2 * s + k, :]
+            rows.append(row)
+        rows = jnp.concatenate(rows, axis=0) * (-SPACING / SCALE)
+        shift = stacked(2 + k)
+        for j in range(TC):
+            shift = shift + jnp.where(note_lane // K == j, rows[:, 32 * j + 16:32 * j + 17], 0.0)
+        return shift
+
+    owner_col = stacked(0).astype(jnp.int32)
+    weight = stacked(4)
+    at_y, at_z = lax.rem(owner_col, 4), owner_col // 4
+    near = [((at_y == y) | (at_y == flipped(y, m))) & ((at_z == z) | (at_z == flipped(z, m))) for m in GATHER_MASK]
+    mine = jnp.where(note_row < 4, near[0].astype(F32), near[1].astype(F32))
+    mine = jnp.where((weight > 0.0) & (note_lane < TC * K), mine, 0.0)
+    slot = jnp.where(at_y == y, 0, 1) + jnp.where(at_z == z, 0, 2)
+    key = slot * TC + stacked(1).astype(jnp.int32)
+    code = ((note_row * TC + note_lane // K) * 16 + key).astype(F32)
+    rank = mine
+    for step in (1, 2, 4, 8, 16):
+        rank = rank + jnp.where(note_lane >= step, pltpu.roll(rank, step, 1), 0.0)
+    above = jnp.sum(mine, axis=1, keepdims=True) + jnp.zeros((8, VC), F32)
+    base = above
+    for step in (1, 2, 4):
+        base = base + jnp.where(note_row >= step, pltpu.roll(base, step, 0), 0.0)
+    total = base[7:8, :]
+    rank = jnp.where(mine > 0.0, rank + (base - above) - 1.0, -1.0)
+    columns = [jnp.transpose(part)[0:TC * K] for part in (rank, code, shifted(0), shifted(1), weight)]
+    place = lax.broadcasted_iota(jnp.int32, (TC * K, LIST), 1).astype(F32)
+    listed = [jnp.zeros((1, LIST), F32)] * 4
+    for n in range(8):
+        chosen = columns[0][:, n:n + 1] == place
+        listed = [old + jnp.sum(jnp.where(chosen, column[:, n:n + 1], 0.0), axis=0, keepdims=True)
+                  for old, column in zip(listed, columns[1:])]
+    list_ref[...] = jnp.concatenate(
+        listed + [jnp.concatenate([total] * (LIST // VC), axis=1), jnp.zeros((3, LIST), F32)], axis=0)
 
     for copy in told:
         copy.wait_send()
@@ -423,13 +461,12 @@
         out_shape=(
             jax.ShapeDtypeStruct(block, F32),
             jax.ShapeDtypeStruct(block, F32),
-            jax.ShapeDtypeStruct((S, 4, 8, VC), F32),
-            jax.ShapeDtypeStruct((S * 4, VC), jnp.int32),
+            jax.ShapeDtypeStruct((8, LIST), F32),
             jax.ShapeDtypeStruct((S, 4, TILE, WIDE), BF16),
             jax.ShapeDtypeStruct((S, 4, TILE, WIDE), BF16),
         ),
         in_specs=[hbm] * 10,
-        out_specs=(vmem,) * 6,
+        out_specs=(vmem,) * 5,
         scratch_shapes=[
             pltpu.VMEM((10, VR, VC), F32),
             pltpu.VMEM(block, F32),
@@ -445,10 +482,10 @@
             pltpu.VMEM((4, 8, VC), F32),
             pltpu.VMEM((S, 5, ROWS, COLS), F32),
             pltpu.VMEM((ITERS + 1, 4, ROWS, COLS), F32),
-            pltpu.VMEM((32, VC), F32),
-            pltpu.VMEM((32, VC), F32),
-            pltpu.VMEM((N_ROW - 1, 32, VC), F32),
-            pltpu.VMEM((N_COL - 1, 32, VC), F32),
+            pltpu.VMEM((16, VC), F32),
+            pltpu.VMEM((16, VC), F32),
+            pltpu.VMEM((N_ROW - 1, 16, VC), F32),
+            pltpu.VMEM((N_COL - 1, 16, VC), F32),
             pltpu.VMEM((NOTE, VC), F32),
             pltpu.VMEM((S, 3, NOTE, VC), F32),
             pltpu.VMEM((32, VC), F32),
@@ -462,21 +499,11 @@
     )(*operands)
 
 
-BATCH = 4
-
-
-def warp_kernel(code_ref, meta_ref, tiles_ref, blank_ref, part_ref, apart, listed):
-    count = 0
-    for n in range(S * 4):
-        def listing(e, total, n=n):
-            code = code_ref[n, n // 4 * TC * K + e]
-            listed[total] = code
-            return total + jnp.where(code >= 0, 1, 0)
-
-        count = lax.fori_loop(0, TC * K, listing, count, unroll=8)
-    for n in range(BATCH - 1):
-        listed[count + n] = -1
-
+BATCH = 6
+
+
+def warp_kernel(list_ref, tiles_ref, blank_ref, part_ref, apart):
+    count = list_ref[4, 0].astype(jnp.int32)
     row = lax.broadcasted_iota(jnp.int32, (TILE, TILE), 0)
     lane = lax.broadcasted_iota(jnp.int32, (TILE, TILE), 1)
     apart[...] = (lane - row).astype(F32).astype(BF16)
@@ -492,23 +519,15 @@
         return jnp.where(matrix == low_place, at_low, jnp.where(matrix == high_place, at_high, jnp.zeros((), BF16)))
 
     def entry(n):
-        code = listed[n]
-        weight_on = jnp.where(code >= 0, 1.0, 0.0)
-        code = jnp.maximum(code, 0)
+        code = list_ref[0, n].astype(jnp.int32)
         key = code & 15
-        e = (code >> 4) & 31
-        place = code >> 9
+        j = (code >> 4) & 3
+        place = code >> 6
         s = place >> 2
-        i = place & 3
-        j = (e * 43) >> 8
-        at = s * TC * K + e
-        sy = meta_ref[s, i, 0, at] + meta_ref[s, i, 3, 32 * j + 16]
-        sx = meta_ref[s, i, 1, at] + meta_ref[s, i, 4, 32 * j + 16]
         source = tiles_ref[s, key >> 2, :, pl.ds(pl.multiple_of((key & 3) * TILE, TILE), TILE)]
-        across = jnp.dot(source, sampled(sx, -1.0), preferred_element_type=F32)
-        down = jnp.dot(sampled(sy, 1.0), across.astype(BF16), preferred_element_type=F32)
-        weight = weight_on * meta_ref[s, i, 2, at]
-        return weight * down, (s, i, slice(None), pl.ds(pl.multiple_of(j * TILE, TILE), TILE))
+        across = jnp.dot(source, sampled(list_ref[2, n], -1.0), preferred_element_type=F32)
+        down = jnp.dot(sampled(list_ref[1, n], 1.0), across.astype(BF16), preferred_element_type=F32)
+        return list_ref[3, n] * down, (s, place & 3, slice(None), pl.ds(pl.multiple_of(j * TILE, TILE), TILE))
 
     def batch(b, carry):
         found = [entry(b * BATCH + n) for n in range(BATCH)]
@@ -519,19 +538,19 @@
     lax.fori_loop(0, (count + BATCH - 1) // BATCH, batch, 0)
 
 
-def warp(codes, metas, tiles, blank):
+def warp(entries, tiles, blank):
     vmem = pl.BlockSpec(memory_space=pltpu.VMEM)
     smem = pl.BlockSpec(memory_space=pltpu.SMEM)
     return pl.pallas_call(
         warp_kernel,
         out_shape=jax.ShapeDtypeStruct((S, 4, TILE, WIDE), BF16),
-        in_specs=[smem, smem, vmem, vmem],
+        in_specs=[smem, vmem, vmem],
         out_specs=vmem,
-        scratch_shapes=[pltpu.VMEM((TILE, TILE), BF16), pltpu.SMEM((256,), jnp.int32)],
-        input_output_aliases={3: 0},
+        scratch_shapes=[pltpu.VMEM((TILE, TILE), BF16)],
+        input_output_aliases={2: 0},
         compiler_params=pltpu.CompilerParams(vmem_limit_bytes=32 * 1024 * 1024),
         name="warp_partials",
-    )(codes, metas, tiles, blank)
+    )(entries, tiles, blank)
 
 
 CHUNK = 64
@@ -678,9 +697,9 @@
 
 def shards(load_force, stiffness, cracks, anchor, images, owners, source_tile, offsets, blend_weight, counts):
     flat = [a.reshape(1, -1) for a in (owners, source_tile)]
-    displacement, residual, metas, codes, tiles, blank = relax(
+    displacement, residual, entries, tiles, blank = relax(
         load_force, stiffness, cracks, anchor, *flat, offsets, blend_weight.reshape(1, -1), counts.reshape(1, -1), images)
-    part = warp(codes, metas, tiles, blank)
+    part = warp(entries, tiles, blank)
     level_zero, level_one, level_two = scatter(part)
     return store(displacement, residual, level_zero, level_one, level_two)
 

time: 64.3 us -> 59.4 us (0.924)
  the two profiles are of different devices: /device:TPU:1 before, /device:TPU:4 now
where the time goes in v4:
time: 59.4 us; the launch traced here: 59 us
  Pallas kernels  58.3 us (98%)
  between operations  0.66 us (1%)
    pallas_call x1, Pallas kernels, relax(): pl.pallas_call(relax_kernel, out_shape=(jax.ShapeDtypeStruct(block, F32),...  29.1 us
    pallas_call x1, Pallas kernels, scatter(): pl.pallas_call(scatter_kernel, out_shape=(jax.ShapeDtypeStruct((S, TILE,...  23.6 us
    pallas_call x1, Pallas kernels, warp(): pl.pallas_call(warp_kernel, out_shape=jax.ShapeDtypeStruct((S, 4, TILE, W...  4.53 us

profile of v4, /device:TPU:4, one launch (start us, length us, event | category | flops | bytes accessed | tf_op | source)
XLA Modules:
  0.0 59.0 jit_solution(4387144915597582403)
XLA Ops:
  0.6 29.1 %relax_and_gather.1 = (f32[2,2,32,128]{3,2,1,0:T(8,128)S(1)}, f32[2,2,32,128]{3,2,1,0:T(8,128)S(1)}, f32[8,256]{1,0:T(8,128)S(1)}, bf16[2,4,256,1024]{3,2,1,0:T(8,128)(2,1)S(1)}, bf16[2,4,256,1024]{3,2,1,0:T(8,128)(2,1)S(1)}) custom-call(f32[2,2,32,128]{3,2,1,0:T(8,128)} %load_hbm.1, f32[2,2,32,128]{3,2,1,0:T(8,128)} %stiff_hbm.1, ...), custom_call_target="tpu_custom_call" | custom-call | tf_op jit(solution)/shard_map/relax_and_gather/pallas_call | solution.py:459
  29.7 4.5 %warp_partials.1.part_ref = bf16[2,4,256,1024]{3,2,1,0:T(8,128)(2,1)S(1)} custom-call(f32[8,256]{1,0:T(8,128)S(1)} %get-tuple-element.15.list_ref, bf16[2,4,256,1024]{3,2,1,0:T(8,128)(2,1)S(1)} %get-tuple-element.16.tiles_ref, bf16[2,4,256,1024]{3,2,1,0:T(8,128)(2,1)S(1)} %get-tuple-element.17.blank_ref), custom_call_target="tpu_custom_call", output_to_operand_aliasing={{}: (2, {})} | custom-call | tf_op jit(solution)/shard_map/warp_partials/pallas_call | solution.py:544
  34.3 23.6 %scatter_and_pool.1 = (bf16[2,256,1024]{2,1,0:T(8,128)(2,1)S(1)}, bf16[2,128,512]{2,1,0:T(8,128)(2,1)S(1)}, bf16[2,64,256]{2,1,0:T(8,128)(2,1)S(1)}) custom-call(bf16[2,4,256,1024]{3,2,1,0:T(8,128)(2,1)S(1)} %warp_partials.1.part_ref), custom_call_target="tpu_custom_call" | custom-call | tf_op jit(solution)/shard_map/scatter_and_pool/pallas_call | solution.py:651
  57.8 1.2 %store_results.1 = (f32[2,2,32,128]{3,2,1,0:T(8,128)}, f32[2,2,32,128]{3,2,1,0:T(8,128)}, bf16[2,256,1024]{2,1,0:T(8,128)(2,1)}, bf16[2,128,512]{2,1,0:T(8,128)(2,1)}, bf16[2,64,256]{2,1,0:T(8,128)(2,1)}) custom-call(f32[2,2,32,128]{3,2,1,0:T(8,128)S(1)} %get-tuple-element.13.refs_0_, f32[2,2,32,128]{3,2,1,0:T(8,128)S(1)} %get-tuple-element.14.refs_1_, ...), custom_call_target="tpu_custom_call" | custom-call | tf_op jit(solution)/shard_map/store_results/pallas_call | solution.py:687

commit v5 on v4

--- a/solution.py
+++ b/solution.py
@@ -14,6 +14,7 @@
 ENT_DEV = 48
 VR = 32
 VC = 128
+VT = 32
 N_ROW = 8
 N_COL = 16
 WIDE = TC * TILE
@@ -40,7 +41,7 @@
 SCATTER_MASK = (3, 1)
 
 
-NOTE = 24
+NOTE = 8
 LIST = 256
 MOMENTS = 2 * ITERS
 SCALE = 8.0
@@ -113,7 +114,7 @@
 
 def relax_kernel(
     load_hbm, stiff_hbm, crack_hbm, anchor_hbm, owner_hbm, source_hbm, offset_hbm, blend_hbm, count_hbm, images_hbm,
-    disp_ref, resid_ref, list_ref, tiles_ref, blank_ref,
+    disp_ref, resid_ref, list_ref, own_ref, place_ref, tiles_ref, blank_ref,
     fields, stiff, crack, owner, source, offset, blend, count,
     strips, halo_v, halo_h, halo_c, coef, krylov,
     part_a, part_b, got_a, got_b, note, notes, sums,
@@ -212,10 +213,9 @@
     for t in range(ENT_DEV // K):
         listed = jnp.where(entry_lane // K == t, count[:, t:t + 1], listed)
     note[...] = jnp.zeros((NOTE, VC), F32)
-    note[0:1, 0:ENT_DEV] = owner[...].astype(F32)
-    note[1:2, 0:ENT_DEV] = source[...].astype(F32)
-    note[2:4, 0:ENT_DEV] = offset[...].astype(F32)
-    note[4:5, 0:ENT_DEV] = jnp.where(lax.rem(entry_lane, K) < listed, blend[...], 0.0)
+    note[0:1, 0:ENT_DEV] = (owner[...] * TC + source[...]).astype(F32)
+    note[1:3, 0:ENT_DEV] = offset[...].astype(F32)
+    note[3:4, 0:ENT_DEV] = jnp.where(lax.rem(entry_lane, K) < listed, blend[...], 0.0)
 
     blank_ref[...] = jnp.zeros(blank_ref.shape, BF16)
 
@@ -264,9 +264,13 @@
             krylov[n + 1, f] = w * (1.0 / SCALE)
 
     middle = 8 + VR // 2
-    for n in range(ITERS):
-        for f in range(4):
-            note[8 + 4 * n + f:9 + 4 * n + f, :] = krylov[n, f, pl.ds(middle, 1), pl.ds(0, VC)]
+    point = lax.rem(lax.broadcasted_iota(jnp.int32, (1, VC), 1), VT) - VT // 2
+    for f in range(4):
+        row = jnp.zeros((1, VC), F32)
+        for n in range(ITERS):
+            line = krylov[n, f, pl.ds(middle, 1), pl.ds(0, VC)]
+            row = jnp.where(point == n, line if n == 0 else pltpu.roll(line, n, 1), row)
+        note[4 + f:5 + f, :] = row
     told = []
     for s in range(S):
         for i in (1, 2, 3):
@@ -310,10 +314,16 @@
             group = merged
             shift //= 2
         packed.append(group[0])
-    packed = [added(pair, tuple(pltpu.roll(part, VC // 2, 1) for part in pair)) for pair in packed]
+    for step in (VC // 2, VC // 4):
+        packed = [added(pair, tuple(pltpu.roll(part, step, 1) for part in pair)) for pair in packed]
     sum_lane = lax.broadcasted_iota(jnp.int32, (8, VC), 1)
-    part_a[...] = jnp.concatenate(
-        [jnp.where(sum_lane < VC // 2, one, two) for one, two in zip(*packed)], axis=0)
+    quarter = VC // 4
+
+    def joined(one, two):
+        return jnp.where(sum_lane < VC // 2, one, two)
+
+    part_a[...] = joined(
+        *[jnp.where(lax.rem(sum_lane, VC // 2) < quarter, one, two) for one, two in zip(*packed)])
 
     @pl.loop(1, N_ROW)
     def _(d):
@@ -328,15 +338,16 @@
             device_id=((down, c), (r, right))[phase], device_id_type=MESH)
 
     def gathered(own_part, got):
-        terms = [(own_part[0:8], own_part[8:16])]
-        terms += [(got[n, 0:8], got[n, 8:16]) for n in range(got.shape[0])]
+        terms = [own_part[...]] + [got[n] for n in range(got.shape[0])]
+        terms = [(term, pltpu.roll(term, VC // 2, 1)) for term in terms]
         while len(terms) > 1:
             terms = [added(terms[n], terms[n + 1]) if n + 1 < len(terms) else terms[n]
                      for n in range(0, len(terms), 2)]
         return terms[0]
 
     sum_copy(0).wait_recv()
-    part_b[...] = jnp.concatenate(gathered(part_a, got_a), axis=0)
+    high, low = gathered(part_a, got_a)
+    part_b[...] = joined(high, pltpu.roll(low, VC // 2, 1))
 
     @pl.loop(1, N_COL)
     def _(d):
@@ -355,16 +366,19 @@
 
     sum_copy(1).wait_recv()
     total = gathered(part_b, got_b)
-    shift = VC // 4
+    shift = quarter // 2
     while shift:
-        inner = lax.rem(sum_lane, VC // 2) < VC // 2 - shift
+        inner = lax.rem(sum_lane, quarter) < quarter - shift
         total = added(total, tuple(
-            jnp.where(inner, pltpu.roll(part, VC - shift, 1), pltpu.roll(part, VC // 2 - shift, 1)) for part in total))
+            jnp.where(inner, pltpu.roll(part, VC - shift, 1), pltpu.roll(part, quarter - shift, 1)) for part in total))
         shift //= 2
-    upper_lanes = sum_lane < VC // 2
-    spread = [(jnp.where(upper_lanes, part, pltpu.roll(part, VC // 2, 1)),
-               jnp.where(upper_lanes, pltpu.roll(part, VC // 2, 1), part)) for part in total]
-    total = [jnp.concatenate(pair, axis=0) for pair in spread]
+    odd = lax.rem(sum_lane // quarter, 2) == 1
+    spread = []
+    for part in total:
+        one = jnp.where(odd, pltpu.roll(part, quarter, 1), part)
+        two = jnp.where(odd, part, pltpu.roll(part, VC - quarter, 1))
+        spread.append(jnp.concatenate([joined(u, pltpu.roll(u, VC // 2, 1)) for u in (one, two)], axis=0))
+    total = spread
     sums[0:16] = total[0]
     sums[16:32] = total[1]
     rho = residual_polynomial([
@@ -393,38 +407,48 @@
         rows = jnp.concatenate([text[n:n + 1, :] for _, text in texts], axis=0)
         return jnp.where(note_row < 4, rows, pltpu.roll(rows, VC - TC * K, 1))
 
+    note_point = lax.rem(note_lane, VT) - VT // 2
+    scales = jnp.zeros((8, VC), F32)
+    for n in range(ITERS):
+        scale = jnp.where(note_row < 4, rho[n + 1][0:1], rho[n + 1][1:2])
+        scales = jnp.where(note_point == n, scale, scales)
+
     def shifted(k):
-        rows = []
-        for s, text in texts:
-            row = rho[1][s:s + 1] * text[8 + 2 * s + k:9 + 2 * s + k, :]
-            for n in range(1, ITERS):
-                row = row + rho[n + 1][s:s + 1] * text[8 + 4 * n + 2 * s + k:9 + 4 * n + 2 * s + k, :]
-            rows.append(row)
-        rows = jnp.concatenate(rows, axis=0) * (-SPACING / SCALE)
-        shift = stacked(2 + k)
+        rows = scales * jnp.concatenate([text[4 + 2 * s + k:5 + 2 * s + k, :] for s, text in texts], axis=0)
+        rows = rows + pltpu.roll(rows, VC - 1, 1)
+        rows = (rows + pltpu.roll(rows, VC - 2, 1)) * (-SPACING / SCALE)
+        shift = stacked(1 + k)
         for j in range(TC):
-            shift = shift + jnp.where(note_lane // K == j, rows[:, 32 * j + 16:32 * j + 17], 0.0)
+            at = VT * j + VT // 2
+            shift = shift + jnp.where(note_lane // K == j, rows[:, at:at + 1], 0.0)
         return shift
 
-    owner_col = stacked(0).astype(jnp.int32)
-    weight = stacked(4)
+    named = stacked(0).astype(jnp.int32)
+    owner_col = named // TC
+    weight = stacked(3)
     at_y, at_z = lax.rem(owner_col, 4), owner_col // 4
     near = [((at_y == y) | (at_y == flipped(y, m))) & ((at_z == z) | (at_z == flipped(z, m))) for m in GATHER_MASK]
     mine = jnp.where(note_row < 4, near[0].astype(F32), near[1].astype(F32))
     mine = jnp.where((weight > 0.0) & (note_lane < TC * K), mine, 0.0)
     slot = jnp.where(at_y == y, 0, 1) + jnp.where(at_z == z, 0, 2)
-    key = slot * TC + stacked(1).astype(jnp.int32)
+    key = slot * TC + lax.rem(named, TC)
     code = ((note_row * TC + note_lane // K) * 16 + key).astype(F32)
-    rank = mine
+    sent = jnp.where(lax.rem(note_row, 4) == 0, 0.0, mine)
+    rank = sent
     for step in (1, 2, 4, 8, 16):
         rank = rank + jnp.where(note_lane >= step, pltpu.roll(rank, step, 1), 0.0)
-    above = jnp.sum(mine, axis=1, keepdims=True) + jnp.zeros((8, VC), F32)
+    above = jnp.sum(sent, axis=1, keepdims=True) + jnp.zeros((8, VC), F32)
     base = above
     for step in (1, 2, 4):
         base = base + jnp.where(note_row >= step, pltpu.roll(base, step, 0), 0.0)
     total = base[7:8, :]
-    rank = jnp.where(mine > 0.0, rank + (base - above) - 1.0, -1.0)
-    columns = [jnp.transpose(part)[0:TC * K] for part in (rank, code, shifted(0), shifted(1), weight)]
+    rank = jnp.where(sent > 0.0, rank + (base - above) - 1.0, -1.0)
+    shift_y, shift_x = shifted(0), shifted(1)
+    columns = [jnp.transpose(part)[0:TC * K] for part in (rank, code, shift_y, shift_x, weight)]
+    own_ref[...] = jnp.concatenate(
+        [part[4 * s:4 * s + 1] for s in range(S) for part in (weight, shift_y, shift_x, mine * weight)], axis=0)
+    place_ref[...] = jnp.concatenate(
+        [part[4 * s:4 * s + 1] for s in range(S) for part in (slot, lax.rem(named, TC), slot, slot)], axis=0)
     place = lax.broadcasted_iota(jnp.int32, (TC * K, LIST), 1).astype(F32)
     listed = [jnp.zeros((1, LIST), F32)] * 4
     for n in range(8):
@@ -462,11 +486,13 @@
             jax.ShapeDtypeStruct(block, F32),
             jax.ShapeDtypeStruct(block, F32),
             jax.ShapeDtypeStruct((8, LIST), F32),
+            jax.ShapeDtypeStruct((8, VC), F32),
+            jax.ShapeDtypeStruct((8, VC), jnp.int32),
             jax.ShapeDtypeStruct((S, 4, TILE, WIDE), BF16),
-            jax.ShapeDtypeStruct((S, 4, TILE, WIDE), BF16),
+            jax.ShapeDtypeStruct((S, 3, TILE, WIDE), BF16),
         ),
         in_specs=[hbm] * 10,
-        out_specs=(vmem,) * 5,
+        out_specs=(vmem,) * 7,
         scratch_shapes=[
             pltpu.VMEM((10, VR, VC), F32),
             pltpu.VMEM(block, F32),
@@ -482,10 +508,10 @@
             pltpu.VMEM((4, 8, VC), F32),
             pltpu.VMEM((S, 5, ROWS, COLS), F32),
             pltpu.VMEM((ITERS + 1, 4, ROWS, COLS), F32),
-            pltpu.VMEM((16, VC), F32),
-            pltpu.VMEM((16, VC), F32),
-            pltpu.VMEM((N_ROW - 1, 16, VC), F32),
-            pltpu.VMEM((N_COL - 1, 16, VC), F32),
+            pltpu.VMEM((8, VC), F32),
+            pltpu.VMEM((8, VC), F32),
+            pltpu.VMEM((N_ROW - 1, 8, VC), F32),
+            pltpu.VMEM((N_COL - 1, 8, VC), F32),
             pltpu.VMEM((NOTE, VC), F32),
             pltpu.VMEM((S, 3, NOTE, VC), F32),
             pltpu.VMEM((32, VC), F32),
@@ -502,21 +528,31 @@
 BATCH = 6
 
 
+def sampled(apart, shift, side):
+    shift = jnp.full((1, TILE), shift, F32)
+    low = jnp.floor(shift)
+    at_low = jnp.maximum(0.0, 1.0 - jnp.abs(low - shift)).astype(BF16)
+    at_high = jnp.maximum(0.0, 1.0 - jnp.abs(low + 1.0 - shift)).astype(BF16)
+    low_place = (side * low).astype(BF16)
+    high_place = (side * (low + 1.0)).astype(BF16)
+    matrix = apart[...]
+    return jnp.where(matrix == low_place, at_low, jnp.where(matrix == high_place, at_high, jnp.zeros((), BF16)))
+
+
+def warped_by(source, apart, shift_y, shift_x):
+    across = jnp.dot(source, sampled(apart, shift_x, -1.0), preferred_element_type=F32)
+    return jnp.dot(sampled(apart, shift_y, 1.0), across.astype(BF16), preferred_element_type=F32)
+
+
+def columns_apart():
+    row = lax.broadcasted_iota(jnp.int32, (TILE, TILE), 0)
+    lane = lax.broadcasted_iota(jnp.int32, (TILE, TILE), 1)
+    return (lane - row).astype(F32).astype(BF16)
+
+
 def warp_kernel(list_ref, tiles_ref, blank_ref, part_ref, apart):
     count = list_ref[4, 0].astype(jnp.int32)
-    row = lax.broadcasted_iota(jnp.int32, (TILE, TILE), 0)
-    lane = lax.broadcasted_iota(jnp.int32, (TILE, TILE), 1)
-    apart[...] = (lane - row).astype(F32).astype(BF16)
-
-    def sampled(shift, side):
-        shift = jnp.full((1, TILE), shift, F32)
-        low = jnp.floor(shift)
-        at_low = jnp.maximum(0.0, 1.0 - jnp.abs(low - shift)).astype(BF16)
-        at_high = jnp.maximum(0.0, 1.0 - jnp.abs(low + 1.0 - shift)).astype(BF16)
-        low_place = (side * low).astype(BF16)
-        high_place = (side * (low + 1.0)).astype(BF16)
-        matrix = apart[...]
-        return jnp.where(matrix == low_place, at_low, jnp.where(matrix == high_place, at_high, jnp.zeros((), BF16)))
+    apart[...] = columns_apart()
 
     def entry(n):
         code = list_ref[0, n].astype(jnp.int32)
@@ -525,9 +561,8 @@
         place = code >> 6
         s = place >> 2
         source = tiles_ref[s, key >> 2, :, pl.ds(pl.multiple_of((key & 3) * TILE, TILE), TILE)]
-        across = jnp.dot(source, sampled(list_ref[2, n], -1.0), preferred_element_type=F32)
-        down = jnp.dot(sampled(list_ref[1, n], 1.0), across.astype(BF16), preferred_element_type=F32)
-        return list_ref[3, n] * down, (s, place & 3, slice(None), pl.ds(pl.multiple_of(j * TILE, TILE), TILE))
+        value = list_ref[3, n] * warped_by(source, apart, list_ref[1, n], list_ref[2, n])
+        return value, (s, jnp.maximum(place & 3, 1) - 1, slice(None), pl.ds(pl.multiple_of(j * TILE, TILE), TILE))
 
     def batch(b, carry):
         found = [entry(b * BATCH + n) for n in range(BATCH)]
@@ -543,7 +578,7 @@
     smem = pl.BlockSpec(memory_space=pltpu.SMEM)
     return pl.pallas_call(
         warp_kernel,
-        out_shape=jax.ShapeDtypeStruct((S, 4, TILE, WIDE), BF16),
+        out_shape=jax.ShapeDtypeStruct((S, 3, TILE, WIDE), BF16),
         in_specs=[smem, vmem, vmem],
         out_specs=vmem,
         scratch_shapes=[pltpu.VMEM((TILE, TILE), BF16)],
@@ -553,14 +588,14 @@
     )(entries, tiles, blank)
 
 
-CHUNK = 64
 HALVES = 2
-SUBS = TILE // CHUNK // HALVES
+SUBS = ((0, 64), (64, 64))
+DEEP = 64
 
 
 def scatter_kernel(
-    part_ref, zero_ref, one_ref, two_ref,
-    relay, onward, got, pool, half, quarter,
+    listed_ref, placed_ref, tiles_ref, part_ref, zero_ref, one_ref, two_ref,
+    own_ref, place_ref, total, apart, relay, onward, got, pool, half, quarter, twos, list_sem,
     relay_send, relay_recv, direct_send, direct_recv, onward_send, onward_recv,
 ):
     r = lax.axis_index("row")
@@ -572,13 +607,21 @@
         for i in (1, 2):
             pl.semaphore_signal(
                 barrier, inc=1, device_id=(r, peer_col(y, z, SCATTER_MASK[s], i)), device_id_type=MESH)
+    listing = [pltpu.make_async_copy(listed_ref, own_ref, list_sem.at[0]),
+               pltpu.make_async_copy(placed_ref, place_ref, list_sem.at[1])]
+    for copy in listing:
+        copy.start()
     row = lax.broadcasted_iota(jnp.int32, (TILE, VC), 0)
     lane = lax.broadcasted_iota(jnp.int32, (TILE, VC), 1)
     pool[...] = jnp.where(row // 2 == lane, 0.25, 0.0).astype(BF16)
+    apart[...] = columns_apart()
     pl.semaphore_wait(barrier, 2 * S)
 
     def rows_of(h, u):
-        return pl.ds((h * SUBS + u) * CHUNK, CHUNK)
+        return pl.ds(h * (TILE // HALVES) + SUBS[u][0], SUBS[u][1])
+
+    def sub_of(u):
+        return pl.ds(*SUBS[u])
 
     def copy_to(s, peer, near, far, send, recv):
         return pltpu.make_async_remote_copy(
@@ -586,28 +629,48 @@
             device_id=(r, peer_col(y, z, SCATTER_MASK[s], peer)), device_id_type=MESH)
 
     def to_relay(s, h, u):
-        return copy_to(s, h + 1, part_ref.at[s, 3, rows_of(h, u)], relay.at[s, h, u],
+        return copy_to(s, h + 1, part_ref.at[s, 2, rows_of(h, u)], relay.at[s, h, sub_of(u)],
                        relay_send.at[s, h, u], relay_recv.at[s, h, u])
 
     def to_end(s, h, u):
-        return copy_to(s, h + 1, part_ref.at[s, h + 1, rows_of(h, u)], got.at[s, h, rows_of(h, u)],
+        return copy_to(s, h + 1, part_ref.at[s, h, rows_of(h, u)], got.at[s, h, rows_of(h, u)],
                        direct_send.at[s, h, u], direct_recv.at[s, h, u])
 
     def to_end_summed(s, h, u):
         other = 1 - h
-        return copy_to(s, other + 1, onward.at[s, h, u], got.at[s, other, rows_of(h, u)],
+        return copy_to(s, other + 1, onward.at[s, h, sub_of(u)], got.at[s, other, rows_of(h, u)],
                        onward_send.at[s, h, u], onward_recv.at[s, h, u])
 
-    steps = [(u, h, s) for u in range(SUBS) for h in range(HALVES) for s in range(S)]
+    steps = [(u, h, s) for u in range(len(SUBS)) for h in range(HALVES) for s in range(S)]
     for u, h, s in steps:
         to_relay(s, h, u).start()
     for u, h, s in steps:
         to_end(s, h, u).start()
+
+    def own_share(s):
+        @pl.loop(0, TC)
+        def _(j):
+            value = None
+            for k in range(K):
+                e = j * K + k
+                tile = place_ref[4 * s + 1, e]
+                wide = tiles_ref[s, place_ref[4 * s, e]]
+                source = wide[:, 0:TILE]
+                for t in range(1, TC):
+                    source = jnp.where(tile == t, wide[:, t * TILE:(t + 1) * TILE], source)
+                term = own_ref[4 * s + 3, e] * warped_by(source, apart, own_ref[4 * s + 1, e], own_ref[4 * s + 2, e])
+                value = term if value is None else value + term
+            total[s, :, pl.ds(pl.multiple_of(j * TILE, TILE), TILE)] = value
+
+    for copy in listing:
+        copy.wait()
     for u, h, s in steps:
         to_relay(s, h, u).wait_recv()
-        added = relay[s, h, u].astype(F32) + part_ref[s, 2 - h, rows_of(h, u)].astype(F32)
-        onward[s, h, u] = added.astype(BF16)
+        added = relay[s, h, sub_of(u)].astype(F32) + part_ref[s, 1 - h, rows_of(h, u)].astype(F32)
+        onward[s, h, sub_of(u)] = added.astype(BF16)
         to_end_summed(s, h, u).start()
+    own_share(0)
+    own_share(1)
 
     def pooled(block):
         high = block.astype(BF16)
@@ -619,24 +682,25 @@
     for u, h, s in steps:
         to_end(s, h, u).wait_recv()
         to_end_summed(s, h, u).wait_recv()
-        q = h * SUBS + u
         rows = rows_of(h, u)
+        start, deep = rows.start, rows.size
         for j in range(TC):
             cols = pl.ds(j * TILE, TILE)
-            block = part_ref[s, 0, rows, cols].astype(F32)
+            block = total[s, rows, cols]
             for i in range(2):
                 block = block + got[s, i, rows, cols].astype(F32)
             zero_ref[s, rows, cols] = block.astype(BF16)
-            half[j] = pooled(block)
+            half[j, pl.ds(0, deep)] = pooled(block)
         ones = []
         for j in range(TC):
-            piece = half[j, pl.ds(0, CHUNK // 2, stride=2), :] + half[j, pl.ds(1, CHUNK // 2, stride=2), :]
-            one_ref[s, pl.ds(q * (CHUNK // 2), CHUNK // 2), pl.ds(j * VC, VC)] = piece.astype(BF16)
+            piece = half[j, pl.ds(0, deep // 2, stride=2), :] + half[j, pl.ds(1, deep // 2, stride=2), :]
+            one_ref[s, pl.ds(start // 2, deep // 2), pl.ds(j * VC, VC)] = piece.astype(BF16)
             ones.append(piece)
         for j in range(2):
-            quarter[j] = pooled(jnp.concatenate(ones[2 * j:2 * j + 2], axis=1))
-            piece = quarter[j, pl.ds(0, CHUNK // 4, stride=2), :] + quarter[j, pl.ds(1, CHUNK // 4, stride=2), :]
-            two_ref[s, pl.ds(q * (CHUNK // 4), CHUNK // 4), pl.ds(j * VC, VC)] = piece.astype(BF16)
+            quarter[j, pl.ds(0, deep // 2)] = pooled(jnp.concatenate(ones[2 * j:2 * j + 2], axis=1))
+            piece = quarter[j, pl.ds(0, deep // 4, stride=2), :] + quarter[j, pl.ds(1, deep // 4, stride=2), :]
+            twos[s, pl.ds(start // 4, deep // 4), pl.ds(j * VC, VC)] = piece
+    two_ref[...] = twos[...].astype(BF16)
 
     for u, h, s in steps:
         to_relay(s, h, u).wait_send()
@@ -644,10 +708,10 @@
         to_end_summed(s, h, u).wait_send()
 
 
-def scatter(part):
+def scatter(own_list, places, tiles, part):
     vmem = pl.BlockSpec(memory_space=pltpu.VMEM)
-    dma = pltpu.SemaphoreType.DMA
-    parts = (S, HALVES, SUBS)
+    dma = pltpu.SemaphoreType.DMA((S, HALVES, len(SUBS)))
+    halved = pltpu.VMEM((S, HALVES, TILE // HALVES, WIDE), BF16)
     return pl.pallas_call(
         scatter_kernel,
         out_shape=(
@@ -655,21 +719,26 @@
             jax.ShapeDtypeStruct((S, TILE // 2, WIDE // 2), BF16),
             jax.ShapeDtypeStruct((S, TILE // 4, WIDE // 4), BF16),
         ),
-        in_specs=[vmem],
+        in_specs=[vmem, vmem, vmem, vmem],
         out_specs=(vmem, vmem, vmem),
         scratch_shapes=[
-            pltpu.VMEM(parts + (CHUNK, WIDE), BF16),
-            pltpu.VMEM(parts + (CHUNK, WIDE), BF16),
+            pltpu.SMEM((8, VC), F32),
+            pltpu.SMEM((8, VC), jnp.int32),
+            pltpu.VMEM((S, TILE, WIDE), F32),
+            pltpu.VMEM((TILE, TILE), BF16),
+            halved,
+            halved,
             pltpu.VMEM((S, 2, TILE, WIDE), BF16),
             pltpu.VMEM((TILE, VC), BF16),
-            pltpu.VMEM((TC, CHUNK, VC), F32),
-            pltpu.VMEM((2, CHUNK // 2, VC), F32),
-            dma(parts), dma(parts), dma(parts), dma(parts), dma(parts), dma(parts),
+            pltpu.VMEM((TC, DEEP, VC), F32),
+            pltpu.VMEM((2, DEEP // 2, VC), F32),
+            pltpu.VMEM((S, TILE // 4, WIDE // 4), F32),
+            pltpu.SemaphoreType.DMA((2,)), dma, dma, dma, dma, dma, dma,
         ],
         compiler_params=pltpu.CompilerParams(
             collective_id=1, has_side_effects=True, vmem_limit_bytes=32 * 1024 * 1024),
         name="scatter_and_pool",
-    )(part)
+    )(own_list, places, tiles, part)
 
 
 def store_kernel(*refs):
@@ -697,10 +766,10 @@
 
 def shards(load_force, stiffness, cracks, anchor, images, owners, source_tile, offsets, blend_weight, counts):
     flat = [a.reshape(1, -1) for a in (owners, source_tile)]
-    displacement, residual, entries, tiles, blank = relax(
+    displacement, residual, entries, own_list, places, tiles, blank = relax(
         load_force, stiffness, cracks, anchor, *flat, offsets, blend_weight.reshape(1, -1), counts.reshape(1, -1), images)
     part = warp(entries, tiles, blank)
-    level_zero, level_one, level_two = scatter(part)
+    level_zero, level_one, level_two = scatter(own_list, places, tiles, part)
     return store(displacement, residual, level_zero, level_one, level_two)
 
 

time: 59.4 us -> 57.1 us (0.961)
  Pallas kernels: 58.3 us -> 55.6 us
    pallas_call x1, Pallas kernels: 23.6 us -> 21.9 us  [scatter(): pl.pallas_call(scatter_kernel, out_shape=(jax.ShapeDtypeStruct((S, TILE,...]
    pallas_call x1, Pallas kernels: 29.1 us -> 28 us  [relax(): pl.pallas_call(relax_kernel, out_shape=(jax.ShapeDtypeStruct(block, F32),...]
where the time goes in v5:
time: 57.1 us; the launch traced here: 56.2 us
  Pallas kernels  55.6 us (97%)
  between operations  0.66 us (1%)
    pallas_call x1, Pallas kernels, relax(): pl.pallas_call(relax_kernel, out_shape=(jax.ShapeDtypeStruct(block, F32),...  28 us
    pallas_call x1, Pallas kernels, scatter(): pl.pallas_call(scatter_kernel, out_shape=(jax.ShapeDtypeStruct((S, TILE,...  21.9 us
    pallas_call x1, Pallas kernels, warp(): pl.pallas_call(warp_kernel, out_shape=jax.ShapeDtypeStruct((S, 3, TILE, W...  4.51 us
    pallas_call x1, Pallas kernels, store(): pl.pallas_call(store_kernel, out_shape=tuple((jax.ShapeDtypeStruct(a.shap...  1.15 us

profile of v5, /device:TPU:4, one launch (start us, length us, event | category | flops | bytes accessed | tf_op | source)
XLA Modules:
  0.0 56.2 jit_solution(10452603772029892752)
XLA Ops:
  0.6 28.0 %relax_and_gather.1 = (f32[2,2,32,128]{3,2,1,0:T(8,128)S(1)}, f32[2,2,32,128]{3,2,1,0:T(8,128)S(1)}, f32[8,256]{1,0:T(8,128)S(1)}, f32[8,128]{1,0:T(8,128)S(1)},...) custom-call(f32[2,2,32,128]{3,2,1,0:T(8,128)} %load_hbm.1, ...), custom_call_target="tpu_custom_call" | custom-call | tf_op jit(solution)/shard_map/relax_and_gather/pallas_call | solution.py:483
  28.7 4.5 %warp_partials.1.part_ref = bf16[2,3,256,1024]{3,2,1,0:T(8,128)(2,1)S(1)} custom-call(f32[8,256]{1,0:T(8,128)S(1)} %get-tuple-element.20.list_ref, bf16[2,4,256,1024]{3,2,1,0:T(8,128)(2,1)S(1)} %get-tuple-element.19.tiles_ref, bf16[2,3,256,1024]{3,2,1,0:T(8,128)(2,1)S(1)} %get-tuple-element.21.blank_ref), custom_call_target="tpu_custom_call", output_to_operand_aliasing={{}: (2, {})} | custom-call | tf_op jit(solution)/shard_map/warp_partials/pallas_call | solution.py:579
  33.2 21.9 %scatter_and_pool.1 = (bf16[2,256,1024]{2,1,0:T(8,128)(2,1)S(1)}, bf16[2,128,512]{2,1,0:T(8,128)(2,1)S(1)}, bf16[2,64,256]{2,1,0:T(8,128)(2,1)S(1)}) custom-call(f32[8,128]{1,0:T(8,128)S(1)} %get-tuple-element.17.listed_ref, s32[8,128]{1,0:T(8,128)S(1)} %get-tuple-element.18.placed_ref, bf16[2,4,256,1024]{3,2,1,0:T(8,128)(2,1)S(1)} %get-tuple-element.19.tiles_ref, ...), custom_call_target="tpu_custom_call" | custom-call | tf_op jit(solution)/shard_map/scatter_and_pool/pallas_call | solution.py:715
  55.1 1.2 %store_results.1 = (f32[2,2,32,128]{3,2,1,0:T(8,128)}, f32[2,2,32,128]{3,2,1,0:T(8,128)}, bf16[2,256,1024]{2,1,0:T(8,128)(2,1)}, bf16[2,128,512]{2,1,0:T(8,128)(2,1)}, bf16[2,64,256]{2,1,0:T(8,128)(2,1)}) custom-call(f32[2,2,32,128]{3,2,1,0:T(8,128)S(1)} %get-tuple-element.15.refs_0_, f32[2,2,32,128]{3,2,1,0:T(8,128)S(1)} %get-tuple-element.16.refs_1_, ...), custom_call_target="tpu_custom_call" | custom-call | tf_op jit(solution)/shard_map/store_results/pallas_call | solution.py:756

commit v6 on v5

--- a/solution.py
+++ b/solution.py
@@ -1,3 +1,5 @@
+import functools
+
 import jax
 import jax.numpy as jnp
 from jax import lax
@@ -131,17 +133,6 @@
 
     barrier = pltpu.get_barrier_semaphore()
 
-    @pl.loop(1, N_ROW)
-    def _(d):
-        pl.semaphore_signal(barrier, inc=1, device_id=(lax.rem(r + d, N_ROW), c), device_id_type=MESH)
-
-    @pl.loop(1, N_COL)
-    def _(d):
-        pl.semaphore_signal(barrier, inc=1, device_id=(r, lax.rem(c + d, N_COL)), device_id_type=MESH)
-
-    for corner in corners:
-        pl.semaphore_signal(barrier, inc=1, device_id=corner, device_id_type=MESH)
-
     loads = []
     for n, (near, far) in enumerate((
         (stiff_hbm, stiff), (crack_hbm, crack),
@@ -152,6 +143,17 @@
         loads.append(pltpu.make_async_copy(near, far, load_sem.at[n]))
     for copy in loads:
         copy.start()
+    @pl.loop(1, N_ROW)
+    def _(d):
+        pl.semaphore_signal(barrier, inc=1, device_id=(lax.rem(r + d, N_ROW), c), device_id_type=MESH)
+
+    @pl.loop(1, N_COL)
+    def _(d):
+        pl.semaphore_signal(barrier, inc=1, device_id=(r, lax.rem(c + d, N_COL)), device_id_type=MESH)
+
+    for corner in corners:
+        pl.semaphore_signal(barrier, inc=1, device_id=corner, device_id_type=MESH)
+
     for copy in loads:
         copy.wait()
     for s in range(S):
@@ -325,8 +327,7 @@
     part_a[...] = joined(
         *[jnp.where(lax.rem(sum_lane, VC // 2) < quarter, one, two) for one, two in zip(*packed)])
 
-    @pl.loop(1, N_ROW)
-    def _(d):
+    for d in range(1, N_ROW):
         pltpu.make_async_remote_copy(
             src_ref=part_a, dst_ref=got_a.at[d - 1], send_sem=send_a,
             recv_sem=recv_a, device_id=(lax.rem(r + d, N_ROW), c), device_id_type=MESH).start()
@@ -349,8 +350,7 @@
     high, low = gathered(part_a, got_a)
     part_b[...] = joined(high, pltpu.roll(low, VC // 2, 1))
 
-    @pl.loop(1, N_COL)
-    def _(d):
+    for d in range(1, N_COL):
         pltpu.make_async_remote_copy(
             src_ref=part_b, dst_ref=got_b.at[d - 1], send_sem=send_b,
             recv_sem=recv_b, device_id=(r, lax.rem(c + d, N_COL)), device_id_type=MESH).start()
@@ -433,7 +433,7 @@
     slot = jnp.where(at_y == y, 0, 1) + jnp.where(at_z == z, 0, 2)
     key = slot * TC + lax.rem(named, TC)
     code = ((note_row * TC + note_lane // K) * 16 + key).astype(F32)
-    sent = jnp.where(lax.rem(note_row, 4) == 0, 0.0, mine)
+    sent = jnp.where(lax.rem(note_row, 4) < 2, 0.0, mine)
     rank = sent
     for step in (1, 2, 4, 8, 16):
         rank = rank + jnp.where(note_lane >= step, pltpu.roll(rank, step, 1), 0.0)
@@ -446,9 +446,11 @@
     shift_y, shift_x = shifted(0), shifted(1)
     columns = [jnp.transpose(part)[0:TC * K] for part in (rank, code, shift_y, shift_x, weight)]
     own_ref[...] = jnp.concatenate(
-        [part[4 * s:4 * s + 1] for s in range(S) for part in (weight, shift_y, shift_x, mine * weight)], axis=0)
+        [part[4 * s + i:4 * s + i + 1] for s in range(S) for i in range(2)
+         for part in (weight, shift_y, shift_x, mine * weight)], axis=0)
     place_ref[...] = jnp.concatenate(
-        [part[4 * s:4 * s + 1] for s in range(S) for part in (slot, lax.rem(named, TC), slot, slot)], axis=0)
+        [part[4 * s + i:4 * s + i + 1] for s in range(S) for i in range(2)
+         for part in (slot, lax.rem(named, TC), slot, slot)], axis=0)
     place = lax.broadcasted_iota(jnp.int32, (TC * K, LIST), 1).astype(F32)
     listed = [jnp.zeros((1, LIST), F32)] * 4
     for n in range(8):
@@ -486,10 +488,10 @@
             jax.ShapeDtypeStruct(block, F32),
             jax.ShapeDtypeStruct(block, F32),
             jax.ShapeDtypeStruct((8, LIST), F32),
-            jax.ShapeDtypeStruct((8, VC), F32),
-            jax.ShapeDtypeStruct((8, VC), jnp.int32),
+            jax.ShapeDtypeStruct((16, VC), F32),
+            jax.ShapeDtypeStruct((16, VC), jnp.int32),
             jax.ShapeDtypeStruct((S, 4, TILE, WIDE), BF16),
-            jax.ShapeDtypeStruct((S, 3, TILE, WIDE), BF16),
+            jax.ShapeDtypeStruct((S, 2, TILE, WIDE), BF16),
         ),
         in_specs=[hbm] * 10,
         out_specs=(vmem,) * 7,
@@ -525,7 +527,7 @@
     )(*operands)
 
 
-BATCH = 6
+BATCH = 8
 
 
 def sampled(apart, shift, side):
@@ -562,7 +564,7 @@
         s = place >> 2
         source = tiles_ref[s, key >> 2, :, pl.ds(pl.multiple_of((key & 3) * TILE, TILE), TILE)]
         value = list_ref[3, n] * warped_by(source, apart, list_ref[1, n], list_ref[2, n])
-        return value, (s, jnp.maximum(place & 3, 1) - 1, slice(None), pl.ds(pl.multiple_of(j * TILE, TILE), TILE))
+        return value, (s, jnp.maximum(place & 3, 2) - 2, slice(None), pl.ds(pl.multiple_of(j * TILE, TILE), TILE))
 
     def batch(b, carry):
         found = [entry(b * BATCH + n) for n in range(BATCH)]
@@ -578,7 +580,7 @@
     smem = pl.BlockSpec(memory_space=pltpu.SMEM)
     return pl.pallas_call(
         warp_kernel,
-        out_shape=jax.ShapeDtypeStruct((S, 3, TILE, WIDE), BF16),
+        out_shape=jax.ShapeDtypeStruct((S, 2, TILE, WIDE), BF16),
         in_specs=[smem, vmem, vmem],
         out_specs=vmem,
         scratch_shapes=[pltpu.VMEM((TILE, TILE), BF16)],
@@ -595,7 +597,7 @@
 
 def scatter_kernel(
     listed_ref, placed_ref, tiles_ref, part_ref, zero_ref, one_ref, two_ref,
-    own_ref, place_ref, total, apart, relay, onward, got, pool, half, quarter, twos, list_sem,
+    own_ref, place_ref, nearer, total, apart, relay, onward, got, pool, half, quarter, twos, list_sem,
     relay_send, relay_recv, direct_send, direct_recv, onward_send, onward_recv,
 ):
     r = lax.axis_index("row")
@@ -629,11 +631,12 @@
             device_id=(r, peer_col(y, z, SCATTER_MASK[s], peer)), device_id_type=MESH)
 
     def to_relay(s, h, u):
-        return copy_to(s, h + 1, part_ref.at[s, 2, rows_of(h, u)], relay.at[s, h, sub_of(u)],
+        return copy_to(s, h + 1, part_ref.at[s, 1, rows_of(h, u)], relay.at[s, h, sub_of(u)],
                        relay_send.at[s, h, u], relay_recv.at[s, h, u])
 
     def to_end(s, h, u):
-        return copy_to(s, h + 1, part_ref.at[s, h, rows_of(h, u)], got.at[s, h, rows_of(h, u)],
+        near = nearer.at[s] if h == 0 else part_ref.at[s, 0]
+        return copy_to(s, h + 1, near.at[rows_of(h, u)], got.at[s, h, rows_of(h, u)],
                        direct_send.at[s, h, u], direct_recv.at[s, h, u])
 
     def to_end_summed(s, h, u):
@@ -645,32 +648,45 @@
     for u, h, s in steps:
         to_relay(s, h, u).start()
     for u, h, s in steps:
-        to_end(s, h, u).start()
-
-    def own_share(s):
+        if h == 1:
+            to_end(s, h, u).start()
+
+    def share(s, i, put):
         @pl.loop(0, TC)
         def _(j):
             value = None
+            base = 4 * (2 * s + i)
             for k in range(K):
                 e = j * K + k
-                tile = place_ref[4 * s + 1, e]
-                wide = tiles_ref[s, place_ref[4 * s, e]]
+                tile = place_ref[base + 1, e]
+                wide = tiles_ref[s, place_ref[base, e]]
                 source = wide[:, 0:TILE]
                 for t in range(1, TC):
                     source = jnp.where(tile == t, wide[:, t * TILE:(t + 1) * TILE], source)
-                term = own_ref[4 * s + 3, e] * warped_by(source, apart, own_ref[4 * s + 1, e], own_ref[4 * s + 2, e])
+                term = own_ref[base + 3, e] * warped_by(source, apart, own_ref[base + 1, e], own_ref[base + 2, e])
                 value = term if value is None else value + term
-            total[s, :, pl.ds(pl.multiple_of(j * TILE, TILE), TILE)] = value
+            put(value, pl.ds(pl.multiple_of(j * TILE, TILE), TILE))
+
+    def put_near(s, value, cols):
+        nearer[s, :, cols] = value.astype(BF16)
+
+    def put_own(s, value, cols):
+        total[s, :, cols] = value
 
     for copy in listing:
         copy.wait()
+    for s in range(S):
+        share(s, 1, functools.partial(put_near, s))
+        for u in range(len(SUBS)):
+            to_end(s, 0, u).start()
     for u, h, s in steps:
         to_relay(s, h, u).wait_recv()
-        added = relay[s, h, sub_of(u)].astype(F32) + part_ref[s, 1 - h, rows_of(h, u)].astype(F32)
-        onward[s, h, sub_of(u)] = added.astype(BF16)
+        ours = part_ref[s, 0, rows_of(h, u)] if h == 0 else nearer[s, rows_of(h, u)]
+        summed = relay[s, h, sub_of(u)].astype(F32) + ours.astype(F32)
+        onward[s, h, sub_of(u)] = summed.astype(BF16)
         to_end_summed(s, h, u).start()
-    own_share(0)
-    own_share(1)
+    for s in range(S):
+        share(s, 0, functools.partial(put_own, s))
 
     def pooled(block):
         high = block.astype(BF16)
@@ -681,14 +697,16 @@
 
     for u, h, s in steps:
         to_end(s, h, u).wait_recv()
+        rows = rows_of(h, u)
+        total[s, rows] = total[s, rows] + got[s, h, rows].astype(F32)
+
+    for u, h, s in steps:
         to_end_summed(s, h, u).wait_recv()
         rows = rows_of(h, u)
         start, deep = rows.start, rows.size
         for j in range(TC):
             cols = pl.ds(j * TILE, TILE)
-            block = total[s, rows, cols]
-            for i in range(2):
-                block = block + got[s, i, rows, cols].astype(F32)
+            block = total[s, rows, cols] + got[s, 1 - h, rows, cols].astype(F32)
             zero_ref[s, rows, cols] = block.astype(BF16)
             half[j, pl.ds(0, deep)] = pooled(block)
         ones = []
@@ -722,8 +740,9 @@
         in_specs=[vmem, vmem, vmem, vmem],
         out_specs=(vmem, vmem, vmem),
         scratch_shapes=[
-            pltpu.SMEM((8, VC), F32),
-            pltpu.SMEM((8, VC), jnp.int32),
+            pltpu.SMEM((16, VC), F32),
+            pltpu.SMEM((16, VC), jnp.int32),
+            pltpu.VMEM((S, TILE, WIDE), BF16),
             pltpu.VMEM((S, TILE, WIDE), F32),
             pltpu.VMEM((TILE, TILE), BF16),
             halved,
@@ -741,10 +760,20 @@
     )(own_list, places, tiles, part)
 
 
+STORES = 8
+
+
 def store_kernel(*refs):
     count = (len(refs) - 1) // 2
     sems = refs[-1]
-    copies = [pltpu.make_async_copy(refs[n], refs[count + n], sems.at[n]) for n in range(count)]
+    copies = []
+    for n in range(count):
+        near, far = refs[n], refs[count + n]
+        pieces = STORES if n == 2 else 1
+        rows = near.shape[1] // pieces
+        for p in range(pieces):
+            span = pl.ds(p * rows, rows)
+            copies.append(pltpu.make_async_copy(near.at[:, span], far.at[:, span], sems.at[len(copies)]))
     for copy in copies:
         copy.start()
     for copy in copies:
@@ -758,7 +787,7 @@
         out_shape=tuple(jax.ShapeDtypeStruct(a.shape, a.dtype) for a in arrays),
         in_specs=[pl.BlockSpec(memory_space=pltpu.VMEM)] * count,
         out_specs=(pl.BlockSpec(memory_space=pltpu.HBM),) * count,
-        scratch_shapes=[pltpu.SemaphoreType.DMA((count,))],
+        scratch_shapes=[pltpu.SemaphoreType.DMA((count + STORES - 1,))],
         compiler_params=pltpu.CompilerParams(vmem_limit_bytes=32 * 1024 * 1024),
         name="store_results",
     )(*arrays)

time: 57.1 us -> 56.1 us (0.982)
    pallas_call x1, Pallas kernels: 4.51 us -> 2.57 us  [warp(): pl.pallas_call(warp_kernel, out_shape=jax.ShapeDtypeStruct((S, 2, TILE, W...]
    pallas_call x1, Pallas kernels: 21.9 us -> 23.3 us  [scatter(): pl.pallas_call(scatter_kernel, out_shape=(jax.ShapeDtypeStruct((S, TILE,...]
where the time goes in v6:
time: 56.1 us; the launch traced here: 55.8 us
  Pallas kernels  55.1 us (98%)
  between operations  0.66 us (1%)
    pallas_call x1, Pallas kernels, relax(): pl.pallas_call(relax_kernel, out_shape=(jax.ShapeDtypeStruct(block, F32),...  28 us
    pallas_call x1, Pallas kernels, scatter(): pl.pallas_call(scatter_kernel, out_shape=(jax.ShapeDtypeStruct((S, TILE,...  23.3 us
    pallas_call x1, Pallas kernels, warp(): pl.pallas_call(warp_kernel, out_shape=jax.ShapeDtypeStruct((S, 2, TILE, W...  2.57 us
    pallas_call x1, Pallas kernels, store(): pl.pallas_call(store_kernel, out_shape=tuple((jax.ShapeDtypeStruct(a.shap...  1.21 us

profile of v6, /device:TPU:4, one launch (start us, length us, event | category | flops | bytes accessed | tf_op | source)
XLA Modules:
  0.0 55.8 jit_solution(9797702397107131556)
XLA Ops:
  0.6 28.0 %relax_and_gather.1 = (f32[2,2,32,128]{3,2,1,0:T(8,128)S(1)}, f32[2,2,32,128]{3,2,1,0:T(8,128)S(1)}, f32[8,256]{1,0:T(8,128)S(1)}, f32[16,128]{1,0:T(8,128)S(1)}...) custom-call(f32[2,2,32,128]{3,2,1,0:T(8,128)} %load_hbm.1, ...), custom_call_target="tpu_custom_call" | custom-call | tf_op jit(solution)/shard_map/relax_and_gather/pallas_call | solution.py:485
  28.7 2.6 %warp_partials.1.part_ref = bf16[2,2,256,1024]{3,2,1,0:T(8,128)(2,1)S(1)} custom-call(f32[8,256]{1,0:T(8,128)S(1)} %get-tuple-element.20.list_ref, bf16[2,4,256,1024]{3,2,1,0:T(8,128)(2,1)S(1)} %get-tuple-element.19.tiles_ref, bf16[2,2,256,1024]{3,2,1,0:T(8,128)(2,1)S(1)} %get-tuple-element.21.blank_ref), custom_call_target="tpu_custom_call", output_to_operand_aliasing={{}: (2, {})} | custom-call | tf_op jit(solution)/shard_map/warp_partials/pallas_call | solution.py:581
  31.2 23.3 %scatter_and_pool.1 = (bf16[2,256,1024]{2,1,0:T(8,128)(2,1)S(1)}, bf16[2,128,512]{2,1,0:T(8,128)(2,1)S(1)}, bf16[2,64,256]{2,1,0:T(8,128)(2,1)S(1)}) custom-call(f32[16,128]{1,0:T(8,128)S(1)} %get-tuple-element.17.listed_ref, s32[16,128]{1,0:T(8,128)S(1)} %get-tuple-element.18.placed_ref, bf16[2,4,256,1024]{3,2,1,0:T(8,128)(2,1)S(1)} %get-tuple-element.19.tiles_ref, ...), custom_call_target="tpu_custom_call" | custom-call | tf_op jit(solution)/shard_map/scatter_and_pool/pallas_call | solution.py:733
  54.6 1.2 %store_results.1 = (f32[2,2,32,128]{3,2,1,0:T(8,128)}, f32[2,2,32,128]{3,2,1,0:T(8,128)}, bf16[2,256,1024]{2,1,0:T(8,128)(2,1)}, bf16[2,128,512]{2,1,0:T(8,128)(2,1)}, bf16[2,64,256]{2,1,0:T(8,128)(2,1)}) custom-call(f32[2,2,32,128]{3,2,1,0:T(8,128)S(1)} %get-tuple-element.15.refs_0_, f32[2,2,32,128]{3,2,1,0:T(8,128)S(1)} %get-tuple-element.16.refs_1_, ...), custom_call_target="tpu_custom_call" | custom-call | tf_op jit(solution)/shard_map/store_results/pallas_call | solution.py:785

commit v7 on v6

--- a/solution.py
+++ b/solution.py
@@ -143,16 +143,12 @@
         loads.append(pltpu.make_async_copy(near, far, load_sem.at[n]))
     for copy in loads:
         copy.start()
-    @pl.loop(1, N_ROW)
-    def _(d):
-        pl.semaphore_signal(barrier, inc=1, device_id=(lax.rem(r + d, N_ROW), c), device_id_type=MESH)
-
-    @pl.loop(1, N_COL)
-    def _(d):
-        pl.semaphore_signal(barrier, inc=1, device_id=(r, lax.rem(c + d, N_COL)), device_id_type=MESH)
-
     for corner in corners:
         pl.semaphore_signal(barrier, inc=1, device_id=corner, device_id_type=MESH)
+    for d in range(1, N_COL):
+        pl.semaphore_signal(barrier, inc=1, device_id=(r, lax.rem(c + d, N_COL)), device_id_type=MESH)
+    for d in range(1, N_ROW):
+        pl.semaphore_signal(barrier, inc=1, device_id=(lax.rem(r + d, N_ROW), c), device_id_type=MESH)
 
     for copy in loads:
         copy.wait()
@@ -630,14 +626,17 @@
             src_ref=near, dst_ref=far, send_sem=send, recv_sem=recv,
             device_id=(r, peer_col(y, z, SCATTER_MASK[s], peer)), device_id_type=MESH)
 
-    def to_relay(s, h, u):
-        return copy_to(s, h + 1, part_ref.at[s, 1, rows_of(h, u)], relay.at[s, h, sub_of(u)],
-                       relay_send.at[s, h, u], relay_recv.at[s, h, u])
-
-    def to_end(s, h, u):
+    def half_of(h):
+        return pl.ds(h * (TILE // HALVES), TILE // HALVES)
+
+    def to_relay(s, h):
+        return copy_to(s, h + 1, part_ref.at[s, 1, half_of(h)], relay.at[s, h],
+                       relay_send.at[s, h], relay_recv.at[s, h])
+
+    def to_end(s, h):
         near = nearer.at[s] if h == 0 else part_ref.at[s, 0]
-        return copy_to(s, h + 1, near.at[rows_of(h, u)], got.at[s, h, rows_of(h, u)],
-                       direct_send.at[s, h, u], direct_recv.at[s, h, u])
+        return copy_to(s, h + 1, near.at[half_of(h)], got.at[s, h, half_of(h)],
+                       direct_send.at[s, h], direct_recv.at[s, h])
 
     def to_end_summed(s, h, u):
         other = 1 - h
@@ -645,11 +644,11 @@
                        onward_send.at[s, h, u], onward_recv.at[s, h, u])
 
     steps = [(u, h, s) for u in range(len(SUBS)) for h in range(HALVES) for s in range(S)]
-    for u, h, s in steps:
-        to_relay(s, h, u).start()
-    for u, h, s in steps:
-        if h == 1:
-            to_end(s, h, u).start()
+    ways = [(h, s) for h in range(HALVES) for s in range(S)]
+    for h, s in ways:
+        to_relay(s, h).start()
+    for s in range(S):
+        to_end(s, 1).start()
 
     def share(s, i, put):
         @pl.loop(0, TC)
@@ -677,10 +676,10 @@
         copy.wait()
     for s in range(S):
         share(s, 1, functools.partial(put_near, s))
-        for u in range(len(SUBS)):
-            to_end(s, 0, u).start()
+        to_end(s, 0).start()
+    for h, s in ways:
+        to_relay(s, h).wait_recv()
     for u, h, s in steps:
-        to_relay(s, h, u).wait_recv()
         ours = part_ref[s, 0, rows_of(h, u)] if h == 0 else nearer[s, rows_of(h, u)]
         summed = relay[s, h, sub_of(u)].astype(F32) + ours.astype(F32)
         onward[s, h, sub_of(u)] = summed.astype(BF16)
@@ -695,9 +694,9 @@
         return (jnp.dot(high, matrix, preferred_element_type=F32)
                 + jnp.dot(low, matrix, preferred_element_type=F32))
 
-    for u, h, s in steps:
-        to_end(s, h, u).wait_recv()
-        rows = rows_of(h, u)
+    for h, s in ways:
+        to_end(s, h).wait_recv()
+        rows = half_of(h)
         total[s, rows] = total[s, rows] + got[s, h, rows].astype(F32)
 
     for u, h, s in steps:
@@ -720,15 +719,17 @@
             twos[s, pl.ds(start // 4, deep // 4), pl.ds(j * VC, VC)] = piece
     two_ref[...] = twos[...].astype(BF16)
 
+    for h, s in ways:
+        to_relay(s, h).wait_send()
+        to_end(s, h).wait_send()
     for u, h, s in steps:
-        to_relay(s, h, u).wait_send()
-        to_end(s, h, u).wait_send()
         to_end_summed(s, h, u).wait_send()
 
 
 def scatter(own_list, places, tiles, part):
     vmem = pl.BlockSpec(memory_space=pltpu.VMEM)
     dma = pltpu.SemaphoreType.DMA((S, HALVES, len(SUBS)))
+    way = pltpu.SemaphoreType.DMA((S, HALVES))
     halved = pltpu.VMEM((S, HALVES, TILE // HALVES, WIDE), BF16)
     return pl.pallas_call(
         scatter_kernel,
@@ -752,7 +753,7 @@
             pltpu.VMEM((TC, DEEP, VC), F32),
             pltpu.VMEM((2, DEEP // 2, VC), F32),
             pltpu.VMEM((S, TILE // 4, WIDE // 4), F32),
-            pltpu.SemaphoreType.DMA((2,)), dma, dma, dma, dma, dma, dma,
+            pltpu.SemaphoreType.DMA((2,)), way, way, way, way, dma, dma,
         ],
         compiler_params=pltpu.CompilerParams(
             collective_id=1, has_side_effects=True, vmem_limit_bytes=32 * 1024 * 1024),

time: 56.1 us -> 55.8 us (level)
  Pallas kernels: 55.1 us -> 54.4 us
where the time goes in v7:
time: 55.8 us; the launch traced here: 55 us
  Pallas kernels  54.4 us (97%)
  between operations  0.66 us (1%)
    pallas_call x1, Pallas kernels, relax(): pl.pallas_call(relax_kernel, out_shape=(jax.ShapeDtypeStruct(block, F32),...  27.7 us
    pallas_call x1, Pallas kernels, scatter(): pl.pallas_call(scatter_kernel, out_shape=(jax.ShapeDtypeStruct((S, TILE,...  22.9 us
    pallas_call x1, Pallas kernels, warp(): pl.pallas_call(warp_kernel, out_shape=jax.ShapeDtypeStruct((S, 2, TILE, W...  2.56 us
    pallas_call x1, Pallas kernels, store(): pl.pallas_call(store_kernel, out_shape=tuple((jax.ShapeDtypeStruct(a.shap...  1.21 us

profile of v7, /device:TPU:4, one launch (start us, length us, event | category | flops | bytes accessed | tf_op | source)
XLA Modules:
  0.0 55.0 jit_solution(15901588017698329257)
XLA Ops:
  0.6 27.7 %relax_and_gather.1 = (f32[2,2,32,128]{3,2,1,0:T(8,128)S(1)}, f32[2,2,32,128]{3,2,1,0:T(8,128)S(1)}, f32[8,256]{1,0:T(8,128)S(1)}, f32[16,128]{1,0:T(8,128)S(1)}...) custom-call(f32[2,2,32,128]{3,2,1,0:T(8,128)} %load_hbm.1, ...), custom_call_target="tpu_custom_call" | custom-call | tf_op jit(solution)/shard_map/relax_and_gather/pallas_call | solution.py:481
  28.3 2.6 %warp_partials.1.part_ref = bf16[2,2,256,1024]{3,2,1,0:T(8,128)(2,1)S(1)} custom-call(f32[8,256]{1,0:T(8,128)S(1)} %get-tuple-element.20.list_ref, bf16[2,4,256,1024]{3,2,1,0:T(8,128)(2,1)S(1)} %get-tuple-element.19.tiles_ref, bf16[2,2,256,1024]{3,2,1,0:T(8,128)(2,1)S(1)} %get-tuple-element.21.blank_ref), custom_call_target="tpu_custom_call", output_to_operand_aliasing={{}: (2, {})} | custom-call | tf_op jit(solution)/shard_map/warp_partials/pallas_call | solution.py:577
  30.9 22.9 %scatter_and_pool.1 = (bf16[2,256,1024]{2,1,0:T(8,128)(2,1)S(1)}, bf16[2,128,512]{2,1,0:T(8,128)(2,1)S(1)}, bf16[2,64,256]{2,1,0:T(8,128)(2,1)S(1)}) custom-call(f32[16,128]{1,0:T(8,128)S(1)} %get-tuple-element.17.listed_ref, s32[16,128]{1,0:T(8,128)S(1)} %get-tuple-element.18.placed_ref, bf16[2,4,256,1024]{3,2,1,0:T(8,128)(2,1)S(1)} %get-tuple-element.19.tiles_ref, ...), custom_call_target="tpu_custom_call" | custom-call | tf_op jit(solution)/shard_map/scatter_and_pool/pallas_call | solution.py:734
  53.8 1.2 %store_results.1 = (f32[2,2,32,128]{3,2,1,0:T(8,128)}, f32[2,2,32,128]{3,2,1,0:T(8,128)}, bf16[2,256,1024]{2,1,0:T(8,128)(2,1)}, bf16[2,128,512]{2,1,0:T(8,128)(2,1)}, bf16[2,64,256]{2,1,0:T(8,128)(2,1)}) custom-call(f32[2,2,32,128]{3,2,1,0:T(8,128)S(1)} %get-tuple-element.15.refs_0_, f32[2,2,32,128]{3,2,1,0:T(8,128)S(1)} %get-tuple-element.16.refs_1_, ...), custom_call_target="tpu_custom_call" | custom-call | tf_op jit(solution)/shard_map/store_results/pallas_call | solution.py:786

commit v8 on v7

--- a/solution.py
+++ b/solution.py
@@ -548,9 +548,12 @@
     return (lane - row).astype(F32).astype(BF16)
 
 
-def warp_kernel(list_ref, tiles_ref, blank_ref, part_ref, apart):
+def warp_kernel(listed_ref, tiles_ref, blank_ref, part_ref, apart, list_ref, list_sem):
+    listing = pltpu.make_async_copy(listed_ref, list_ref, list_sem)
+    listing.start()
+    apart[...] = columns_apart()
+    listing.wait()
     count = list_ref[4, 0].astype(jnp.int32)
-    apart[...] = columns_apart()
 
     def entry(n):
         code = list_ref[0, n].astype(jnp.int32)
@@ -573,13 +576,13 @@
 
 def warp(entries, tiles, blank):
     vmem = pl.BlockSpec(memory_space=pltpu.VMEM)
-    smem = pl.BlockSpec(memory_space=pltpu.SMEM)
     return pl.pallas_call(
         warp_kernel,
         out_shape=jax.ShapeDtypeStruct((S, 2, TILE, WIDE), BF16),
-        in_specs=[smem, vmem, vmem],
+        in_specs=[vmem, vmem, vmem],
         out_specs=vmem,
-        scratch_shapes=[pltpu.VMEM((TILE, TILE), BF16)],
+        scratch_shapes=[
+            pltpu.VMEM((TILE, TILE), BF16), pltpu.SMEM((8, LIST), F32), pltpu.SemaphoreType.DMA],
         input_output_aliases={2: 0},
         compiler_params=pltpu.CompilerParams(vmem_limit_bytes=32 * 1024 * 1024),
         name="warp_partials",

time: 55.8 us -> 55.4 us (level)
    pallas_call x1, Pallas kernels: 2.56 us -> 3.5 us  [warp(): pl.pallas_call(warp_kernel, out_shape=jax.ShapeDtypeStruct((S, 2, TILE, W...]
    pallas_call x1, Pallas kernels: 22.9 us -> 22 us  [scatter(): pl.pallas_call(scatter_kernel, out_shape=(jax.ShapeDtypeStruct((S, TILE,...]
where the time goes in v8:
time: 55.4 us; the launch traced here: 55.1 us
  Pallas kernels  54.4 us (98%)
  between operations  0.66 us (1%)
    pallas_call x1, Pallas kernels, relax(): pl.pallas_call(relax_kernel, out_shape=(jax.ShapeDtypeStruct(block, F32),...  27.7 us
    pallas_call x1, Pallas kernels, scatter(): pl.pallas_call(scatter_kernel, out_shape=(jax.ShapeDtypeStruct((S, TILE,...  22 us
    pallas_call x1, Pallas kernels, warp(): pl.pallas_call(warp_kernel, out_shape=jax.ShapeDtypeStruct((S, 2, TILE, W...  3.5 us
    pallas_call x1, Pallas kernels, store(): pl.pallas_call(store_kernel, out_shape=tuple((jax.ShapeDtypeStruct(a.shap...  1.21 us

profile of v8, /device:TPU:4, one launch (start us, length us, event | category | flops | bytes accessed | tf_op | source)
XLA Modules:
  0.0 55.1 jit_solution(12512295212240538042)
XLA Ops:
  0.6 27.7 %relax_and_gather.1 = (f32[2,2,32,128]{3,2,1,0:T(8,128)S(1)}, f32[2,2,32,128]{3,2,1,0:T(8,128)S(1)}, f32[8,256]{1,0:T(8,128)S(1)}, f32[16,128]{1,0:T(8,128)S(1)}...) custom-call(f32[2,2,32,128]{3,2,1,0:T(8,128)} %load_hbm.1, ...), custom_call_target="tpu_custom_call" | custom-call | tf_op jit(solution)/shard_map/relax_and_gather/pallas_call | solution.py:481
  28.3 3.5 %warp_partials.1.part_ref = bf16[2,2,256,1024]{3,2,1,0:T(8,128)(2,1)S(1)} custom-call(f32[8,256]{1,0:T(8,128)S(1)} %get-tuple-element.20.listed_ref, bf16[2,4,256,1024]{3,2,1,0:T(8,128)(2,1)S(1)} %get-tuple-element.19.tiles_ref, bf16[2,2,256,1024]{3,2,1,0:T(8,128)(2,1)S(1)} %get-tuple-element.21.blank_ref), custom_call_target="tpu_custom_call", output_to_operand_aliasing={{}: (2, {})} | custom-call | tf_op jit(solution)/shard_map/warp_partials/pallas_call | solution.py:579
  31.8 22.0 %scatter_and_pool.1 = (bf16[2,256,1024]{2,1,0:T(8,128)(2,1)S(1)}, bf16[2,128,512]{2,1,0:T(8,128)(2,1)S(1)}, bf16[2,64,256]{2,1,0:T(8,128)(2,1)S(1)}) custom-call(f32[16,128]{1,0:T(8,128)S(1)} %get-tuple-element.17.listed_ref, s32[16,128]{1,0:T(8,128)S(1)} %get-tuple-element.18.placed_ref, bf16[2,4,256,1024]{3,2,1,0:T(8,128)(2,1)S(1)} %get-tuple-element.19.tiles_ref, ...), custom_call_target="tpu_custom_call" | custom-call | tf_op jit(solution)/shard_map/scatter_and_pool/pallas_call | solution.py:737
  53.9 1.2 %store_results.1 = (f32[2,2,32,128]{3,2,1,0:T(8,128)}, f32[2,2,32,128]{3,2,1,0:T(8,128)}, bf16[2,256,1024]{2,1,0:T(8,128)(2,1)}, bf16[2,128,512]{2,1,0:T(8,128)(2,1)}, bf16[2,64,256]{2,1,0:T(8,128)(2,1)}) custom-call(f32[2,2,32,128]{3,2,1,0:T(8,128)S(1)} %get-tuple-element.15.refs_0_, f32[2,2,32,128]{3,2,1,0:T(8,128)S(1)} %get-tuple-element.16.refs_1_, ...), custom_call_target="tpu_custom_call" | custom-call | tf_op jit(solution)/shard_map/store_results/pallas_call | solution.py:789

commit v9 on v7

--- a/solution.py
+++ b/solution.py
@@ -688,11 +688,7 @@
         share(s, 0, functools.partial(put_own, s))
 
     def pooled(block):
-        high = block.astype(BF16)
-        low = (block - high.astype(F32)).astype(BF16)
-        matrix = pool[...]
-        return (jnp.dot(high, matrix, preferred_element_type=F32)
-                + jnp.dot(low, matrix, preferred_element_type=F32))
+        return jnp.dot(block.astype(BF16), pool[...], preferred_element_type=F32)
 
     for h, s in ways:
         to_end(s, h).wait_recv()

time: 55.8 us -> 55.7 us (level)
  no operation moved by 1% of the time
where the time goes in v9:
time: 55.7 us; the launch traced here: 54.9 us
  Pallas kernels  54.2 us (97%)
  between operations  0.66 us (1%)
    pallas_call x1, Pallas kernels, relax(): pl.pallas_call(relax_kernel, out_shape=(jax.ShapeDtypeStruct(block, F32),...  27.7 us
    pallas_call x1, Pallas kernels, scatter(): pl.pallas_call(scatter_kernel, out_shape=(jax.ShapeDtypeStruct((S, TILE,...  22.7 us
    pallas_call x1, Pallas kernels, warp(): pl.pallas_call(warp_kernel, out_shape=jax.ShapeDtypeStruct((S, 2, TILE, W...  2.57 us
    pallas_call x1, Pallas kernels, store(): pl.pallas_call(store_kernel, out_shape=tuple((jax.ShapeDtypeStruct(a.shap...  1.21 us

profile of v9, /device:TPU:4, one launch (start us, length us, event | category | flops | bytes accessed | tf_op | source)
XLA Modules:
  0.0 54.9 jit_solution(929562969843243356)
XLA Ops:
  0.6 27.7 %relax_and_gather.1 = (f32[2,2,32,128]{3,2,1,0:T(8,128)S(1)}, f32[2,2,32,128]{3,2,1,0:T(8,128)S(1)}, f32[8,256]{1,0:T(8,128)S(1)}, f32[16,128]{1,0:T(8,128)S(1)}...) custom-call(f32[2,2,32,128]{3,2,1,0:T(8,128)} %load_hbm.1, ...), custom_call_target="tpu_custom_call" | custom-call | tf_op jit(solution)/shard_map/relax_and_gather/pallas_call | solution.py:481
  28.3 2.6 %warp_partials.1.part_ref = bf16[2,2,256,1024]{3,2,1,0:T(8,128)(2,1)S(1)} custom-call(f32[8,256]{1,0:T(8,128)S(1)} %get-tuple-element.20.list_ref, bf16[2,4,256,1024]{3,2,1,0:T(8,128)(2,1)S(1)} %get-tuple-element.19.tiles_ref, bf16[2,2,256,1024]{3,2,1,0:T(8,128)(2,1)S(1)} %get-tuple-element.21.blank_ref), custom_call_target="tpu_custom_call", output_to_operand_aliasing={{}: (2, {})} | custom-call | tf_op jit(solution)/shard_map/warp_partials/pallas_call | solution.py:577
  30.9 22.7 %scatter_and_pool.1 = (bf16[2,256,1024]{2,1,0:T(8,128)(2,1)S(1)}, bf16[2,128,512]{2,1,0:T(8,128)(2,1)S(1)}, bf16[2,64,256]{2,1,0:T(8,128)(2,1)S(1)}) custom-call(f32[16,128]{1,0:T(8,128)S(1)} %get-tuple-element.17.listed_ref, s32[16,128]{1,0:T(8,128)S(1)} %get-tuple-element.18.placed_ref, bf16[2,4,256,1024]{3,2,1,0:T(8,128)(2,1)S(1)} %get-tuple-element.19.tiles_ref, ...), custom_call_target="tpu_custom_call" | custom-call | tf_op jit(solution)/shard_map/scatter_and_pool/pallas_call | solution.py:730
  53.6 1.2 %store_results.1 = (f32[2,2,32,128]{3,2,1,0:T(8,128)}, f32[2,2,32,128]{3,2,1,0:T(8,128)}, bf16[2,256,1024]{2,1,0:T(8,128)(2,1)}, bf16[2,128,512]{2,1,0:T(8,128)(2,1)}, bf16[2,64,256]{2,1,0:T(8,128)(2,1)}) custom-call(f32[2,2,32,128]{3,2,1,0:T(8,128)S(1)} %get-tuple-element.15.refs_0_, f32[2,2,32,128]{3,2,1,0:T(8,128)S(1)} %get-tuple-element.16.refs_1_, ...), custom_call_target="tpu_custom_call" | custom-call | tf_op jit(solution)/shard_map/store_results/pallas_call | solution.py:782
